TPU v7x, 32 devices: a whole 2x2x4 slice. The times are simulated.
32 devices in a mesh: seqs: 4 (over y, x), span: 8 (over z, core).
Axes of the slice: x: 2, y: 2, z: 4, core: 2. Of those that a mesh axis runs over, the one named last changes fastest.
Arguments:
- tokens: bfloat16 [4, 2, 512, 2048], P('seqs', None, 'span'), may hold values from -6 to 6
- attn_weight: bfloat16 [2048, 8448], P(('seqs', 'span')), may hold values from -0.1875 to 0.1875
- mlp_weight: bfloat16 [2048, 16896], P(('seqs', 'span')), may hold values from -0.125 to 0.125
- norm1_gain: bfloat16 [2048], P(('seqs', 'span')), may hold values from 0.5 to 1.5
- norm2_gain: bfloat16 [2048], P(('seqs', 'span')), may hold values from 0.5 to 1.5
- gate_bias: bfloat16 [256], P(('seqs', 'span')), may hold values from 1 to 8
- lengths: int32 [4, 2, 4], P('seqs'), may hold values from 1 to 509, as said below
- cotangent: bfloat16 [4, 2, 512, 2048], P('seqs', None, 'span'), may hold values from -6 to 6
Outputs:
- mixed: bfloat16 [4, 2, 512, 2048], P('seqs', None, 'span')
- grad_tokens: float32 [4, 2, 512, 2048], P('seqs', None, 'span')
- grad_attn: float32 [2048, 8448], P(('seqs', 'span'))
- grad_mlp: float32 [2048, 16896], P(('seqs', 'span'))
- grad_gain1: float32 [2048], P(('seqs', 'span'))
- grad_gain2: float32 [2048], P(('seqs', 'span'))
- grad_bias: float32 [256], P(('seqs', 'span'))
Inputs may be any that keep to these rules, and one draw needn't show every extreme that they name: In every row lengths[g, p, :] the 4 lengths add up to 512; one document of each row, its place drawn from the seed, begins in the first 64 positions and ends in the last 64.
All inputs are finite; a program needn't handle non-finite values.
Results may differ from a plain program's by a relative error of at most 0.018.
Values may be sent and summed in bfloat16 or wider, within the bound.
No kernel may reach another device: no remote copies, remote signals or barrier semaphores. Data moves between devices by JAX's collectives and lax.ppermute only.
A program may use at most 512 MiB of HBM per device.

v0:
```python
import jax
import jax.numpy as jnp
from jax import lax
from jax.sharding import PartitionSpec as P

HEADS = 4
HEAD_DIM = 512
SLOTS = 64
FF = 5632


NORM_EPS = 1e-05
GATE_SOFTENING = 8.0
HIGHEST = lax.Precision.HIGHEST


def carried_in(value, axis, join, neutral):
    place = lax.axis_index(axis)
    gathered = jax.tree.map(
        lambda a, kind: lax.all_gather(a.astype(kind), axis),
        value,
        (jnp.bfloat16, jnp.bfloat16, jnp.bfloat16),
    )
    state = jax.tree.map(lambda a, e: jnp.zeros_like(a) + jnp.asarray(e, a.dtype), value, neutral)

    def carried_one(lap, state):
        return join(
            state,
            jax.tree.map(
                lambda a, own: lax.dynamic_index_in_dim(a, lap, 0, False).astype(own.dtype),
                gathered,
                value,
            ),
        )

    return lax.fori_loop(0, place, carried_one, state)


def prefix(value, axis, join, neutral):
    count = lax.axis_size(axis)
    place = lax.axis_index(axis)
    ahead = count - 1 - place
    gathered = jax.tree.map(
        lambda a, kind: lax.all_gather(a.astype(kind), axis),
        value,
        jax.tree.map(lambda a: jnp.bfloat16 if a.dtype == jnp.float32 else a.dtype, value),
    )
    state = jax.tree.map(lambda a, e: jnp.zeros_like(a) + jnp.asarray(e, a.dtype), value, neutral)

    def prefix_one(lap, state):
        source = count - 1 - lap
        return join(
            state,
            jax.tree.map(
                lambda a, own: lax.dynamic_index_in_dim(a, source, 0, False).astype(own.dtype),
                gathered,
                value,
            ),
        )

    return lax.fori_loop(0, ahead, prefix_one, state)


def exact_dot(left_side, right_side):
    return jnp.dot(left_side, right_side, precision=HIGHEST, preferred_element_type=jnp.float32)


def plain_dot(left_side, right_side):
    return jnp.dot(left_side, right_side, preferred_element_type=jnp.float32)


def dot_left_t(left_side, right_side):
    return lax.dot_general(
        left_side, right_side, (((0,), (0,)), ((), ())), preferred_element_type=jnp.float32
    )


def dot_right_t(left_side, right_side):
    return lax.dot_general(
        left_side, right_side, (((1,), (1,)), ((), ())), preferred_element_type=jnp.float32
    )


def rms_scale(values):
    return lax.rsqrt(jnp.mean(values * values, axis=-1, keepdims=True) + NORM_EPS)


def swish(values):
    return values * jax.nn.sigmoid(values)


def swish_slope(values):
    sigmoid_val = jax.nn.sigmoid(values)
    return sigmoid_val * (1.0 + values * (1.0 - sigmoid_val))


def logarithmic_sigmoid(values):
    return jnp.minimum(values, 0.0) - jnp.log1p(jnp.exp(-jnp.abs(values)))


def segment_ids(lengths_row, positions):
    offsets = jnp.cumsum(lengths_row) - lengths_row
    return jnp.sum((positions[:, None] >= offsets[None, 1:]).astype(jnp.int32), axis=1)


def build_masks(lengths_row, positions, start_pos):
    segments = segment_ids(lengths_row, positions)
    before = segment_ids(lengths_row, jnp.reshape(start_pos - 1, (1,)))[0]
    previous = jnp.where(start_pos > 0, before, -1)
    order_idx = jnp.arange(positions.shape[0], dtype=jnp.int32)
    same_mask = (
        (segments[:, None] == segments[None, :]) & (order_idx[:, None] >= order_idx[None, :])
    ).astype(jnp.float32)
    carry_mask = (segments == previous).astype(jnp.float32)
    last_mask = (segments == segments[-1]).astype(jnp.float32)
    return (same_mask, carry_mask, last_mask)


def head_output(
    query_part, key_part, value_part, gate_part, same_mask, carry_mask, keys_in, values_in
):
    scale_factor = query_part.shape[-1] ** (-0.5)
    cumulative = jnp.cumsum(gate_part, axis=0)
    written = -jnp.expm1(gate_part)
    decay_pairs = (
        jnp.exp(jnp.minimum(cumulative[:, None, :] - cumulative[None, :, :], 0.0))
        * same_mask[:, :, None]
    )
    weighted = decay_pairs * written[None, :, :]
    affinity = exact_dot(query_part, key_part.T) * scale_factor
    entering = jnp.exp(cumulative) * carry_mask[:, None]
    scores = (
        jnp.sum(affinity[:, :, None] * weighted, axis=1)
        + entering * exact_dot(query_part, keys_in.T) * scale_factor
    )
    shifted = scores - jnp.max(scores, axis=1, keepdims=True)
    exp_scores = jnp.exp(shifted)
    slot_probs = exp_scores / jnp.sum(exp_scores, axis=1, keepdims=True)
    mixing = jnp.sum(slot_probs[:, None, :] * weighted, axis=2)
    slot_output = exact_dot(mixing, value_part) + exact_dot(slot_probs * entering, values_in)
    return slot_output * rms_scale(slot_output)


def head_states(key_part, value_part, gate_part, last_mask, carry_mask):
    cumulative = jnp.cumsum(gate_part, axis=0)
    written = -jnp.expm1(gate_part)
    tail_weight = jnp.exp(cumulative[-1][None, :] - cumulative) * written * last_mask[:, None]
    new_keys = exact_dot(tail_weight.T, key_part)
    new_values = exact_dot(tail_weight.T, value_part)
    fade_out = jnp.exp(cumulative[-1]) * carry_mask[-1]
    return (new_keys, new_values, fade_out)


def output_item(one_item):
    query_part, key_part, value_part, gate_part, same_mask, carry_mask, keys_in, values_in = (
        one_item
    )
    return head_output(
        query_part.astype(jnp.float32),
        key_part.astype(jnp.float32),
        value_part.astype(jnp.float32),
        gate_part,
        same_mask,
        carry_mask,
        keys_in,
        values_in,
    )


def states_item(one_item):
    key_part, value_part, gate_part, last_mask, carry_mask = one_item
    return head_states(
        key_part.astype(jnp.float32),
        value_part.astype(jnp.float32),
        gate_part,
        last_mask,
        carry_mask,
    )


def output_back(one_item):
    (
        query_part,
        key_part,
        value_part,
        gate_part,
        same_mask,
        carry_mask,
        keys_in,
        values_in,
        grad_slot,
    ) = one_item

    def local_output(query_f, key_f, value_f, gate_f, keys_f, values_f):
        return head_output(query_f, key_f, value_f, gate_f, same_mask, carry_mask, keys_f, values_f)

    unused, pull_back = jax.vjp(
        local_output,
        query_part.astype(jnp.float32),
        key_part.astype(jnp.float32),
        value_part.astype(jnp.float32),
        gate_part,
        keys_in,
        values_in,
    )
    return pull_back(grad_slot)


def states_back(one_item):
    key_part, value_part, gate_part, last_mask, carry_mask, grad_keys, grad_values, grad_fade = (
        one_item
    )

    def local_states(key_f, value_f, gate_f):
        return head_states(key_f, value_f, gate_f, last_mask, carry_mask)

    unused, pull_back = jax.vjp(
        local_states, key_part.astype(jnp.float32), value_part.astype(jnp.float32), gate_part
    )
    return pull_back((grad_keys, grad_values, grad_fade))


def fold_states(first_part, second_part):
    rate = second_part[0][..., None]
    return (
        first_part[0] * second_part[0],
        rate * first_part[1] + second_part[1],
        rate * first_part[2] + second_part[2],
    )


def by_head(values, phase_total, inner_dim):
    block_rows = values.shape[0] // phase_total
    shaped = values.reshape(phase_total, block_rows, HEADS, inner_dim).transpose(0, 2, 1, 3)
    return shaped.reshape(phase_total * HEADS, block_rows, inner_dim)


def source_head_rows(values, phase_total):
    block_rows, inner_dim = (values.shape[1], values.shape[2])
    shaped = values.reshape(phase_total, HEADS, block_rows, inner_dim).transpose(0, 2, 1, 3)
    return shaped.reshape(phase_total * block_rows, HEADS * inner_dim)


def fetch_attn(attn_weight, norm1_gain, gate_bias):
    return (
        lax.all_gather(attn_weight, ("seqs", "span"), axis=0, tiled=True),
        lax.all_gather(norm1_gain, ("seqs", "span"), axis=0, tiled=True),
        lax.all_gather(gate_bias, ("seqs", "span"), axis=0, tiled=True),
    )


def fetch_mlp(mlp_weight, norm2_gain):
    return (
        lax.all_gather(mlp_weight, ("seqs", "span"), axis=0, tiled=True),
        lax.all_gather(norm2_gain, ("seqs", "span"), axis=0, tiled=True),
    )


def local(tokens, attn_weight, mlp_weight, norm1_gain, norm2_gain, gate_bias, lengths, cotangent):
    phase_total, block_len, model_width = (tokens.shape[1], tokens.shape[2], tokens.shape[3])
    row_count = phase_total * block_len
    qkv_cols = 3 * model_width
    gate_cols = HEADS * SLOTS
    proj_cols = qkv_cols + gate_cols
    residual = tokens.reshape(row_count, model_width).astype(jnp.float32)
    attn_full, gain_one, bias_full = fetch_attn(attn_weight, norm1_gain, gate_bias)
    scale_one = rms_scale(residual)
    normed_one = residual * scale_one
    input_one = (normed_one * gain_one.astype(jnp.float32)).astype(jnp.bfloat16)
    projected = plain_dot(input_one, attn_full[:, :proj_cols])
    pre_feats = projected[:, :qkv_cols]
    gate_before_activation = projected[:, qkv_cols:] + bias_full.astype(jnp.float32)
    features = swish(pre_feats).astype(jnp.bfloat16)
    logged_gate = logarithmic_sigmoid(gate_before_activation) / GATE_SOFTENING
    head_query = by_head(features[:, :model_width], phase_total, HEAD_DIM)
    head_key = by_head(features[:, model_width : 2 * model_width], phase_total, HEAD_DIM)
    head_value = by_head(features[:, 2 * model_width :], phase_total, HEAD_DIM)
    head_gate = by_head(logged_gate, phase_total, SLOTS)
    block_index = lax.axis_index("span")
    start_pos = block_index * block_len
    positions = start_pos + jnp.arange(block_len, dtype=jnp.int32)
    same_mask, carry_mask, last_mask = jax.vmap(build_masks, in_axes=(0, None, None))(
        lengths[0], positions, start_pos
    )
    same_mask = jnp.repeat(same_mask, HEADS, axis=0)
    carry_mask = jnp.repeat(carry_mask, HEADS, axis=0)
    last_mask = jnp.repeat(last_mask, HEADS, axis=0)
    new_keys, new_values, fade_out = lax.map(
        states_item, (head_key, head_value, head_gate, last_mask, carry_mask)
    )
    identity = (jnp.ones_like(fade_out), jnp.zeros_like(new_keys), jnp.zeros_like(new_values))
    carried = carried_in((fade_out, new_keys, new_values), "span", fold_states, identity)
    keys_in, values_in = (carried[1], carried[2])
    slot_out = lax.map(
        output_item,
        (head_query, head_key, head_value, head_gate, same_mask, carry_mask, keys_in, values_in),
    )
    slot_low = source_head_rows(slot_out, phase_total).astype(jnp.bfloat16)
    attn_out = dot_right_t(slot_low, attn_full[:, proj_cols:])
    after_attn = residual + attn_out
    mlp_full, gain_two = fetch_mlp(mlp_weight, norm2_gain)
    scale_two = rms_scale(after_attn)
    normed_two = after_attn * scale_two
    input_two = (normed_two * gain_two.astype(jnp.float32)).astype(jnp.bfloat16)
    gate_up = plain_dot(input_two, mlp_full[:, : 2 * FF])
    gate_pre = gate_up[:, :FF]
    up_pre = gate_up[:, FF:]
    hidden = (swish(gate_pre) * up_pre).astype(jnp.bfloat16)
    mlp_out = dot_right_t(hidden, mlp_full[:, 2 * FF :])
    mixed_out = (after_attn + mlp_out).astype(jnp.bfloat16).reshape(tokens.shape)
    mlp_back, gain_back_two = fetch_mlp(mlp_weight, norm2_gain)
    grad_rows = cotangent.reshape(row_count, model_width).astype(jnp.float32)
    grad_low = grad_rows.astype(jnp.bfloat16)
    grad_hidden = plain_dot(grad_low, mlp_back[:, 2 * FF :])
    grad_gate = (grad_hidden * up_pre * swish_slope(gate_pre)).astype(jnp.bfloat16)
    grad_up = (grad_hidden * swish(gate_pre)).astype(jnp.bfloat16)
    grad_gate_up = jnp.concatenate([grad_gate, grad_up], axis=1)
    grad_input_two = dot_right_t(grad_gate_up, mlp_back[:, : 2 * FF])
    weight_gate_up = dot_left_t(input_two, grad_gate_up)
    weight_down = dot_left_t(grad_low, hidden)
    gain_grad_two = jnp.sum(grad_input_two * normed_two, axis=0)
    scaled_two = grad_input_two * gain_back_two.astype(jnp.float32)
    grad_after = grad_rows + scale_two * (
        scaled_two - normed_two * jnp.mean(scaled_two * normed_two, axis=1, keepdims=True)
    )
    mlp_shares = (
        lax.psum_scatter(weight_gate_up, ("seqs", "span"), scatter_dimension=0, tiled=True),
        lax.psum_scatter(weight_down, ("seqs", "span"), scatter_dimension=0, tiled=True),
        lax.psum_scatter(gain_grad_two, ("seqs", "span"), scatter_dimension=0, tiled=True),
    )
    attn_back, gain_back_one, bias_again = fetch_attn(attn_weight, norm1_gain, gate_bias)
    after_low = grad_after.astype(jnp.bfloat16)
    grad_slot = plain_dot(after_low, attn_back[:, proj_cols:])
    weight_out = dot_left_t(after_low, slot_low)
    head_grad = by_head(grad_slot, phase_total, HEAD_DIM)
    local_grads = lax.map(
        output_back,
        (
            head_query,
            head_key,
            head_value,
            head_gate,
            same_mask,
            carry_mask,
            keys_in,
            values_in,
            head_grad,
        ),
    )
    grad_query, grad_key, grad_value, gradient_logged_gate, grad_keys_in, grad_values_in = (
        local_grads
    )
    back_identity = (
        jnp.ones_like(fade_out),
        jnp.zeros_like(grad_keys_in),
        jnp.zeros_like(grad_values_in),
    )
    reversed_states = prefix(
        (fade_out, grad_keys_in, grad_values_in), "span", fold_states, back_identity
    )
    later_keys, later_values = (reversed_states[1], reversed_states[2])
    grad_fade = jnp.sum(later_keys * keys_in, axis=2) + jnp.sum(later_values * values_in, axis=2)
    state_terms = lax.map(
        states_back,
        (
            head_key,
            head_value,
            head_gate,
            last_mask,
            carry_mask,
            later_keys,
            later_values,
            grad_fade,
        ),
    )
    grad_key = grad_key + state_terms[0]
    grad_value = grad_value + state_terms[1]
    gradient_logged_gate = gradient_logged_gate + state_terms[2]
    grad_feats = jnp.concatenate(
        [
            source_head_rows(grad_query, phase_total),
            source_head_rows(grad_key, phase_total),
            source_head_rows(grad_value, phase_total),
        ],
        axis=1,
    )
    grad_pre_feats = (grad_feats * swish_slope(pre_feats)).astype(jnp.bfloat16)
    grad_pre_gate = (
        source_head_rows(gradient_logged_gate, phase_total)
        * jax.nn.sigmoid(-gate_before_activation)
        / GATE_SOFTENING
    ).astype(jnp.bfloat16)
    grad_projected = jnp.concatenate([grad_pre_feats, grad_pre_gate], axis=1)
    grad_input_one = dot_right_t(grad_projected, attn_back[:, :proj_cols])
    weight_in = dot_left_t(input_one, grad_projected)
    bias_grad = jnp.sum(grad_pre_gate.astype(jnp.float32), axis=0)
    gain_grad_one = jnp.sum(grad_input_one * normed_one, axis=0)
    scaled_one = grad_input_one * gain_back_one.astype(jnp.float32)
    grad_input = grad_after + scale_one * (
        scaled_one - normed_one * jnp.mean(scaled_one * normed_one, axis=1, keepdims=True)
    )
    attn_shares = (
        lax.psum_scatter(weight_in, ("seqs", "span"), scatter_dimension=0, tiled=True),
        lax.psum_scatter(weight_out, ("seqs", "span"), scatter_dimension=0, tiled=True),
        lax.psum_scatter(gain_grad_one, ("seqs", "span"), scatter_dimension=0, tiled=True),
        lax.psum_scatter(bias_grad, ("seqs", "span"), scatter_dimension=0, tiled=True),
    )
    grad_attn = jnp.concatenate([attn_shares[0], attn_shares[1]], axis=1)
    grad_mlp = jnp.concatenate([mlp_shares[0], mlp_shares[1]], axis=1)
    return (
        mixed_out,
        grad_input.reshape(tokens.shape),
        grad_attn,
        grad_mlp,
        attn_shares[2],
        mlp_shares[2],
        attn_shares[3],
    )


def solution(mesh):
    placed = (
        P("seqs", None, "span", None),
        P(("seqs", "span"), None),
        P(("seqs", "span"), None),
        P(("seqs", "span")),
        P(("seqs", "span")),
        P(("seqs", "span")),
        P("seqs", None, None),
        P("seqs", None, "span", None),
    )
    return jax.shard_map(
        local,
        mesh=mesh,
        in_specs=placed,
        out_specs=(
            P("seqs", None, "span", None),
            P("seqs", None, "span", None),
            P(("seqs", "span"), None),
            P(("seqs", "span"), None),
            P(("seqs", "span")),
            P(("seqs", "span")),
            P(("seqs", "span")),
        ),
        check_vma=False,
    )
```

profile of v0, /device:TPU:5, one launch (start us, length us, event | category | flops | bytes accessed | tf_op | source)
XLA Modules:
  0.0 3279.4 jit_solution(1135227614777068239)
XLA Ops:
  8.9 41.6 %all-reduce.9 = (bf16[2048]{0:T(1024)(128)(2,1)S(1)}, bf16[256]{0:T(256)(128)(2,1)S(1)}, bf16[2048]{0:T(1024)(128)(2,1)S(1)}) all-reduce(bf16[2048]{0:T(1024)(128)(2,1)S(1)} %dynamic-update-slice, bf16[256]{0:T(256)(128)(2,1)S(1)} %dynamic-update-slice.1, ...), channel_id=1, replica_groups=mesh['seqs'=4,'span'=8] {'seqs','span'}, use_global_device_ids=true, to_apply=%add.2 | all-reduce | flops 4352 | bytes 17408
  51.8 161.9 %all-gather.12.cloned.1.call-done = bf16[2048,8448]{1,0:T(8,128)(2,1)} async-done(((bf16[64,8448]{1,0:T(8,128)(2,1)}), bf16[2048,8448]{1,0:T(8,128)(2,1)}) %all-gather.12.cloned.1.call-update) | async-done | bytes 34603024 | tf_op jit(solution)/shard_map/all_gather | solution.py:246
  232.9 16.7 while.88
  267.7 28.4 all-gather.16.cloned.1.call-done
  296.1 47.3 %all-gather.18.cloned.1.call-done = bf16[64,64,512]{2,1,0:T(8,128)(2,1)} async-done(((bf16[8,64,512]{2,1,0:T(8,128)(2,1)}), bf16[64,64,512]{2,1,0:T(8,128)(2,1)}) %all-gather.18.cloned.1.call-update) | async-done | bytes 4194320 | tf_op jit(solution)/shard_map/all_gather | solution.py:20
  346.7 65.4 %while.90 = (s32[]{:T(128)}, bf16[8,64,512]{2,1,0:T(8,128)(2,1)}, bf16[8,64,512]{2,1,0:T(8,128)(2,1)}, bf16[8,64,512]{2,1,0:T(8,128)(2,1)}, f32[8,64,64]{2,1,0:T...) while((s32[]{:T(128)}, bf16[8,64,512]{2,1,0:T(8,128)(2,1)}, ...), condition=%wide.region_16.17_spmd, body=%wide.region_9.16_spmd.sunk | while | flops 83271616 | bytes 1693589 | solution.py:294
  421.6 289.9 %all-gather.14.cloned.1.call-done = bf16[2048,16896]{1,0:T(8,128)(2,1)} async-done(((bf16[64,16896]{1,0:T(8,128)(2,1)}), bf16[2048,16896]{1,0:T(8,128)(2,1)}) %all-gather.14.cloned.1.call-update) | async-done | bytes 69206032 | tf_op jit(solution)/shard_map/all_gather | solution.py:254
  711.5 19.9 fusion.152
  731.4 13.6 multiply_convert_fusion.2
  745.0 23.1 multiply_reduce_fusion.5
  786.6 185.2 %while.91 = (s32[]{:T(128)}, f32[8,64,512]{2,1,0:T(8,128)}, f32[8,64,512]{2,1,0:T(8,128)}, f32[8,64,512]{2,1,0:T(8,128)}, f32[8,64,64]{2,1,0:T(8,128)}, /*index=...) while((s32[]{:T(128)}, f32[8,64,512]{2,1,0:T(8,128)}, ...), condition=%wide.region_36.37_spmd, body=%wide.region_19.36_spmd.sunk | while | flops 292294912 | bytes 4910557 | solution.py:336
  986.4 31.6 all-gather.20.cloned.1.call-done
  1018.1 47.4 %all-gather.22.cloned.1.call-done = bf16[64,64,512]{2,1,0:T(8,128)(2,1)} async-done(((bf16[8,64,512]{2,1,0:T(8,128)(2,1)}), bf16[64,64,512]{2,1,0:T(8,128)(2,1)}) %all-gather.22.cloned.1.call-update) | async-done | bytes 4194320 | tf_op jit(solution)/shard_map/all_gather | solution.py:44
  1066.6 19.0 while.92
  1089.1 54.1 %while.93 = (s32[]{:T(128)}, f32[8,64,512]{2,1,0:T(8,128)S(1)}, f32[8,64,512]{2,1,0:T(8,128)}, f32[8,64,64]{2,1,0:T(8,128)}, f32[8,64,64]{2,1,0:T(8,128)S(1)}, /...) while((s32[]{:T(128)}, f32[8,64,512]{2,1,0:T(8,128)S(1)}, ...), condition=%wide.region_45.46_spmd, body=%wide.region_41.45_spmd.sunk | while | flops 101273664 | bytes 1387701 | solution.py:363
  1152.5 20.8 fusion.178
  1174.8 18.3 convolution_bitcast_fusion.8
  1194.4 34.7 %fusion.177 = f32[2048,11264]{1,0:T(8,128)} fusion(bf16[128,5632]{1,0:T(8,128)(2,1)} %get-tuple-element.624, bf16[128,5632]{1,0:T(8,128)(2,1)} %get-tuple-element.623, f32[128,2048]{1,0:T(8,128)S(1)} %copy-done.7, f32[2048]{0:T(1024)S(1)} %convert_element_type.192, f32[128]{0:T(128)S(1)} %add_rsqrt_fusion.2), kind=kOutput, calls=%fused_computation.253 | convolution fusion | flops 5912133632 | bytes 96215552 | tf_op jit(solution)/shard_map/dot_general | solution.py:73
  1229.2 13.1 fusion.174
  1242.3 13.7 multiply_reduce_fusion.6
  1256.0 42.0 %all-reduce.8 = (f32[2048]{0:T(1024)S(1)}, f32[2048]{0:T(1024)S(1)}, f32[256]{0:T(256)S(1)}) all-reduce(f32[2048]{0:T(1024)S(1)} %get-tuple-element.456, f32[2048]{0:T(1024)S(1)} %copy-done.23, f32[256]{0:T(256)S(1)} %copy-done.24), channel_id=11, replica_groups=mesh['seqs'=4,'span'=8] {'seqs','span'}, use_global_device_ids=true, to_apply=%region_52.53.clone | all-reduce | flops 4352 | bytes 34816
  1302.3 504.8 %reduce-scatter.5.cloned.1.call-done = f32[64,6400]{1,0:T(8,128)} async-done(((f32[2048,6400]{1,0:T(8,128)}), f32[64,6400]{1,0:T(8,128)}) %reduce-scatter.5.cloned.1.call-update) | async-done | bytes 1638416 | tf_op jit(solution)/shard_map/reduce_scatter | solution.py:403
  1810.2 487.7 %reduce-scatter.11.cloned.1.call-done = f32[64,5632]{1,0:T(8,128)} async-done(((f32[2048,5632]{1,0:T(8,128)}), f32[64,5632]{1,0:T(8,128)}) %reduce-scatter.11.cloned.1.call-update) | async-done | bytes 1441808 | tf_op jit(solution)/shard_map/reduce_scatter | solution.py:328
  2297.9 969.6 %reduce-scatter.9.cloned.1.call-done = f32[64,11264]{1,0:T(8,128)} async-done(((f32[2048,11264]{1,0:T(8,128)}), f32[64,11264]{1,0:T(8,128)}) %reduce-scatter.9.cloned.1.call-update) | async-done | bytes 2883600 | tf_op jit(solution)/shard_map/reduce_scatter | solution.py:327
  (715 shorter events, 454.1 us)
Async XLA Ops:
  7.2 43.3 %copy-start.5 = (bf16[1,2,64,2048]{3,2,1,0:T(8,128)(2,1)S(1)}, bf16[1,2,64,2048]{3,2,1,0:T(8,128)(2,1)}, u32[]{:S(2)}) copy-start(bf16[1,2,64,2048]{3,2,1,0:T(8,128)(2,1)} %param.20) | copy-start | bytes 1572868
  7.2 43.6 %copy-start.25 = (s32[1,2,4]{2,1,0:T(2,128)S(1)}, s32[1,2,4]{2,1,0:T(2,128)}, u32[]{:S(2)}) copy-start(s32[1,2,4]{2,1,0:T(2,128)} %param.26) | copy-start | bytes 100
  7.2 206.6 %all-gather.12.cloned.1.call-start = ((), (), s32[]{:S(2)}) async-start(), calls=%async_computation.4 | async-start | bytes 35684352 | tf_op jit(solution)/shard_map/all_gather | solution.py:246
  8.0 288.2 %all-gather.16.cloned.1.call-start = ((), (), s32[]{:S(2)}) async-start(), calls=%async_computation.10 | async-start | bytes 4718592 | tf_op jit(solution)/shard_map/all_gather | solution.py:20
  50.5 173.7 %copy-start.21 = (f32[2048]{0:T(1024)}, f32[2048]{0:T(1024)S(1)}, u32[]{:S(2)}) copy-start(f32[2048]{0:T(1024)S(1)} %convert_element_type.176) | copy-start | bytes 24580
  50.8 173.4 %copy-start.26 = (f32[128]{0:T(128)}, f32[128]{0:T(128)S(1)}, u32[]{:S(2)}) copy-start(f32[128]{0:T(128)S(1)} %rsqrt.38) | copy-start | bytes 1540
  51.8 172.4 %copy-start.12 = (bf16[128,2048]{1,0:T(8,128)(2,1)}, bf16[128,2048]{1,0:T(8,128)(2,1)S(1)}, u32[]{:S(2)}) copy-start(bf16[128,2048]{1,0:T(8,128)(2,1)S(1)} %multiply_convert_fusion.5) | copy-start | bytes 1572868
  249.6 3.8 copy-start.3
  249.6 3.8 copy-start.4
  250.4 93.0 %all-gather.18.cloned.1.call-start = ((), (), s32[]{:S(2)}) async-start(), calls=%async_computation.11 | async-start | bytes 4718592 | tf_op jit(solution)/shard_map/all_gather | solution.py:20
  251.2 460.3 %all-gather.14.cloned.1.call-start = ((), (), s32[]{:S(2)}) async-start(), calls=%async_computation.5 | async-start | bytes 71368704 | tf_op jit(solution)/shard_map/all_gather | solution.py:254
  251.7 766.3 %all-gather.20.cloned.1.call-start = ((), (), s32[]{:S(2)}) async-start(), calls=%async_computation.12 | async-start | bytes 4718592 | tf_op jit(solution)/shard_map/all_gather | solution.py:44
  413.8 7.7 copy-start.15
  972.6 92.8 %all-gather.22.cloned.1.call-start = ((), (), s32[]{:S(2)}) async-start(), calls=%async_computation.13 | async-start | bytes 4718592 | tf_op jit(solution)/shard_map/all_gather | solution.py:44
  973.2 329.1 %reduce-scatter.7.cloned.1.call-start = ((), (), s32[]{:S(2)}) async-start(), calls=%async_computation.7 | async-start | bytes 17301504 | tf_op jit(solution)/shard_map/reduce_scatter | solution.py:404
  983.2 823.9 %reduce-scatter.5.cloned.1.call-start = ((), (), s32[]{:S(2)}) async-start(), calls=%async_computation.6 | async-start | bytes 54067200 | tf_op jit(solution)/shard_map/reduce_scatter | solution.py:403
  1173.3 1124.6 %reduce-scatter.11.cloned.1.call-start = ((), (), s32[]{:S(2)}) async-start(), calls=%async_computation.9 | async-start | bytes 47579136 | tf_op jit(solution)/shard_map/reduce_scatter | solution.py:328
  1193.2 2074.3 %reduce-scatter.9.cloned.1.call-start = ((), (), s32[]{:S(2)}) async-start(), calls=%async_computation.8 | async-start | bytes 95158272 | tf_op jit(solution)/shard_map/reduce_scatter | solution.py:327
  1229.1 13.1 copy-start.6
  1229.1 13.1 copy-start.20
  1229.1 13.1 copy-start.22
  1229.1 13.1 copy-start.27
  1242.3 13.7 copy-start.23
  1242.3 13.7 copy-start.24
  (17 other events, 24.1 us)
Sparse Core Ops, SparseCore 0:
  11.1 202.6 all-gather.11
  250.5 45.5 all-gather.15
  297.7 45.6 all-gather.17
  346.3 365.1 all-gather.13
  972.7 45.2 all-gather.19
  1019.5 45.8 all-gather.21
  1067.7 180.9 reduce-scatter.6
  1251.0 556.0 reduce-scatter.4
  1809.4 488.4 reduce-scatter.10
  2300.1 967.3 reduce-scatter.8
where the time goes:
time: 3300 us; the launch traced here: 3280 us
  waiting for transfers between devices  2570 us (78%)
  matrix products  364 us (11%)
  other arithmetic  181 us (5%)
  blocking collectives  96.5 us (3%)
  local copies, waits for them, and re-layouts  48.6 us (1%)
    reduce_scatter x1, waiting for transfers between devices, local(): lax.psum_scatter(weight_gate_up, ('seqs', 'span'), scatter_dimension=0, t...  970 us
    reduce_scatter x1, waiting for transfers between devices, local(): lax.psum_scatter(weight_in, ('seqs', 'span'), scatter_dimension=0, tiled=...  505 us
    reduce_scatter x1, waiting for transfers between devices, local(): lax.psum_scatter(weight_down, ('seqs', 'span'), scatter_dimension=0, tile...  488 us
    all_gather x1, waiting for transfers between devices, fetch_mlp(): lax.all_gather(mlp_weight, ('seqs', 'span'), axis=0, tiled=True)  290 us
    dot_general x176, matrix products, exact_dot(): jnp.dot(left_side, right_side, precision=HIGHEST, preferred_element_type=...  173 us
    all_gather x1, waiting for transfers between devices, fetch_attn(): lax.all_gather(attn_weight, ('seqs', 'span'), axis=0, tiled=True)  162 us
    dot_general x4, matrix products, dot_left_t(): lax.dot_general(left_side, right_side, (((0,), (0,)), ((), ())), preferre...  83.8 us
    unnamed x2, blocking collectives  83.6 us
  transfers between devices with their start and end apart: 10, of which 9 were waited for; matrix products, arithmetic and copies ran while one was open for 9% of the time, Pallas kernels for 0%

commit v1 on v0

v1 whole, which is shorter than its diff:
```python
import functools
import jax
import jax.numpy as jnp
from jax import lax
from jax.experimental import pallas as pl
from jax.experimental.pallas import tpu as pltpu
from jax.sharding import PartitionSpec as P

BLOCK = 64
SUB = 16
SLOTS = 64
HEAD_DIM = 512
NORM_EPS = 1e-05


def mm(a, b, dims):
    return lax.dot_general(
        a.astype(jnp.bfloat16), b.astype(jnp.bfloat16), (dims, ((), ())), preferred_element_type=jnp.float32
    )


def halves(a):
    if a.dtype == jnp.bfloat16:
        return a, None
    high = a.astype(jnp.bfloat16)
    return high, (a - high.astype(jnp.float32)).astype(jnp.bfloat16)


def fine(a, b, dims):
    (a_high, a_low), (b_high, b_low) = halves(a), halves(b)
    out = mm(a_high, b_high, dims)
    if b_low is not None:
        out = out + mm(a_high, b_low, dims)
    if a_low is not None:
        out = out + mm(a_low, b_high, dims)
    return out


NN, NT, TN = ((1,), (0,)), ((1,), (1,)), ((0,), (0,))


def nn(a, b):
    return mm(a, b, NN)


def nt(a, b):
    return mm(a, b, NT)


def tn(a, b):
    return mm(a, b, TN)


def exact(a, b):
    return lax.dot_general(
        a, b, (((1,), (0,)), ((), ())), precision=lax.Precision.HIGHEST, preferred_element_type=jnp.float32
    )


def iota(shape, dim):
    return lax.broadcasted_iota(jnp.int32, shape, dim)


def block_decay(gate, write, seg_col, seg_row, seg_prev):
    row, col = iota((BLOCK, BLOCK), 0), iota((BLOCK, BLOCK), 1)
    same = jnp.where((seg_col == seg_row) & (row >= col), 1.0, 0.0)
    lower = jnp.where(row >= col, 1.0, 0.0)
    cum = exact(lower, gate)
    total = cum[BLOCK - 1 :]
    carry = jnp.where(seg_col == seg_prev, 1.0, 0.0)
    last = jnp.where(seg_col == seg_col[BLOCK - 1 :], 1.0, 0.0)
    enter = jnp.exp(cum) * carry
    tail = jnp.exp(total - cum) * last
    fade = jnp.exp(total) * carry[BLOCK - 1 :]
    falls, rises = [], []
    for i in range(1, BLOCK // SUB):
        base = cum[i * SUB - 1 : i * SUB]
        falls.append(jnp.exp(cum[i * SUB : (i + 1) * SUB] - base))
        rises.append(jnp.exp(base - cum[: i * SUB]))
    return same, cum, enter, tail, fade, falls, rises


def diagonal(square):
    return jnp.concatenate([square[i : i + SUB, i : i + SUB] for i in range(0, BLOCK, SUB)], axis=0)


def undiagonal(strip):
    row, col = iota((BLOCK, BLOCK), 0), iota((BLOCK, BLOCK), 1)
    wide = jnp.concatenate([strip] * (BLOCK // SUB), axis=1)
    return jnp.where(row // SUB == col // SUB, wide, 0.0)


def parts(values):
    return values.reshape(BLOCK // SUB, SUB, values.shape[-1])


def decay_at(cum, j):
    cum_parts = parts(cum)
    return jnp.exp(jnp.minimum(cum_parts - cum_parts[:, j : j + 1], 0.0))


def over_sources(pairs, cum, write, falls, rises):
    strip = parts(diagonal(pairs))
    write_parts = parts(write)
    near = jnp.zeros((BLOCK // SUB, SUB, SLOTS), jnp.float32)
    for j in range(SUB):
        near = near + strip[:, :, j : j + 1] * (decay_at(cum, j) * write_parts[:, j : j + 1])
    near = near.reshape(BLOCK, SLOTS)
    far = [jnp.zeros((SUB, SLOTS), jnp.float32)]
    for i in range(1, BLOCK // SUB):
        rows = pairs[i * SUB : (i + 1) * SUB, : i * SUB]
        far.append(falls[i - 1] * fine(rows, rises[i - 1] * write[: i * SUB], NN))
    return near + jnp.concatenate(far, axis=0)


def over_slots(values, cum, write, falls, rises):
    value_parts, write_parts = parts(values), parts(write)
    lane = iota((BLOCK // SUB, SUB, SUB), 2)
    strip = jnp.zeros((BLOCK // SUB, SUB, SUB), jnp.float32)
    for j in range(SUB):
        term = value_parts * (decay_at(cum, j) * write_parts[:, j : j + 1])
        strip = jnp.where(lane == j, jnp.sum(term, axis=2, keepdims=True), strip)
    out = undiagonal(strip.reshape(BLOCK, SUB))
    far = [jnp.zeros((SUB, BLOCK), jnp.float32)]
    for i in range(1, BLOCK // SUB):
        rows = values[i * SUB : (i + 1) * SUB] * falls[i - 1]
        piece = fine(rows, rises[i - 1] * write[: i * SUB], NT)
        far.append(jnp.concatenate([piece, jnp.zeros((SUB, BLOCK - i * SUB), jnp.float32)], axis=1))
    return out + jnp.concatenate(far, axis=0)


def over_targets(pairs_values, cum, falls, rises):
    row = iota((BLOCK // SUB, SUB, SLOTS), 1)
    near = jnp.zeros((BLOCK // SUB, SUB, SLOTS), jnp.float32)
    strips = [(parts(diagonal(p)), parts(v)) for p, v in pairs_values]
    for j in range(SUB):
        term = sum(strip[:, :, j : j + 1] * value for strip, value in strips) * decay_at(cum, j)
        near = jnp.where(row == j, jnp.sum(term, axis=1, keepdims=True), near)
    out = near.reshape(BLOCK, SLOTS)
    far = jnp.zeros((BLOCK, SLOTS), jnp.float32)
    for i in range(1, BLOCK // SUB):
        here = slice(i * SUB, (i + 1) * SUB)
        piece = sum(fine(p[here, : i * SUB], v[here] * falls[i - 1], TN) for p, v in pairs_values)
        piece = rises[i - 1] * piece
        far = far + jnp.concatenate([piece, jnp.zeros((BLOCK - i * SUB, SLOTS), jnp.float32)], axis=0)
    return out + far


def load_block(i, q_ref, k_ref, v_ref, gate_ref, write_ref, segc_ref, segr_ref):
    here = pl.ds(pl.multiple_of(i * BLOCK, BLOCK), BLOCK)
    seg_col = segc_ref[here, :]
    seg_row = segr_ref[i]
    before = segc_ref[pl.ds(jnp.maximum(i * BLOCK - 1, 0), 1), :]
    seg_prev = jnp.where(i > 0, before, -1)
    return here, q_ref[here, :], k_ref[here, :], v_ref[here, :], gate_ref[here, :], write_ref[here, :], seg_col, seg_row, seg_prev


def forward_kernel(q_ref, k_ref, v_ref, gate_ref, write_ref, segc_ref, segr_ref,
                   low_ref, out_ref, score_ref, prob_ref, pair_ref, mix_ref, keys_ref, values_ref, key_state, value_state):
    scale = HEAD_DIM ** -0.5
    key_state[...] = jnp.zeros_like(key_state)
    value_state[...] = jnp.zeros_like(value_state)

    def step(i, _):
        here, q, k, v, gate, write, seg_col, seg_row, seg_prev = load_block(i, q_ref, k_ref, v_ref, gate_ref, write_ref, segc_ref, segr_ref)
        same, cum, enter, tail, fade, falls, rises = block_decay(gate, write, seg_col, seg_row, seg_prev)
        keys_in, values_in = key_state[...], value_state[...]
        keys_ref[i], values_ref[i] = keys_in, values_in
        keep = fade.reshape(SLOTS, 1)
        send = tail * write
        key_state[...] = keep * keys_in + tn(send, k)
        value_state[...] = keep * values_in + fine(send, v, TN)
        pairs = nt(q, k) * same
        score = scale * (over_sources(pairs, cum, write, falls, rises) + enter * nt(q, keys_in))
        prob = jnp.exp(score - jnp.max(score, axis=1, keepdims=True))
        prob = prob / jnp.sum(prob, axis=1, keepdims=True)
        mix = over_slots(prob, cum, write, falls, rises) * same
        out = fine(mix, v, NN) + fine(prob * enter, values_in, NN)
        scaled = out * lax.rsqrt(jnp.mean(out * out, axis=1, keepdims=True) + NORM_EPS)
        low_ref[here, :] = scaled.astype(jnp.bfloat16)
        out_ref[here, :] = out
        score_ref[here, :] = score
        prob_ref[here, :] = prob
        pair_ref[here, :] = pairs
        mix_ref[here, :] = mix
        return 0

    lax.fori_loop(0, q_ref.shape[0] // BLOCK, step, 0)


def backward_kernel(q_ref, k_ref, v_ref, gate_ref, write_ref, segc_ref, segr_ref,
                    out_ref, score_ref, prob_ref, pair_ref, mix_ref, keys_ref, values_ref, don_ref,
                    dq_ref, dk_ref, dv_ref, dgate_ref, key_state, value_state, key_next, value_next):
    scale = HEAD_DIM ** -0.5
    blocks = q_ref.shape[0] // BLOCK
    for state in (key_state, value_state, key_next, value_next):
        state[...] = jnp.zeros_like(state)

    def step(lap, _):
        i = blocks - 1 - lap
        here, q, k, v, gate, write, seg_col, seg_row, seg_prev = load_block(i, q_ref, k_ref, v_ref, gate_ref, write_ref, segc_ref, segr_ref)
        same, cum, enter, tail, fade, falls, rises = block_decay(gate, write, seg_col, seg_row, seg_prev)
        last = jnp.where(seg_col == seg_col[BLOCK - 1 :], 1.0, 0.0)
        score, prob, pairs, mix = score_ref[here, :], prob_ref[here, :], pair_ref[here, :], mix_ref[here, :]
        keys_in, values_in = keys_ref[i], values_ref[i]
        out, don = out_ref[here, :], don_ref[here, :]
        unit = lax.rsqrt(jnp.mean(out * out, axis=1, keepdims=True) + NORM_EPS)
        normed = out * unit
        dout = unit * (don - normed * jnp.mean(don * normed, axis=1, keepdims=True))
        dmix = fine(dout, v, NT) * same
        dprob = over_sources(dmix, cum, write, falls, rises) + enter * fine(dout, values_in, NT)
        inner = prob * dprob
        dscore = inner - prob * jnp.sum(inner, axis=1, keepdims=True)
        slope = scale * dscore
        dpairs = over_slots(slope, cum, write, falls, rises) * same
        dcross = slope * enter
        dkeys, dvalues = key_state[...], value_state[...]
        send = tail * write
        dq_ref[here, :] = nn(dpairs, k) + nn(dcross, keys_in)
        dk_ref[here, :] = tn(dpairs, q) + nn(send, dkeys)
        dv_ref[here, :] = tn(mix, dout) + nn(send, dvalues)
        heard = over_targets([(pairs, slope), (dmix, prob)], cum, falls, rises)
        heard = heard + tail * (nt(k, dkeys) + nt(v, dvalues))
        ones = jnp.ones((8, HEAD_DIM), jnp.float32)
        held = lax.dot_general(ones, dkeys * key_next[...] + dvalues * value_next[...], (((1,), (1,)), ((), ())),
                               precision=lax.Precision.HIGHEST, preferred_element_type=jnp.float32)[:1]
        upper = same.T
        flow = exact(upper, dscore * score + inner - write * heard)
        dgate_ref[here, :] = flow - jnp.exp(gate) * heard + last * held
        keep = fade.reshape(SLOTS, 1)
        key_state[...] = keep * dkeys + tn(dcross, q)
        value_state[...] = keep * dvalues + fine(prob * enter, dout, TN)
        key_next[...], value_next[...] = keys_in, values_in
        return 0

    lax.fori_loop(0, blocks, step, 0)


def vmem_call(kernel, outs, scratch, flops, args, limit=48):
    nbytes = sum(a.size * a.dtype.itemsize for a in args) + sum(o.size * o.dtype.itemsize for o in outs)
    return pl.pallas_call(
        kernel,
        out_shape=outs,
        in_specs=[pl.BlockSpec(memory_space=pltpu.VMEM)] * len(args),
        out_specs=[pl.BlockSpec(memory_space=pltpu.VMEM)] * len(outs),
        scratch_shapes=scratch,
        cost_estimate=pl.CostEstimate(flops=flops, bytes_accessed=nbytes, transcendentals=0),
        compiler_params=pltpu.CompilerParams(vmem_limit_bytes=limit * 2**20),
    )(*args)


def forward_mix(q, k, v, gate, write, seg):
    length = q.shape[0]
    blocks = length // BLOCK
    shape = jax.ShapeDtypeStruct
    slots = shape((length, SLOTS), jnp.float32)
    states = shape((blocks, SLOTS, HEAD_DIM), jnp.float32)
    state = pltpu.VMEM((SLOTS, HEAD_DIM), jnp.float32)
    outs = [shape((length, HEAD_DIM), jnp.bfloat16), shape((length, HEAD_DIM), jnp.float32), slots, slots, slots, slots, states, states]
    args = (q, k, v, gate, write, seg.reshape(length, 1), seg.reshape(blocks, 1, BLOCK))
    return vmem_call(forward_kernel, outs, [state] * 2, 8 * length * HEAD_DIM * SLOTS * 2, args)


def backward_mix(q, k, v, gate, write, seg, saved, don):
    length = q.shape[0]
    blocks = length // BLOCK
    shape = jax.ShapeDtypeStruct
    wide = shape((length, HEAD_DIM), jnp.float32)
    state = pltpu.VMEM((SLOTS, HEAD_DIM), jnp.float32)
    outs = [wide, wide, wide, shape((length, SLOTS), jnp.float32)]
    args = (q, k, v, gate, write, seg.reshape(length, 1), seg.reshape(blocks, 1, BLOCK), *saved, don)
    return vmem_call(backward_kernel, outs, [state] * 4, 20 * length * HEAD_DIM * SLOTS * 2, args)


HEADS = 4
FF = 5632
GATE_SOFTENING = 8.0


def dot(a, b, dims, kind=jnp.float32):
    out = lax.dot_general(a, b, (dims, ((), ())), preferred_element_type=jnp.float32)
    return out.astype(kind)


def rms_scale(values):
    return lax.rsqrt(jnp.mean(values * values, axis=-1, keepdims=True) + NORM_EPS)


def swish(values):
    return values * jax.nn.sigmoid(values)


def swish_slope(values):
    sigmoid_val = jax.nn.sigmoid(values)
    return sigmoid_val * (1.0 + values * (1.0 - sigmoid_val))


def logarithmic_sigmoid(values):
    return jnp.minimum(values, 0.0) - jnp.log1p(jnp.exp(-jnp.abs(values)))


def plus(a, b):
    return (a.astype(jnp.float32) + b.astype(jnp.float32)).astype(a.dtype)


def behind(value, *others):
    return lax.optimization_barrier((value, others))[0]


def tn_pair_kernel(a_ref, b_ref, c_ref, d_ref, e_ref, f_ref, out_ref):
    first, width = dot(a_ref[...], b_ref[...], TN), b_ref.shape[1]
    if e_ref.shape[1] == 1:
        extra = e_ref[...] * f_ref[...]
        out_ref[:, : width - 128] = first[:, : width - 128].astype(jnp.bfloat16)
        out_ref[:, width - 128 : width] = (first[:, width - 128 :] + extra).astype(jnp.bfloat16)
    else:
        out_ref[:, :width] = first.astype(jnp.bfloat16)
    out_ref[:, width:] = dot(c_ref[...], d_ref[...], TN, jnp.bfloat16)


def tn_pair(a, b, c, d, block, e=None, f=None):
    length, rows = a.shape
    cols = b.shape[1] + d.shape[1]
    if e is None:
        e, f = jnp.zeros((rows, 128), jnp.float32), jnp.zeros((1, 128), jnp.float32)
    whole = lambda v: pl.BlockSpec(v.shape, lambda i: (0, 0))
    strip = pl.BlockSpec((length, block), lambda i: (0, i))
    return pl.pallas_call(
        tn_pair_kernel,
        grid=(rows // block,),
        in_specs=[strip, whole(b), strip, whole(d), pl.BlockSpec((block, e.shape[1]), lambda i: (i, 0)), whole(f)],
        out_specs=pl.BlockSpec((block, cols), lambda i: (i, 0)),
        out_shape=jax.ShapeDtypeStruct((rows, cols), jnp.bfloat16),
        cost_estimate=pl.CostEstimate(flops=2 * length * rows * cols, bytes_accessed=2 * rows * cols, transcendentals=0),
        compiler_params=pltpu.CompilerParams(vmem_limit_bytes=48 * 2**20),
    )(a, b, c, d, e, f)


def hidden_kernel(width, x_ref, y_ref, w_ref, hid_ref, grad_ref, acc):
    step = pl.program_id(0)

    @pl.when(step == 0)
    def _():
        acc[...] = jnp.zeros_like(acc)

    acc[:, : 2 * width] += dot(x_ref[...], w_ref[:, : 2 * width], NN)
    acc[:, 2 * width :] += dot(y_ref[...], w_ref[:, 2 * width : 3 * width], NN)

    @pl.when(step == pl.num_programs(0) - 1)
    def _():
        gate, up, back = acc[:, :width], acc[:, width : 2 * width], acc[:, 2 * width :]
        sig = jax.nn.sigmoid(gate)
        act = gate * sig
        hid_ref[...] = (act * up).astype(jnp.bfloat16)
        grad_ref[:, :width] = (back * up * (sig * (1.0 + gate * (1.0 - sig)))).astype(jnp.bfloat16)
        grad_ref[:, width:] = (back * act).astype(jnp.bfloat16)


def hidden_and_grads(x, y, weights, width, cols, block):
    length, depth = x.shape
    strip = pl.BlockSpec((length, block), lambda i: (0, i))
    return pl.pallas_call(
        functools.partial(hidden_kernel, width),
        grid=(depth // block,),
        in_specs=[strip, strip, pl.BlockSpec((block, cols), lambda i: (i, 0))],
        out_specs=[pl.BlockSpec((length, n * width), lambda i: (0, 0)) for n in (1, 2)],
        out_shape=[jax.ShapeDtypeStruct((length, n * width), jnp.bfloat16) for n in (1, 2)],
        scratch_shapes=[pltpu.VMEM((length, 3 * width), jnp.float32)],
        cost_estimate=pl.CostEstimate(flops=6 * length * depth * width, bytes_accessed=6 * depth * width, transcendentals=0),
        compiler_params=pltpu.CompilerParams(vmem_limit_bytes=56 * 2**20),
    )(x, y, weights)


class Layout:
    def __init__(self, phases):
        self.seqs, self.span, self.phases = lax.axis_size("seqs"), lax.axis_size("span"), phases
        self.ranks = self.span // phases
        self.half = self.ranks // phases
        place = lax.axis_index("span")
        self.rank, self.phase = place // phases, place % phases
        self.slot = (self.rank % self.half) * phases + self.phase
        self.groups = [
            [s * self.span + z * phases + c for s in range(self.seqs) for c in range(phases)]
            for z in range(self.ranks)
        ]

    def across(self, value, k):
        step = k * self.phases
        return lax.ppermute(value, "span", [(i, i ^ step) for i in range(self.span)])

    def outward(self, k):
        pairs = []
        for i in range(self.span):
            z, c = divmod(i, self.phases)
            slot = (z % self.half) * self.phases + c
            pairs.append((i, (slot ^ k) * self.phases + z // self.half))
        return pairs

    def swap(self, value):
        mine = lax.dynamic_index_in_dim(value, self.phase, 0, False)
        other = lax.dynamic_index_in_dim(value, 1 - self.phase, 0, False)
        got = lax.ppermute(other, "span", [(i, i ^ 1) for i in range(self.span)])
        first = self.phase == 0
        return jnp.stack([jnp.where(first, mine, got), jnp.where(first, got, mine)])

    def between(self, value, pairs):
        p = self.phases
        return lax.ppermute(value, "span", [(a * p + c, b * p + c) for a, b in pairs for c in range(p)])

    def spread_near(self, value, step=1):
        if self.ranks != 4:
            return [self.across(value, k) for k in range(step, self.ranks, step)]
        return [self.across(value, 1), self.between(value, [(1, 2), (2, 1)])]

    def spread_far(self, got):
        if self.ranks != 4:
            return got
        near, middle = behind(got)
        inner = self.between(near, [(1, 2), (2, 1)])
        outer = self.between(middle, [(1, 0), (2, 3)])
        inner, outer = behind([inner, outer])
        last = self.between(inner, [(1, 0), (2, 3)])
        end = (self.rank == 0) | (self.rank == 3)
        return [near, jnp.where(end, outer, inner), jnp.where(end, last, middle)]

    def in_order(self, pieces, first, axis=0):
        size = pieces[0].shape[axis]
        shape = list(pieces[0].shape)
        shape[axis] = len(pieces) * size
        out = jnp.zeros(shape, pieces[0].dtype)
        for k, piece in enumerate(pieces):
            out = lax.dynamic_update_slice_in_dim(out, piece, (first ^ k) * size, axis)
        return out

    def gather(self, value):
        return self.in_order([value] + self.spread_far(self.spread_near(value)), self.rank)

    def piece(self, value, k):
        size = value.shape[0] // self.ranks
        return lax.dynamic_slice_in_dim(value, (self.rank ^ k) * size, size, 0)

    def split(self, value):
        return [self.piece(value, k) for k in range(self.ranks)]

    def sum_far(self, pieces):
        if self.ranks != 4:
            return [self.across(pieces[k], k) for k in range(1, self.ranks)]
        return [self.between(pieces[3], [(0, 1), (3, 2)])]

    def sum_middle(self, pieces, got):
        if self.ranks != 4:
            return got
        inner = self.between(plus(pieces[2], got[0]), [(1, 2), (2, 1)])
        outer = self.between(pieces[2], [(0, 1), (3, 2)])
        return behind([inner, outer])

    def sum_near(self, pieces, got):
        if self.ranks != 4:
            return got
        inner, outer = got
        return [self.across(plus(pieces[1], inner), 1), self.between(plus(pieces[3], outer), [(1, 2), (2, 1)])]

    def total(self, pieces, got):
        out = pieces[0].astype(jnp.float32)
        for piece in got:
            out = out + piece.astype(jnp.float32)
        return out

    def deal(self, blocks, *gates):
        pieces = []
        for k in range(self.ranks):
            block = lax.dynamic_index_in_dim(blocks, self.slot ^ k, 0, False) if blocks.shape[0] > 1 else blocks[0]
            pieces.append(lax.ppermute(block, "span", self.outward(k)))
        return self.in_order(behind(pieces, *gates), self.rank)

    def home(self, rows_of, step=1):
        blocks = rows_of.reshape(self.ranks, -1, rows_of.shape[1])
        pieces = []
        for k in range(0, self.ranks, step):
            block = lax.dynamic_index_in_dim(blocks, self.rank ^ k, 0, False)
            pieces.append(lax.ppermute(block, "span", [(b, a) for a, b in self.outward(k)]))
        return pieces

    def fetch(self, value):
        return lax.all_gather(value, ("seqs", "span"), axis=0, tiled=True, axis_index_groups=self.groups)

    def share(self, value):
        return lax.psum_scatter(
            value, ("seqs", "span"), scatter_dimension=0, tiled=True, axis_index_groups=self.groups
        )


def segment_ids(lengths_row, count):
    offsets = jnp.cumsum(lengths_row) - lengths_row
    positions = jnp.arange(count, dtype=jnp.int32)
    return jnp.sum((positions[:, None] >= offsets[None, 1:]).astype(jnp.int32), axis=1)


def local(tokens, attn_weight, mlp_weight, norm1_gain, norm2_gain, gate_bias, lengths, cotangent):
    phases, block_len, width = tokens.shape[1:]
    at = Layout(phases)
    rows = attn_weight.shape[0]
    ranks, copies = at.ranks, at.ranks // HEADS
    proj_cols = 3 * width + HEADS * SLOTS
    share_ff = FF // ranks
    qkv = 3 * HEAD_DIM
    gate_end = qkv + SLOTS
    bias_len = gate_bias.shape[0]
    head = at.rank // copies

    def by_head(part, inner):
        return part.reshape(rows, -1, HEADS, inner).transpose(2, 0, 1, 3).reshape(HEADS, rows, -1)

    extra = jnp.zeros((rows, SLOTS), jnp.bfloat16)
    extra = extra.at[0, :bias_len].set(gate_bias).at[1, :rows].set(norm1_gain).at[2, :rows].set(norm2_gain)
    in_blocks = jnp.concatenate(
        [
            by_head(attn_weight[:, : 3 * width], HEAD_DIM),
            by_head(attn_weight[:, 3 * width : proj_cols], SLOTS),
            jnp.broadcast_to(extra, (HEADS, rows, SLOTS)),
        ],
        axis=2,
    )
    rest = at.swap(tokens[0]).reshape(-1, width)
    dy = at.swap(cotangent[0]).reshape(-1, width)
    mlp_blocks = mlp_weight.reshape(rows, 3, ranks, share_ff).transpose(2, 0, 1, 3).reshape(ranks, rows, -1)
    in_dealt = at.deal(jnp.repeat(in_blocks, copies, axis=0), rest, dy, mlp_blocks)
    w_in = at.fetch(in_dealt)
    late_blocks = jnp.concatenate(
        [mlp_blocks, jnp.broadcast_to(attn_weight[:, proj_cols:], (ranks, rows, width))], axis=2
    )
    late_dealt = at.deal(behind(late_blocks, in_dealt))
    w_late = at.fetch(behind(late_dealt, w_in))
    w_gate_up, w_down = w_late[:, : 2 * share_ff], w_late[:, 2 * share_ff : 3 * share_ff]
    w_out = w_late[:, 3 * share_ff :]
    x_all = at.gather(behind(rest, late_dealt))

    extras = w_in.reshape(-1, rows, w_in.shape[1])[:, :3, gate_end:]
    bias = lax.dynamic_slice_in_dim(extras[:, 0, :bias_len].reshape(-1), head * SLOTS, SLOTS, 0)
    gain_one = extras[:, 1, :rows].reshape(-1).astype(jnp.float32)
    gain_two = extras[:, 2, :rows].reshape(-1).astype(jnp.float32)

    x_float = x_all.astype(jnp.float32)
    in_one = (x_float * rms_scale(x_float) * gain_one).astype(jnp.bfloat16)
    projected = dot(in_one, w_in, NN)
    pre = projected[:, :qkv]
    feats = swish(pre).astype(jnp.bfloat16)
    q, k, v = feats[:, :HEAD_DIM], feats[:, HEAD_DIM : 2 * HEAD_DIM], feats[:, 2 * HEAD_DIM :]
    hf = projected[:, qkv:gate_end] + bias.astype(jnp.float32)
    gate = logarithmic_sigmoid(hf) / GATE_SOFTENING
    write = -jnp.expm1(gate)
    lengths_row = lax.dynamic_index_in_dim(lengths[0], at.phase, 0, False)
    seg = segment_ids(lengths_row, x_all.shape[0])
    dy_near = at.spread_near(behind(dy, x_all))
    low, *saved = forward_mix(q, k, v, gate, write, seg)
    low_near = at.spread_near(behind(low, dy_near), copies)
    low_all = at.in_order([low] + at.spread_far(low_near), head, 1)

    dy_far = at.spread_far(behind(dy_near, low_all))
    after_all = x_float + dot(low_all, w_out, NT)
    in_two = (after_all * rms_scale(after_all) * gain_two).astype(jnp.bfloat16)
    after = at.piece(after_all, 0)
    scale_two = rms_scale(after)
    normed_two = after * scale_two

    dyl = at.in_order([dy] + dy_far, at.rank)
    mlp_cols = 3 * share_ff if share_ff % 128 == 0 else w_late.shape[1]
    hidden, grad_gate_up = hidden_and_grads(in_two, dyl, w_late, share_ff, mlp_cols, 512)
    two_part = dot(grad_gate_up, w_gate_up, NT, jnp.bfloat16)
    two_pieces = at.split(two_part)
    two_far = at.sum_far(two_pieces)
    hidden_later, grad_later = behind((hidden, grad_gate_up), two_pieces)
    grad_mlp_w = tn_pair(in_two, grad_later, dyl, hidden_later, 256)
    share_mlp = at.share(grad_mlp_w)
    two_middle = at.sum_middle(two_pieces, behind(two_far, grad_mlp_w))
    mlp_part = dot(behind(hidden, grad_mlp_w), w_down, NT, jnp.bfloat16)
    two_near = at.sum_near(two_pieces, behind(two_middle, mlp_part))
    back_two = at.total(two_pieces, two_near)
    scaled_two = back_two * gain_two

    grad_after = dy.astype(jnp.float32) + scale_two * (
        scaled_two - normed_two * jnp.mean(scaled_two * normed_two, axis=1, keepdims=True)
    )
    dal = at.gather(grad_after.astype(jnp.bfloat16))
    mlp_pieces = at.split(behind(mlp_part, dal))
    mlp_far = at.sum_far(mlp_pieces)

    w_out_head = lax.dynamic_slice_in_dim(w_late, 3 * share_ff + head * HEAD_DIM, HEAD_DIM, 1)
    don = dot(behind(dal, mlp_pieces), w_out_head, NN)
    dq, dk, dv, dgate = backward_mix(q, k, v, gate, write, seg, saved, don)
    grad_pre = (jnp.concatenate([dq, dk, dv], axis=1) * swish_slope(pre)).astype(jnp.bfloat16)
    grad_hf = (dgate * jax.nn.sigmoid(-hf) / GATE_SOFTENING).astype(jnp.bfloat16)
    grad_proj = jnp.concatenate([grad_pre, grad_hf, jnp.zeros_like(grad_hf)], axis=1)
    bias_grad = jnp.sum(grad_hf.astype(jnp.float32), axis=0)
    bias_grad = jnp.concatenate([jnp.zeros((gate_end,), jnp.float32), bias_grad])
    row_ids = jnp.arange(width, dtype=jnp.int32)
    owners = SLOTS // bias_len
    holds = ((row_ids % rows == 0) & (row_ids // (rows * owners) == head)).astype(jnp.float32)
    mlp_middle = at.sum_middle(mlp_pieces, behind(mlp_far, grad_proj))
    grad_proj = behind(grad_proj, mlp_far)
    grad_attn_w = tn_pair(in_one, grad_proj, dal, low, 512, holds[:, None], bias_grad[None, -128:])
    share_attn = at.share(behind(grad_attn_w, share_mlp))
    one_part = dot(behind(grad_proj, grad_attn_w), w_in, NT, jnp.bfloat16)
    one_pieces = at.split(one_part)
    mlp_near = at.sum_near(mlp_pieces, behind(mlp_middle, grad_attn_w))
    one_far = at.sum_far(behind(one_pieces, mlp_middle))
    one_middle = at.sum_middle(one_pieces, one_far)
    mlp_out = at.total(mlp_pieces, behind(mlp_near, one_far))
    mixed_rows = (after + mlp_out).astype(jnp.bfloat16)
    mixed = at.swap(mixed_rows.reshape(phases, block_len, width))[None]
    one_near = at.sum_near(one_pieces, one_middle)
    back_one = at.total(one_pieces, one_near) / copies
    scaled_one = back_one * gain_one
    rest_float = rest.astype(jnp.float32)
    scale_one = rms_scale(rest_float)
    normed_one = rest_float * scale_one
    grad_rows = grad_after + scale_one * (
        scaled_one - normed_one * jnp.mean(scaled_one * normed_one, axis=1, keepdims=True)
    )
    grad_tokens = at.swap(grad_rows.reshape(phases, block_len, width))[None]

    mlp_home = at.home(behind(share_mlp, back_one))
    attn_home = at.home(share_attn, copies)

    gate_up_weight = mlp_weight[:, : 2 * FF].astype(jnp.float32)
    down = at.in_order([p[:, 2 * share_ff :] for p in mlp_home], at.slot, 1).astype(jnp.float32)
    gates = at.in_order([p[:, :share_ff] for p in mlp_home], at.slot, 1).astype(jnp.float32)
    ups = at.in_order([p[:, share_ff : 2 * share_ff] for p in mlp_home], at.slot, 1).astype(jnp.float32)
    grad_mlp = jnp.concatenate([gates, ups, down], axis=1)
    gain_grad_two = jnp.sum(grad_mlp[:, : 2 * FF] * gate_up_weight, axis=1) / norm2_gain.astype(jnp.float32)

    slot_head = at.slot // copies
    parts = [
        at.in_order([p[:, j * HEAD_DIM : (j + 1) * HEAD_DIM] for p in attn_home], slot_head, 1) for j in range(3)
    ]
    parts.append(at.in_order([p[:, qkv:gate_end] for p in attn_home], slot_head, 1))
    parts.append(at.in_order([p[:, gate_end + SLOTS :] for p in attn_home], slot_head, 1))
    grad_attn = jnp.concatenate(parts, axis=1).astype(jnp.float32)
    attn_float = attn_weight[:, :proj_cols].astype(jnp.float32)
    gain_grad_one = jnp.sum(grad_attn[:, :proj_cols] * attn_float, axis=1) / norm1_gain.astype(jnp.float32)
    bias_sums = sum(p[0, gate_end : gate_end + SLOTS].astype(jnp.float32) for p in attn_home)
    owner = lax.axis_index("seqs") * at.span + lax.axis_index("span")
    bias_home = lax.dynamic_slice_in_dim(bias_sums, owner % owners * bias_len, bias_len, 0)
    return (mixed, grad_tokens, grad_attn, grad_mlp, gain_grad_one, gain_grad_two, bias_home)


def solution(mesh):
    placed = (
        P("seqs", None, "span", None),
        P(("seqs", "span"), None),
        P(("seqs", "span"), None),
        P(("seqs", "span")),
        P(("seqs", "span")),
        P(("seqs", "span")),
        P("seqs", None, None),
        P("seqs", None, "span", None),
    )
    return jax.shard_map(
        local,
        mesh=mesh,
        in_specs=placed,
        out_specs=(
            P("seqs", None, "span", None),
            P("seqs", None, "span", None),
            P(("seqs", "span"), None),
            P(("seqs", "span"), None),
            P(("seqs", "span")),
            P(("seqs", "span")),
            P(("seqs", "span")),
        ),
        check_vma=False,
    )
```

time: 3300 us -> 636 us (0.19)
  waiting for transfers between devices: 2570 us -> 265 us
  matrix products: 364 us -> 45.9 us
  other arithmetic: 181 us -> 39.1 us
  starting transfers between devices: 0.65 us -> 121 us
  blocking collectives: 96.5 us -> 0 us
  Pallas kernels: 0 us -> 72.4 us
    reduce_scatter x4 -> x2, waiting for transfers between devices: 1960 us -> 0.96 us  [share(): lax.psum_scatter(value, ('seqs', 'span'), scatter_dimension=0, tiled=True...]
    all_gather x6 -> x2, waiting for transfers between devices: 607 us -> 0.02 us  [fetch(): lax.all_gather(value, ('seqs', 'span'), axis=0, tiled=True, axis_index_gr...]
    dot_general x188 -> x6, matrix products: 364 us -> 45.9 us  [dot(): lax.dot_general(a, b, (dims, ((), ())), preferred_element_type=jnp.float32)]
    ppermute x0 -> x55, waiting for transfers between devices: none -> 263 us  [the longest x28 93.8 us: between(): lax.ppermute(value, 'span', [(a * p + c, b * p + c) for a, b in pairs for...]
    ppermute x0 -> x55, starting transfers between devices: none -> 121 us  [the longest x28 44.1 us: between(): lax.ppermute(value, 'span', [(a * p + c, b * p + c) for a, b in pairs for...]
    unnamed x2 -> x0, blocking collectives: 83.6 us -> none
    reduce_sum x82 -> x5, other arithmetic: 81.5 us -> 1.74 us  [the longest x1 0.46 us: local(): jnp.mean(scaled_one * normed_one, axis=1, keepdims=True)]
    pallas_call x0 -> x5, Pallas kernels: none -> 72.4 us  [the longest x2 32.8 us: vmem_call(): pl.pallas_call(kernel, out_shape=outs, in_specs=[pl.BlockSpec(memory_spac...]
  transfers between devices with their start and end apart: 10 -> 59, of which waited for: 9 -> 27; matrix products, arithmetic and copies ran while one was open for 9% -> 15% of each run, Pallas kernels for 0% -> 7%
where the time goes in v1:
time: 636 us; the launch traced here: 627 us
  waiting for transfers between devices  265 us (42%)
  starting transfers between devices  121 us (19%)
  Pallas kernels  72.4 us (11%)
  local copies, waits for them, and re-layouts  68.6 us (11%)
  matrix products  45.9 us (7%)
  other arithmetic  39.1 us (6%)
  between operations  15.8 us (2%)
    ppermute x28, waiting for transfers between devices, between(): lax.ppermute(value, 'span', [(a * p + c, b * p + c) for a, b in pairs for...  93.8 us
    ppermute x8, waiting for transfers between devices, deal(): pieces.append(lax.ppermute(block, 'span', self.outward(k)))  65.7 us
    ppermute x8, waiting for transfers between devices, home(): lax.ppermute(block, 'span', [(b, a) for a, b in self.outward(k)])  60.7 us
    dot_general x6, matrix products, dot(): lax.dot_general(a, b, (dims, ((), ())), preferred_element_type=jnp.float32)  45.9 us
    ppermute x28, starting transfers between devices, between(): lax.ppermute(value, 'span', [(a * p + c, b * p + c) for a, b in pairs for...  44.1 us
    ppermute x7, waiting for transfers between devices, across(): lax.ppermute(value, 'span', [(i, i ^ step) for i in range(self.span)])  43.3 us
    pallas_call x2, Pallas kernels, vmem_call(): pl.pallas_call(kernel, out_shape=outs, in_specs=[pl.BlockSpec(memory_spac...  32.8 us
    ppermute x4, starting transfers between devices, swap(): got = lax.ppermute(other, 'span', [(i, i ^ 1) for i in range(self.span)])  23.5 us
  transfers between devices with their start and end apart: 59, of which 27 were waited for; matrix products, arithmetic and copies ran while one was open for 15% of the time, Pallas kernels for 7%

profile of v1, /device:TPU:5, one launch (start us, length us, event | category | flops | bytes accessed | tf_op | source)
XLA Modules:
  0.0 627.2 jit_solution(15759521854590579138)
XLA Ops:
  53.3 14.6 %collective-permute-done.6 = bf16[64,6272]{1,0:T(8,128)(2,1)S(1)} collective-permute-done((bf16[64,6272]{1,0:T(8,128)(2,1)S(1)}, bf16[64,6272]{1,0:T(8,128)(2,1)S(1)}, u32[]{:S(2)}, u32[]{:S(2)}) %collective-permute-start.6) | collective-permute-done | bytes 802848 | tf_op jit(solution)/shard_map/ppermute | solution.py:473
  67.9 48.9 %collective-permute-done.7 = bf16[64,6272]{1,0:T(8,128)(2,1)S(1)} collective-permute-done((bf16[64,6272]{1,0:T(8,128)(2,1)S(1)}, bf16[64,6272]{1,0:T(8,128)(2,1)S(1)}, u32[]{:S(2)}, u32[]{:S(2)}) %collective-permute-start.7) | collective-permute-done | bytes 802848 | tf_op jit(solution)/shard_map/ppermute | solution.py:473
  123.2 10.6 %collective-permute-done.10 = bf16[128,2048]{1,0:T(8,128)(2,1)} collective-permute-done((bf16[128,2048]{1,0:T(8,128)(2,1)}, bf16[128,2048]{1,0:T(8,128)(2,1)}, u32[]{:S(2)}, u32[]{:S(2)}) %collective-permute-start.10) | collective-permute-done | bytes 524320 | tf_op jit(solution)/shard_map/ppermute | solution.py:389
  137.3 10.7 %collective-permute-done.13 = bf16[128,2048]{1,0:T(8,128)(2,1)} collective-permute-done((bf16[128,2048]{1,0:T(8,128)(2,1)}, bf16[128,2048]{1,0:T(8,128)(2,1)}, u32[]{:S(2)}, u32[]{:S(2)}) %collective-permute-start.13) | collective-permute-done | bytes 524320 | tf_op jit(solution)/shard_map/ppermute | solution.py:408
  151.6 8.3 %collective-permute-done.14 = bf16[128,2048]{1,0:T(8,128)(2,1)S(1)} collective-permute-done((bf16[128,2048]{1,0:T(8,128)(2,1)}, bf16[128,2048]{1,0:T(8,128)(2,1)S(1)}, u32[]{:S(2)}, u32[]{:S(2)}) %collective-permute-start.14) | collective-permute-done | bytes 524320 | tf_op jit(solution)/shard_map/ppermute | solution.py:408
  175.3 14.5 %shard_map.135 = (bf16[512,512]{1,0:T(8,128)(2,1)S(1)}, f32[512,512]{1,0:T(8,128)S(1)}, f32[512,64]{1,0:T(8,128)S(1)}, f32[512,64]{1,0:T(8,128)S(1)}, f32[512,64...) custom-call(bf16[512,512]{1,0:T(8,128)(2,1)S(1)} %get-tuple-element.213.q_ref, ...), custom_call_target="tpu_custom_call" | custom-call | flops 268435456 | bytes 6033408 | tf_op jit(solution)/shard_map/pallas_call | solution.py:241
  207.2 11.1 %collective-permute-done.20 = bf16[512,512]{1,0:T(8,128)(2,1)S(1)} collective-permute-done((bf16[512,512]{1,0:T(8,128)(2,1)S(1)}, bf16[512,512]{1,0:T(8,128)(2,1)S(1)}, u32[]{:S(2)}, u32[]{:S(2)}) %collective-permute-start.20) | collective-permute-done | bytes 524320 | tf_op jit(solution)/shard_map/ppermute | solution.py:408
  224.6 9.1 %collective-permute-done.21 = bf16[512,512]{1,0:T(8,128)(2,1)} collective-permute-done((bf16[512,512]{1,0:T(8,128)(2,1)}, bf16[512,512]{1,0:T(8,128)(2,1)}, u32[]{:S(2)}, u32[]{:S(2)}) %collective-permute-start.21) | collective-permute-done | bytes 524320 | tf_op jit(solution)/shard_map/ppermute | solution.py:408
  240.2 9.3 %collective-permute-done.23 = bf16[128,2048]{1,0:T(8,128)(2,1)} collective-permute-done((bf16[128,2048]{1,0:T(8,128)(2,1)}, bf16[128,2048]{1,0:T(8,128)(2,1)}, u32[]{:S(2)}, u32[]{:S(2)}) %collective-permute-start.23) | collective-permute-done | bytes 524320 | tf_op jit(solution)/shard_map/ppermute | solution.py:408
  262.9 9.3 %multiply_reduce_fusion = (f32[512]{0:T(512)S(1)}, f32[512,2048]{1,0:T(8,128)S(1)}) fusion(bf16[512,2048]{1,0:T(8,128)(2,1)} %select_dynamic-update-slice_fusion.4, bf16[2048,6272]{1,0:T(8,128)(2,1)} %all-gather.5.cloned.1.call-done.w_ref, bf16[512,2048]{1,0:T(8,128)(2,1)} %copy-done.18), kind=kOutput, calls=%fused_computation.14 | convolution fusion | flops 4299161088 | bytes 16779264 | tf_op jit(solution)/shard_map/dot_general | solution.py:281
  275.9 16.8 %shard_map.136 = (bf16[512,1408]{1,0:T(8,128)(2,1)}, bf16[512,2816]{1,0:T(8,128)(2,1)}) custom-call(bf16[512,2048]{1,0:T(8,128)(2,1)} %multiply_convert_fusion.x_ref.a_ref, bf16[512,2048]{1,0:T(8,128)(2,1)} %select_dynamic-update-slice_fusion.2.y_ref.c_ref, bf16[2048,6272]{1,0:T(8,128)(2,1)} %all-gather.5.cloned.1.call-done.w_ref), custom_call_target="tpu_custom_call" | custom-call | flops 8858370048 | bytes 17301504 | tf_op jit(solution)/shard_map/pallas_call | solution.py:362
  292.7 9.9 %fusion.12 = bf16[512,2048]{1,0:T(8,128)(2,1)S(1)} fusion(bf16[512,2816]{1,0:T(8,128)(2,1)} %get-tuple-element.142.b_ref, bf16[2048,6272]{1,0:T(8,128)(2,1)} %all-gather.5.cloned.1.call-done.w_ref), kind=kOutput, calls=%fused_computation.20 | convolution fusion | flops 5906628608 | bytes 16515072 | tf_op jit(solution)/shard_map/dot_general | solution.py:281
  305.7 14.5 %shard_map.137 = bf16[2048,4224]{1,0:T(8,128)(2,1)} custom-call(bf16[512,2048]{1,0:T(8,128)(2,1)S(1)} %copy-done, bf16[512,2816]{1,0:T(8,128)(2,1)} %get-tuple-element.142.b_ref, bf16[512,2048]{1,0:T(8,128)(2,1)} %select_dynamic-update-slice_fusion.2.y_ref.c_ref, bf16[512,1408]{1,0:T(8,128)(2,1)S(1)} %copy-done.17, f32[2048,128]{1,0:T(8,128)S(1)} %broadcast_in_dim.26.e_ref, ...), custom_call_target="tpu_custom_call" | custom-call | flops 8858370048 | bytes 17301504 | tf_op jit(solution)/shard_map/pallas_call | solution.py:328
  346.6 8.5 %collective-permute-done.28 = bf16[128,2048]{1,0:T(8,128)(2,1)S(1)} collective-permute-done((bf16[128,2048]{1,0:T(8,128)(2,1)S(1)}, bf16[128,2048]{1,0:T(8,128)(2,1)S(1)}, u32[]{:S(2)}, u32[]{:S(2)}) %collective-permute-start.28) | collective-permute-done | bytes 524320 | tf_op jit(solution)/shard_map/ppermute | solution.py:389
  362.3 8.1 %collective-permute-done.30 = bf16[128,2048]{1,0:T(8,128)(2,1)} collective-permute-done((bf16[128,2048]{1,0:T(8,128)(2,1)S(1)}, bf16[128,2048]{1,0:T(8,128)(2,1)}, u32[]{:S(2)}, u32[]{:S(2)}) %collective-permute-start.30) | collective-permute-done | bytes 524320 | tf_op jit(solution)/shard_map/ppermute | solution.py:389
  373.3 21.2 %collective-permute-done.33 = bf16[128,2048]{1,0:T(8,128)(2,1)} collective-permute-done((bf16[128,2048]{1,0:T(8,128)(2,1)}, bf16[128,2048]{1,0:T(8,128)(2,1)}, u32[]{:S(2)}, u32[]{:S(2)}) %collective-permute-start.33) | collective-permute-done | bytes 524320 | tf_op jit(solution)/shard_map/ppermute | solution.py:408
  399.9 8.6 %collective-permute-done.34 = bf16[128,2048]{1,0:T(8,128)(2,1)S(1)} collective-permute-done((bf16[128,2048]{1,0:T(8,128)(2,1)}, bf16[128,2048]{1,0:T(8,128)(2,1)S(1)}, u32[]{:S(2)}, u32[]{:S(2)}) %collective-permute-start.34) | collective-permute-done | bytes 524320 | tf_op jit(solution)/shard_map/ppermute | solution.py:408
  417.7 18.3 %shard_map.138 = (f32[512,512]{1,0:T(8,128)S(1)}, f32[512,512]{1,0:T(8,128)S(1)}, f32[512,512]{1,0:T(8,128)}, f32[512,64]{1,0:T(8,128)S(1)}) custom-call(bf16[512,512]{1,0:T(8,128)(2,1)S(1)} %get-tuple-element.213.q_ref, bf16[512,512]{1,0:T(8,128)(2,1)S(1)} %get-tuple-element.212.k_ref, bf16[512,512]{1,0:T(8,128)(2,1)S(1)} %get-tuple-element.211.v_ref, ...), custom_call_target="tpu_custom_call" | custom-call | flops 671088640 | bytes 9834496 | tf_op jit(solution)/shard_map/pallas_call | solution.py:241
  445.8 8.4 %shard_map.139 = bf16[2048,2176]{1,0:T(8,128)(2,1)} custom-call(bf16[512,2048]{1,0:T(8,128)(2,1)S(1)} %copy-done.2, bf16[512,1664]{1,0:T(8,128)(2,1)S(1)} %copy-done.3, bf16[512,2048]{1,0:T(8,128)(2,1)} %select_dynamic-update-slice_fusion.c_ref, bf16[512,512]{1,0:T(8,128)(2,1)S(1)} %copy-done.8, f32[2048,1]{1,0:T(8,128)S(1)} %fusion.30.e_ref, ...), custom_call_target="tpu_custom_call" | custom-call | flops 4563402752 | bytes 8912896 | tf_op jit(solution)/shard_map/pallas_call | solution.py:328
  490.6 17.3 %collective-permute-start.41 = (bf16[64,2048]{1,0:T(8,128)(2,1)S(1)}, bf16[64,2048]{1,0:T(8,128)(2,1)S(1)}, u32[]{:S(2)}, u32[]{:S(2)}) collective-permute-start(bf16[64,2048]{1,0:T(8,128)(2,1)S(1)} %dynamic-slice_bitcast_fusion.13), channel_id=1, source_target_pairs={{0,1},{1,0},{2,3},{3,2},{4,5},{5,4},{6,7},{7,6},{8,9},{9,8},{10,11... | collective-permute-start | bytes 786440 | tf_op jit(solution)/shard_map/ppermute | solution.py:402
  541.7 11.3 %collective-permute-done.52 = bf16[64,4224]{1,0:T(8,128)(2,1)S(1)} collective-permute-done((bf16[64,4224]{1,0:T(8,128)(2,1)S(1)}, bf16[64,4224]{1,0:T(8,128)(2,1)S(1)}, u32[]{:S(2)}, u32[]{:S(2)}) %collective-permute-start.52) | collective-permute-done | bytes 540704 | tf_op jit(solution)/shard_map/ppermute | solution.py:481
  553.1 9.6 %collective-permute-done.53 = bf16[64,4224]{1,0:T(8,128)(2,1)S(1)} collective-permute-done((bf16[64,4224]{1,0:T(8,128)(2,1)S(1)}, bf16[64,4224]{1,0:T(8,128)(2,1)S(1)}, u32[]{:S(2)}, u32[]{:S(2)}) %collective-permute-start.53) | collective-permute-done | bytes 540704 | tf_op jit(solution)/shard_map/ppermute | solution.py:481
  562.8 17.3 %collective-permute-done.54 = bf16[64,4224]{1,0:T(8,128)(2,1)S(1)} collective-permute-done((bf16[64,4224]{1,0:T(8,128)(2,1)S(1)}, bf16[64,4224]{1,0:T(8,128)(2,1)S(1)}, u32[]{:S(2)}, u32[]{:S(2)}) %collective-permute-start.54) | collective-permute-done | bytes 540704 | tf_op jit(solution)/shard_map/ppermute | solution.py:481
  602.5 8.6 %collective-permute-done.50 = bf16[64,2176]{1,0:T(8,128)(2,1)S(1)} collective-permute-done((bf16[64,2176]{1,0:T(8,128)(2,1)S(1)}, bf16[64,2176]{1,0:T(8,128)(2,1)S(1)}, u32[]{:S(2)}, u32[]{:S(2)}) %collective-permute-start.50) | collective-permute-done | bytes 278560 | tf_op jit(solution)/shard_map/ppermute | solution.py:481
  (393 shorter events, 286.8 us)
Async XLA Ops:
  7.2 110.2 %all-gather.3.cloned.1.call-start = ((), (), s32[]{:S(2)}) async-start(), calls=%async_computation.2 | async-start | bytes 7667712 | tf_op jit(solution)/shard_map/all_gather | solution.py:485
  9.0 24.1 %collective-permute-start.5 = (bf16[64,2048]{1,0:T(8,128)(2,1)}, bf16[64,2048]{1,0:T(8,128)(2,1)}, u32[]{:S(2)}, u32[]{:S(2)}) collective-permute-start(bf16[64,2048]{1,0:T(8,128)(2,1)} %dynamic-slice_bitcast_fusion.14), channel_id=1, source_target_pairs={{0,1},{1,0},{2,3},{3,2},{4,5},{5,4},{6,7},{7,6},{8,9},{9,8},{10,11... | collective-permute-start | bytes 786440 | tf_op jit(solution)/shard_map/ppermute | solution.py:402
  15.1 21.3 %collective-permute-start.1 = (bf16[64,1664]{1,0:T(8,128)(2,1)}, bf16[64,1664]{1,0:T(8,128)(2,1)}, u32[]{:S(2)}, u32[]{:S(2)}) collective-permute-start(bf16[64,1664]{1,0:T(8,128)(2,1)} %get-tuple-element.221), channel_id=1, source_target_pairs={{0,0},{1,2},{2,4},{3,6},{4,1},{5,3},{6,5},{7,7},{8,8},{9,10},{10,1... | collective-permute-start | bytes 638984 | tf_op jit(solution)/shard_map/ppermute | solution.py:473
  18.2 20.4 %collective-permute-start.2 = (bf16[64,1664]{1,0:T(8,128)(2,1)}, bf16[64,1664]{1,0:T(8,128)(2,1)}, u32[]{:S(2)}, u32[]{:S(2)}) collective-permute-start(bf16[64,1664]{1,0:T(8,128)(2,1)} %get-tuple-element.220), channel_id=1, source_target_pairs={{0,2},{1,0},{2,6},{3,4},{4,3},{5,1},{6,7},{7,5},{8,10},{9,8},{10,1... | collective-permute-start | bytes 638984 | tf_op jit(solution)/shard_map/ppermute | solution.py:473
  18.6 20.0 %collective-permute-start.3 = (bf16[64,1664]{1,0:T(8,128)(2,1)}, bf16[64,1664]{1,0:T(8,128)(2,1)}, u32[]{:S(2)}, u32[]{:S(2)}) collective-permute-start(bf16[64,1664]{1,0:T(8,128)(2,1)} %get-tuple-element.219), channel_id=1, source_target_pairs={{0,4},{1,6},{2,0},{3,2},{4,5},{5,7},{6,1},{7,3},{8,12},{9,14},{10,... | collective-permute-start | bytes 638984 | tf_op jit(solution)/shard_map/ppermute | solution.py:473
  43.7 219.3 %all-gather.5.cloned.1.call-start = ((), (), s32[]{:S(2)}) async-start(), calls=%async_computation.3 | async-start | bytes 28901376 | tf_op jit(solution)/shard_map/all_gather | solution.py:485
  44.4 23.5 %collective-permute-start.6 = (bf16[64,6272]{1,0:T(8,128)(2,1)S(1)}, bf16[64,6272]{1,0:T(8,128)(2,1)S(1)}, u32[]{:S(2)}, u32[]{:S(2)}) collective-permute-start(bf16[64,6272]{1,0:T(8,128)(2,1)S(1)} %get-tuple-element.194), channel_id=1, source_target_pairs={{0,0},{1,2},{2,4},{3,6},{4,1},{5,3},{6,5},{7,7},{8,8},{9,10},{10,1... | collective-permute-start | bytes 2408456 | tf_op jit(solution)/shard_map/ppermute | solution.py:473
  46.7 70.0 %collective-permute-start.7 = (bf16[64,6272]{1,0:T(8,128)(2,1)S(1)}, bf16[64,6272]{1,0:T(8,128)(2,1)S(1)}, u32[]{:S(2)}, u32[]{:S(2)}) collective-permute-start(bf16[64,6272]{1,0:T(8,128)(2,1)S(1)} %get-tuple-element.193), channel_id=1, source_target_pairs={{0,2},{1,0},{2,6},{3,4},{4,3},{5,1},{6,7},{7,5},{8,10},{9,8},{10,1... | collective-permute-start | bytes 2408456 | tf_op jit(solution)/shard_map/ppermute | solution.py:473
  46.8 69.9 %collective-permute-start.8 = (bf16[64,6272]{1,0:T(8,128)(2,1)S(1)}, bf16[64,6272]{1,0:T(8,128)(2,1)S(1)}, u32[]{:S(2)}, u32[]{:S(2)}) collective-permute-start(bf16[64,6272]{1,0:T(8,128)(2,1)S(1)} %get-tuple-element.192), channel_id=1, source_target_pairs={{0,4},{1,6},{2,0},{3,2},{4,5},{5,7},{6,1},{7,3},{8,12},{9,14},{10,... | collective-permute-start | bytes 2408456 | tf_op jit(solution)/shard_map/ppermute | solution.py:473
  49.7 67.0 %collective-permute-start.9 = (bf16[64,6272]{1,0:T(8,128)(2,1)S(1)}, bf16[64,6272]{1,0:T(8,128)(2,1)S(1)}, u32[]{:S(2)}, u32[]{:S(2)}) collective-permute-start(bf16[64,6272]{1,0:T(8,128)(2,1)S(1)} %get-tuple-element.191), channel_id=1, source_target_pairs={{0,6},{1,4},{2,2},{3,0},{4,7},{5,5},{6,3},{7,1},{8,14},{9,12},{10,... | collective-permute-start | bytes 2408456 | tf_op jit(solution)/shard_map/ppermute | solution.py:473
  119.1 336.1 %reduce-scatter.3.cloned.1.call-start = ((), (), s32[]{:S(2)}) async-start(), calls=%async_computation.4 | async-start | bytes 19464192 | tf_op jit(solution)/shard_map/reduce_scatter | solution.py:488
  160.0 34.5 %collective-permute-start.15 = (bf16[128,2048]{1,0:T(8,128)(2,1)S(1)}, bf16[128,2048]{1,0:T(8,128)(2,1)}, u32[]{:S(2)}, u32[]{:S(2)}) collective-permute-start(bf16[128,2048]{1,0:T(8,128)(2,1)S(1)} %bitcast.135), channel_id=1, source_target_pairs={{0,2},{1,3},{2,0},{3,1},{4,6},{5,7},{6,4},{7,5},{8,10},{9,11},{10,... | collective-permute-start | bytes 1572872 | tf_op jit(solution)/shard_map/ppermute | solution.py:389
  160.4 34.2 %collective-permute-start.16 = (bf16[128,2048]{1,0:T(8,128)(2,1)S(1)}, bf16[128,2048]{1,0:T(8,128)(2,1)}, u32[]{:S(2)}, u32[]{:S(2)}) collective-permute-start(bf16[128,2048]{1,0:T(8,128)(2,1)S(1)} %bitcast.136), channel_id=1, source_target_pairs={{2,4},{3,5},{4,2},{5,3},{10,12},{11,13},{12,10},{13,11},{18,20},{1... | collective-permute-start | bytes 1572872 | tf_op jit(solution)/shard_map/ppermute | solution.py:408
  320.2 262.6 %reduce-scatter.5.cloned.1.call-start = ((), (), s32[]{:S(2)}) async-start(), calls=%async_computation.5 | async-start | bytes 10027008 | tf_op jit(solution)/shard_map/reduce_scatter | solution.py:488
  371.9 22.6 %collective-permute-start.33 = (bf16[128,2048]{1,0:T(8,128)(2,1)}, bf16[128,2048]{1,0:T(8,128)(2,1)}, u32[]{:S(2)}, u32[]{:S(2)}) collective-permute-start(bf16[128,2048]{1,0:T(8,128)(2,1)} %collective-permute-done.31), channel_id=1, source_target_pairs={{2,0},{3,1},{4,6},{5,7},{10,8},{11,9},{12,14},{13,15},{18,16},{19,... | collective-permute-start | bytes 1572872 | tf_op jit(solution)/shard_map/ppermute | solution.py:408
  410.7 32.5 %collective-permute-start.35 = (bf16[128,2048]{1,0:T(8,128)(2,1)}, bf16[128,2048]{1,0:T(8,128)(2,1)}, u32[]{:S(2)}, u32[]{:S(2)}) collective-permute-start(bf16[128,2048]{1,0:T(8,128)(2,1)} %get-tuple-element.204), channel_id=1, source_target_pairs={{0,2},{1,3},{6,4},{7,5},{8,10},{9,11},{14,12},{15,13},{16,18},{17,... | collective-permute-start | bytes 1572872 | tf_op jit(solution)/shard_map/ppermute | solution.py:408
  475.8 32.2 %collective-permute-start.43 = (bf16[128,2048]{1,0:T(8,128)(2,1)S(1)}, bf16[128,2048]{1,0:T(8,128)(2,1)S(1)}, u32[]{:S(2)}, u32[]{:S(2)}) collective-permute-start(bf16[128,2048]{1,0:T(8,128)(2,1)S(1)} %get-tuple-element.200), channel_id=1, source_target_pairs={{0,2},{1,3},{6,4},{7,5},{8,10},{9,11},{14,12},{15,13},{16,18},{17,... | collective-permute-start | bytes 1572872 | tf_op jit(solution)/shard_map/ppermute | solution.py:408
  484.2 23.7 %collective-permute-start.42 = (bf16[128,2048]{1,0:T(8,128)(2,1)S(1)}, bf16[128,2048]{1,0:T(8,128)(2,1)S(1)}, u32[]{:S(2)}, u32[]{:S(2)}) collective-permute-start(bf16[128,2048]{1,0:T(8,128)(2,1)S(1)} %add_convert_fusion.2), channel_id=1, source_target_pairs={{2,4},{3,5},{4,2},{5,3},{10,12},{11,13},{12,10},{13,11},{18,20},{1... | collective-permute-start | bytes 1572872 | tf_op jit(solution)/shard_map/ppermute | solution.py:408
  490.6 20.9 %collective-permute-start.41 = (bf16[64,2048]{1,0:T(8,128)(2,1)S(1)}, bf16[64,2048]{1,0:T(8,128)(2,1)S(1)}, u32[]{:S(2)}, u32[]{:S(2)}) collective-permute-start(bf16[64,2048]{1,0:T(8,128)(2,1)S(1)} %dynamic-slice_bitcast_fusion.13), channel_id=1, source_target_pairs={{0,1},{1,0},{2,3},{3,2},{4,5},{5,4},{6,7},{7,6},{8,9},{9,8},{10,11... | collective-permute-start | bytes 786440 | tf_op jit(solution)/shard_map/ppermute | solution.py:402
  524.7 16.7 %collective-permute-start.51 = (bf16[64,4224]{1,0:T(8,128)(2,1)S(1)}, bf16[64,4224]{1,0:T(8,128)(2,1)S(1)}, u32[]{:S(2)}, u32[]{:S(2)}) collective-permute-start(bf16[64,4224]{1,0:T(8,128)(2,1)S(1)} %get-tuple-element.198), channel_id=1, source_target_pairs={{0,0},{2,1},{4,2},{6,3},{1,4},{3,5},{5,6},{7,7},{8,8},{10,9},{12,1... | collective-permute-start | bytes 1622024 | tf_op jit(solution)/shard_map/ppermute | solution.py:481
  532.6 20.5 %collective-permute-start.52 = (bf16[64,4224]{1,0:T(8,128)(2,1)S(1)}, bf16[64,4224]{1,0:T(8,128)(2,1)S(1)}, u32[]{:S(2)}, u32[]{:S(2)}) collective-permute-start(bf16[64,4224]{1,0:T(8,128)(2,1)S(1)} %get-tuple-element.197), channel_id=1, source_target_pairs={{2,0},{0,1},{6,2},{4,3},{3,4},{1,5},{7,6},{5,7},{10,8},{8,9},{14,1... | collective-permute-start | bytes 1622024 | tf_op jit(solution)/shard_map/ppermute | solution.py:481
  532.6 30.1 %collective-permute-start.53 = (bf16[64,4224]{1,0:T(8,128)(2,1)S(1)}, bf16[64,4224]{1,0:T(8,128)(2,1)S(1)}, u32[]{:S(2)}, u32[]{:S(2)}) collective-permute-start(bf16[64,4224]{1,0:T(8,128)(2,1)S(1)} %get-tuple-element.196), channel_id=1, source_target_pairs={{4,0},{6,1},{0,2},{2,3},{5,4},{7,5},{1,6},{3,7},{12,8},{14,9},{8,1... | collective-permute-start | bytes 1622024 | tf_op jit(solution)/shard_map/ppermute | solution.py:481
  534.7 45.3 %collective-permute-start.54 = (bf16[64,4224]{1,0:T(8,128)(2,1)S(1)}, bf16[64,4224]{1,0:T(8,128)(2,1)S(1)}, u32[]{:S(2)}, u32[]{:S(2)}) collective-permute-start(bf16[64,4224]{1,0:T(8,128)(2,1)S(1)} %get-tuple-element.195), channel_id=1, source_target_pairs={{6,0},{4,1},{2,2},{0,3},{7,4},{5,5},{3,6},{1,7},{14,8},{12,9},{10,... | collective-permute-start | bytes 1622024 | tf_op jit(solution)/shard_map/ppermute | solution.py:481
  591.3 19.8 %collective-permute-start.50 = (bf16[64,2176]{1,0:T(8,128)(2,1)S(1)}, bf16[64,2176]{1,0:T(8,128)(2,1)S(1)}, u32[]{:S(2)}, u32[]{:S(2)}) collective-permute-start(bf16[64,2176]{1,0:T(8,128)(2,1)S(1)} %get-tuple-element.214), channel_id=1, source_target_pairs={{6,0},{4,1},{2,2},{0,3},{7,4},{5,5},{3,6},{1,7},{14,8},{12,9},{10,... | collective-permute-start | bytes 835592 | tf_op jit(solution)/shard_map/ppermute | solution.py:481
  (98 other events, 703.3 us)
Sparse Core Ops, SparseCore 0:
  43.8 48.4 all-gather.2
  119.2 129.7 all-gather.4
  320.4 134.7 reduce-scatter.2
  459.0 81.0 reduce-scatter.4

commit v2 on v1

v2 whole, which is shorter than its diff:
```python
import functools
import jax
import jax.numpy as jnp
from jax import lax
from jax.experimental import pallas as pl
from jax.experimental.pallas import tpu as pltpu
from jax.sharding import PartitionSpec as P

BLOCK = 64
GATE_SOFTENING = 8.0
SUB = 16
SLOTS = 64
HEAD_DIM = 512
NORM_EPS = 1e-05


def mm(a, b, dims):
    return lax.dot_general(
        a.astype(jnp.bfloat16), b.astype(jnp.bfloat16), (dims, ((), ())), preferred_element_type=jnp.float32
    )


def halves(a):
    if a.dtype == jnp.bfloat16:
        return a, None
    high = a.astype(jnp.bfloat16)
    return high, (a - high.astype(jnp.float32)).astype(jnp.bfloat16)


def fine(a, b, dims):
    (a_high, a_low), (b_high, b_low) = halves(a), halves(b)
    out = mm(a_high, b_high, dims)
    if b_low is not None:
        out = out + mm(a_high, b_low, dims)
    if a_low is not None:
        out = out + mm(a_low, b_high, dims)
    return out


NN, NT, TN = ((1,), (0,)), ((1,), (1,)), ((0,), (0,))


def nn(a, b):
    return mm(a, b, NN)


def nt(a, b):
    return mm(a, b, NT)


def tn(a, b):
    return mm(a, b, TN)


def exact(a, b):
    return lax.dot_general(
        a, b, (((1,), (0,)), ((), ())), precision=lax.Precision.HIGHEST, preferred_element_type=jnp.float32
    )


def iota(shape, dim):
    return lax.broadcasted_iota(jnp.int32, shape, dim)


def block_decay(gate, write, seg_col, seg_row, seg_prev):
    row, col = iota((BLOCK, BLOCK), 0), iota((BLOCK, BLOCK), 1)
    same = jnp.where((seg_col == seg_row) & (row >= col), 1.0, 0.0)
    lower = jnp.where(row >= col, 1.0, 0.0)
    cum = exact(lower, gate)
    total = cum[BLOCK - 1 :]
    carry = jnp.where(seg_col == seg_prev, 1.0, 0.0)
    last = jnp.where(seg_col == seg_col[BLOCK - 1 :], 1.0, 0.0)
    enter = jnp.exp(cum) * carry
    tail = jnp.exp(total - cum) * last
    fade = jnp.exp(total) * carry[BLOCK - 1 :]
    falls, rises = [], []
    for i in range(1, BLOCK // SUB):
        base = cum[i * SUB - 1 : i * SUB]
        falls.append(jnp.exp(cum[i * SUB : (i + 1) * SUB] - base))
        rises.append(jnp.exp(base - cum[: i * SUB]))
    return same, cum, enter, tail, fade, falls, rises


def diagonal(square):
    return jnp.concatenate([square[i : i + SUB, i : i + SUB] for i in range(0, BLOCK, SUB)], axis=0)


def undiagonal(strip):
    row, col = iota((BLOCK, BLOCK), 0), iota((BLOCK, BLOCK), 1)
    wide = jnp.concatenate([strip] * (BLOCK // SUB), axis=1)
    return jnp.where(row // SUB == col // SUB, wide, 0.0)


def parts(values):
    return values.reshape(BLOCK // SUB, SUB, values.shape[-1])


def decay_at(cum, j):
    cum_parts = parts(cum)
    return jnp.exp(jnp.minimum(cum_parts - cum_parts[:, j : j + 1], 0.0))


def over_sources(pairs, cum, write, falls, rises):
    strip = parts(diagonal(pairs))
    write_parts = parts(write)
    near = jnp.zeros((BLOCK // SUB, SUB, SLOTS), jnp.float32)
    for j in range(SUB):
        near = near + strip[:, :, j : j + 1] * (decay_at(cum, j) * write_parts[:, j : j + 1])
    near = near.reshape(BLOCK, SLOTS)
    far = [jnp.zeros((SUB, SLOTS), jnp.float32)]
    for i in range(1, BLOCK // SUB):
        rows = pairs[i * SUB : (i + 1) * SUB, : i * SUB]
        far.append(falls[i - 1] * fine(rows, rises[i - 1] * write[: i * SUB], NN))
    return near + jnp.concatenate(far, axis=0)


def over_slots(values, cum, write, falls, rises):
    value_parts, write_parts = parts(values), parts(write)
    lane = iota((BLOCK // SUB, SUB, SUB), 2)
    strip = jnp.zeros((BLOCK // SUB, SUB, SUB), jnp.float32)
    for j in range(SUB):
        term = value_parts * (decay_at(cum, j) * write_parts[:, j : j + 1])
        strip = jnp.where(lane == j, jnp.sum(term, axis=2, keepdims=True), strip)
    out = undiagonal(strip.reshape(BLOCK, SUB))
    far = [jnp.zeros((SUB, BLOCK), jnp.float32)]
    for i in range(1, BLOCK // SUB):
        rows = values[i * SUB : (i + 1) * SUB] * falls[i - 1]
        piece = fine(rows, rises[i - 1] * write[: i * SUB], NT)
        far.append(jnp.concatenate([piece, jnp.zeros((SUB, BLOCK - i * SUB), jnp.float32)], axis=1))
    return out + jnp.concatenate(far, axis=0)


def over_targets(pairs_values, cum, falls, rises):
    row = iota((BLOCK // SUB, SUB, SLOTS), 1)
    near = jnp.zeros((BLOCK // SUB, SUB, SLOTS), jnp.float32)
    strips = [(parts(diagonal(p)), parts(v)) for p, v in pairs_values]
    for j in range(SUB):
        term = sum(strip[:, :, j : j + 1] * value for strip, value in strips) * decay_at(cum, j)
        near = jnp.where(row == j, jnp.sum(term, axis=1, keepdims=True), near)
    out = near.reshape(BLOCK, SLOTS)
    far = jnp.zeros((BLOCK, SLOTS), jnp.float32)
    for i in range(1, BLOCK // SUB):
        here = slice(i * SUB, (i + 1) * SUB)
        piece = sum(fine(p[here, : i * SUB], v[here] * falls[i - 1], TN) for p, v in pairs_values)
        piece = rises[i - 1] * piece
        far = far + jnp.concatenate([piece, jnp.zeros((BLOCK - i * SUB, SLOTS), jnp.float32)], axis=0)
    return out + far


QKV = 3 * HEAD_DIM
GATE_END = QKV + SLOTS


def load_block(i, proj_ref, bias_ref, segc_ref, segr_ref):
    here = pl.ds(pl.multiple_of(i * BLOCK, BLOCK), BLOCK)
    pre = proj_ref[here, :QKV]
    sig = jax.nn.sigmoid(pre)
    feats = (pre * sig).astype(jnp.bfloat16)
    q, k, v = (feats[:, n * HEAD_DIM : (n + 1) * HEAD_DIM] for n in range(3))
    logits = proj_ref[here, QKV:GATE_END] + bias_ref[...]
    gate = (jnp.minimum(logits, 0.0) - jnp.log1p(jnp.exp(-jnp.abs(logits)))) / GATE_SOFTENING
    seg_prev = jnp.where(i > 0, segc_ref[pl.ds(jnp.maximum(i * BLOCK - 1, 0), 1), :], -1)
    return here, pre, sig, q, k, v, logits, gate, -small_exp(gate), segc_ref[here, :], segr_ref[i], seg_prev


def small_exp(x):
    near = x * (1.0 + x / 2 * (1.0 + x / 3 * (1.0 + x / 4 * (1.0 + x / 5 * (1.0 + x / 6)))))
    return jnp.where(x > -0.1, near, jnp.exp(x) - 1.0)


def forward_kernel(proj_ref, bias_ref, segc_ref, segr_ref, low_ref, out_hbm, small_hbm, states_hbm,
                   out_ref, small_ref, states_ref, state, sems):
    scale = HEAD_DIM ** -0.5
    blocks = proj_ref.shape[0] // BLOCK
    state[...] = jnp.zeros_like(state)

    def copies(i):
        here = pl.ds(pl.multiple_of(i * BLOCK, BLOCK), BLOCK)
        return [
            pltpu.make_async_copy(a, b, sems.at[n, i])
            for n, (a, b) in enumerate(
                [
                    (out_ref.at[here], out_hbm.at[here]),
                    (small_ref.at[here], small_hbm.at[here]),
                    (states_ref.at[i], states_hbm.at[i]),
                ]
            )
        ]

    def step(i, _):
        here, _, _, q, k, v, _, gate, write, seg_col, seg_row, seg_prev = load_block(i, proj_ref, bias_ref, segc_ref, segr_ref)
        same, cum, enter, tail, fade, falls, rises = block_decay(gate, write, seg_col, seg_row, seg_prev)
        keys_in, values_in = state[:SLOTS], state[SLOTS:]
        states_ref[i] = state[...]
        keep = fade.reshape(SLOTS, 1)
        send = tail * write
        state[:SLOTS] = keep * keys_in + tn(send, k)
        state[SLOTS:] = keep * values_in + fine(send, v, TN)
        pairs = nt(q, k) * same
        score = scale * (over_sources(pairs, cum, write, falls, rises) + enter * nt(q, keys_in))
        prob = jnp.exp(score - jnp.max(score, axis=1, keepdims=True))
        prob = prob / jnp.sum(prob, axis=1, keepdims=True)
        mix = over_slots(prob, cum, write, falls, rises) * same
        out = fine(mix, v, NN) + fine(prob * enter, values_in, NN)
        low_ref[here, :] = (out * lax.rsqrt(jnp.mean(out * out, axis=1, keepdims=True) + NORM_EPS)).astype(jnp.bfloat16)
        out_ref[here, :] = out
        small_ref[here, :] = jnp.concatenate([score, prob, pairs, mix], axis=1)
        for copy in copies(i):
            copy.start()
        return 0

    lax.fori_loop(0, blocks, step, 0, unroll=4)

    def finish(i, _):
        for copy in copies(i):
            copy.wait()
        return 0

    lax.fori_loop(0, blocks, finish, 0)


def backward_kernel(proj_ref, bias_ref, segc_ref, segr_ref, out_ref, small_ref, states_ref, don_ref,
                    grad_ref, bias_grad_ref, state, state_next):
    scale = HEAD_DIM ** -0.5
    blocks = proj_ref.shape[0] // BLOCK
    state[...] = jnp.zeros_like(state)
    state_next[...] = jnp.zeros_like(state)
    bias_grad_ref[...] = jnp.zeros_like(bias_grad_ref)

    def step(lap, _):
        i = blocks - 1 - lap
        here, pre, sig, q, k, v, logits, gate, write, seg_col, seg_row, seg_prev = load_block(i, proj_ref, bias_ref, segc_ref, segr_ref)
        same, cum, enter, tail, fade, falls, rises = block_decay(gate, write, seg_col, seg_row, seg_prev)
        last = jnp.where(seg_col == seg_col[BLOCK - 1 :], 1.0, 0.0)
        score, prob, pairs, mix = (small_ref[here, n * SLOTS : (n + 1) * SLOTS] for n in range(4))
        states_in = states_ref[i]
        keys_in, values_in = states_in[:SLOTS], states_in[SLOTS:]
        out, don = out_ref[here, :], don_ref[here, :]
        unit = lax.rsqrt(jnp.mean(out * out, axis=1, keepdims=True) + NORM_EPS)
        normed = out * unit
        dout = unit * (don - normed * jnp.mean(don * normed, axis=1, keepdims=True))
        dmix = fine(dout, v, NT) * same
        dprob = over_sources(dmix, cum, write, falls, rises) + enter * fine(dout, values_in, NT)
        inner = prob * dprob
        dscore = inner - prob * jnp.sum(inner, axis=1, keepdims=True)
        slope = scale * dscore
        dpairs = over_slots(slope, cum, write, falls, rises) * same
        dcross = slope * enter
        dstate = state[...]
        dkeys, dvalues = dstate[:SLOTS], dstate[SLOTS:]
        send = tail * write
        dfeats = jnp.concatenate(
            [
                nn(dpairs, k) + nn(dcross, keys_in),
                tn(dpairs, q) + nn(send, dkeys),
                tn(mix, dout) + nn(send, dvalues),
            ],
            axis=1,
        )
        grad_ref[here, :QKV] = (dfeats * (sig * (1.0 + pre * (1.0 - sig)))).astype(jnp.bfloat16)
        heard = over_targets([(pairs, slope), (dmix, prob)], cum, falls, rises)
        heard = heard + tail * (nt(k, dkeys) + nt(v, dvalues))
        product = dstate * state_next[...]
        held = lax.dot_general(jnp.ones((8, HEAD_DIM), jnp.float32), product[:SLOTS] + product[SLOTS:],
                               (((1,), (1,)), ((), ())), precision=lax.Precision.HIGHEST, preferred_element_type=jnp.float32)[:1]
        flow = exact(same.T, dscore * score + inner - write * heard)
        dgate = flow - (1.0 - write) * heard + last * held
        dlogits = (dgate * jax.nn.sigmoid(-logits) / GATE_SOFTENING).astype(jnp.bfloat16)
        grad_ref[here, QKV:] = jnp.concatenate([dlogits, jnp.zeros_like(dlogits)], axis=1)
        bias_grad_ref[...] += jnp.sum(dlogits.astype(jnp.float32), axis=0, keepdims=True)
        keep = fade.reshape(SLOTS, 1)
        state[:SLOTS] = keep * dkeys + tn(dcross, q)
        state[SLOTS:] = keep * dvalues + fine(prob * enter, dout, TN)
        state_next[...] = states_in
        return 0

    lax.fori_loop(0, blocks, step, 0)


VMEM = pl.BlockSpec(memory_space=pltpu.VMEM)


def slot_call(kernel, outs, out_specs, scratch, args, cost):
    return pl.pallas_call(
        kernel,
        out_shape=outs,
        in_specs=[VMEM] * len(args),
        out_specs=out_specs,
        scratch_shapes=scratch,
        cost_estimate=pl.CostEstimate(flops=cost, bytes_accessed=0, transcendentals=0),
        compiler_params=pltpu.CompilerParams(vmem_limit_bytes=58 * 2**20),
    )(*args)


def forward_mix(proj, bias, seg):
    length = proj.shape[0]
    blocks = length // BLOCK
    shapes = [(length, HEAD_DIM), (length, 4 * SLOTS), (blocks, 2 * SLOTS, HEAD_DIM)]
    outs = [jax.ShapeDtypeStruct((length, HEAD_DIM), jnp.bfloat16)] + [jax.ShapeDtypeStruct(n, jnp.float32) for n in shapes]
    specs = [VMEM] + [pl.BlockSpec(memory_space=pltpu.HBM)] * 3
    scratch = [pltpu.VMEM(n, jnp.float32) for n in shapes]
    scratch += [pltpu.VMEM((2 * SLOTS, HEAD_DIM), jnp.float32), pltpu.SemaphoreType.DMA((3, blocks))]
    args = (proj, bias.reshape(1, SLOTS), seg.reshape(length, 1), seg.reshape(blocks, 1, BLOCK))
    return slot_call(forward_kernel, outs, specs, scratch, args, 12 * 10**9)


def backward_mix(proj, bias, seg, saved, don):
    length = proj.shape[0]
    blocks = length // BLOCK
    outs = [jax.ShapeDtypeStruct(proj.shape, jnp.bfloat16), jax.ShapeDtypeStruct((1, SLOTS), jnp.float32)]
    scratch = [pltpu.VMEM((2 * SLOTS, HEAD_DIM), jnp.float32)] * 2
    args = (proj, bias.reshape(1, SLOTS), seg.reshape(length, 1), seg.reshape(blocks, 1, BLOCK), *saved, don)
    return slot_call(backward_kernel, outs, [VMEM] * 2, scratch, args, 16 * 10**9)


HEADS = 4
FF = 5632


def dot(a, b, dims, kind=jnp.float32):
    out = lax.dot_general(a, b, (dims, ((), ())), preferred_element_type=jnp.float32)
    return out.astype(kind)


def rms_scale(values):
    return lax.rsqrt(jnp.mean(values * values, axis=-1, keepdims=True) + NORM_EPS)


def plus(a, b):
    return (a.astype(jnp.float32) + b.astype(jnp.float32)).astype(a.dtype)


def behind(value, *others):
    return lax.optimization_barrier((value, others))[0]


def tn_pair_kernel(a_ref, b_ref, c_ref, d_ref, out_ref):
    width = b_ref.shape[1]
    out_ref[:, :width] = dot(a_ref[...], b_ref[...], TN, jnp.bfloat16)
    out_ref[:, width:] = dot(c_ref[...], d_ref[...], TN, jnp.bfloat16)


def tn_kernel(a_ref, b_ref, out_ref):
    out_ref[...] = dot(a_ref[...], b_ref[...], TN, jnp.bfloat16)


def tn_extra_kernel(a_ref, b_ref, e_ref, f_ref, out_ref):
    out, last = dot(a_ref[...], b_ref[...], TN), b_ref.shape[1] - 128
    out_ref[:, :last] = out[:, :last].astype(jnp.bfloat16)
    out_ref[:, last:] = (out[:, last:] + e_ref[...] * f_ref[...]).astype(jnp.bfloat16)


def weight_grads(kernel, block, *operands):
    length, rows = operands[0].shape
    cols = sum(v.shape[1] for v in operands[1:4:2]) if kernel is tn_pair_kernel else operands[1].shape[1]
    whole = lambda v: pl.BlockSpec(v.shape, lambda i: (0, 0))
    strip = pl.BlockSpec((length, block), lambda i: (0, i))
    specs = [strip, whole(operands[1])]
    if kernel is tn_pair_kernel:
        specs += [strip, whole(operands[3])]
    elif kernel is tn_extra_kernel:
        specs += [pl.BlockSpec((block, 1), lambda i: (i, 0)), whole(operands[3])]
    return pl.pallas_call(
        kernel,
        grid=(rows // block,),
        in_specs=specs,
        out_specs=pl.BlockSpec((block, cols), lambda i: (i, 0)),
        out_shape=jax.ShapeDtypeStruct((rows, cols), jnp.bfloat16),
        cost_estimate=pl.CostEstimate(flops=2 * length * rows * cols, bytes_accessed=2 * rows * cols, transcendentals=0),
        compiler_params=pltpu.CompilerParams(vmem_limit_bytes=48 * 2**20),
    )(*operands)


def hidden_kernel(width, x_ref, y_ref, w_ref, hid_ref, grad_ref, acc):
    step = pl.program_id(0)

    @pl.when(step == 0)
    def _():
        acc[...] = jnp.zeros_like(acc)

    acc[:, : 2 * width] += dot(x_ref[...], w_ref[:, : 2 * width], NN)
    acc[:, 2 * width :] += dot(y_ref[...], w_ref[:, 2 * width : 3 * width], NN)

    @pl.when(step == pl.num_programs(0) - 1)
    def _():
        gate, up, back = acc[:, :width], acc[:, width : 2 * width], acc[:, 2 * width :]
        sig = jax.nn.sigmoid(gate)
        act = gate * sig
        hid_ref[...] = (act * up).astype(jnp.bfloat16)
        grad_ref[:, :width] = (back * up * (sig * (1.0 + gate * (1.0 - sig)))).astype(jnp.bfloat16)
        grad_ref[:, width:] = (back * act).astype(jnp.bfloat16)


def hidden_and_grads(x, y, weights, width, cols, block):
    length, depth = x.shape
    strip = pl.BlockSpec((length, block), lambda i: (0, i))
    return pl.pallas_call(
        functools.partial(hidden_kernel, width),
        grid=(depth // block,),
        in_specs=[strip, strip, pl.BlockSpec((block, cols), lambda i: (i, 0))],
        out_specs=[pl.BlockSpec((length, n * width), lambda i: (0, 0)) for n in (1, 2)],
        out_shape=[jax.ShapeDtypeStruct((length, n * width), jnp.bfloat16) for n in (1, 2)],
        scratch_shapes=[pltpu.VMEM((length, 3 * width), jnp.float32)],
        cost_estimate=pl.CostEstimate(flops=6 * length * depth * width, bytes_accessed=6 * depth * width, transcendentals=0),
        compiler_params=pltpu.CompilerParams(vmem_limit_bytes=56 * 2**20),
    )(x, y, weights)


def place_kernel(axis, choices, place_ref, *refs):
    pieces, out_ref = refs[:-1], refs[-1]
    size = pieces[0].shape[axis]

    def put(k, piece):
        start = pl.multiple_of((place_ref[0] ^ k) * size, size)
        where = (pl.ds(start, size), slice(None)) if axis == 0 else (slice(None), pl.ds(start, size))
        out_ref[where] = piece[...]

    for k, choice in enumerate(choices):
        if len(choice) == 1:
            put(k, pieces[choice[0]])
        else:
            pl.when(place_ref[1] == 1)(functools.partial(put, k, pieces[choice[0]]))
            pl.when(place_ref[1] == 0)(functools.partial(put, k, pieces[choice[1]]))


def place_pieces(pieces, choices, first, end, axis=0):
    shape = list(pieces[0].shape)
    shape[axis] *= len(choices)
    vmem = pl.BlockSpec(memory_space=pltpu.VMEM)
    nbytes = 4 * shape[0] * shape[1]
    return pl.pallas_call(
        functools.partial(place_kernel, axis, choices),
        out_shape=jax.ShapeDtypeStruct(shape, pieces[0].dtype),
        in_specs=[pl.BlockSpec(memory_space=pltpu.SMEM)] + [vmem] * len(pieces),
        out_specs=vmem,
        cost_estimate=pl.CostEstimate(flops=0, bytes_accessed=nbytes, transcendentals=0),
        compiler_params=pltpu.CompilerParams(vmem_limit_bytes=48 * 2**20),
    )(jnp.stack([first, end]).astype(jnp.int32), *pieces)


def tokens_kernel(choices, place_ref, gain_ref, *refs):
    pieces, (x_ref, normed_ref) = refs[:-2], refs[-2:]
    size = pieces[0].shape[0]

    def put(k, piece):
        here = pl.ds(pl.multiple_of((place_ref[0] ^ k) * size, size), size)
        x_ref[here, :] = piece[...]
        values = piece[...].astype(jnp.float32)
        normed_ref[here, :] = (values * rms_scale(values) * gain_ref[...]).astype(jnp.bfloat16)

    for k, choice in enumerate(choices):
        if len(choice) == 1:
            put(k, pieces[choice[0]])
        else:
            pl.when(place_ref[1] == 1)(functools.partial(put, k, pieces[choice[0]]))
            pl.when(place_ref[1] == 0)(functools.partial(put, k, pieces[choice[1]]))


def place_tokens(pieces, choices, first, end, gain):
    size, width = pieces[0].shape
    shape = jax.ShapeDtypeStruct((len(choices) * size, width), jnp.bfloat16)
    return pl.pallas_call(
        functools.partial(tokens_kernel, choices),
        out_shape=[shape] * 2,
        in_specs=[pl.BlockSpec(memory_space=pltpu.SMEM)] + [VMEM] * (len(pieces) + 1),
        out_specs=[VMEM] * 2,
        cost_estimate=pl.CostEstimate(flops=0, bytes_accessed=10 * len(choices) * size * width, transcendentals=0),
        compiler_params=pltpu.CompilerParams(vmem_limit_bytes=48 * 2**20),
    )(jnp.stack([first, end]).astype(jnp.int32), gain, *pieces)


class Layout:
    def __init__(self, phases):
        self.seqs, self.span, self.phases = lax.axis_size("seqs"), lax.axis_size("span"), phases
        self.ranks = self.span // phases
        self.half = self.ranks // phases
        place = lax.axis_index("span")
        self.rank, self.phase = place // phases, place % phases
        self.slot = (self.rank % self.half) * phases + self.phase
        self.groups = [
            [s * self.span + z * phases + c for s in range(self.seqs) for c in range(phases)]
            for z in range(self.ranks)
        ]

    def across(self, value, k):
        step = k * self.phases
        return lax.ppermute(value, "span", [(i, i ^ step) for i in range(self.span)])

    def outward(self, k):
        pairs = []
        for i in range(self.span):
            z, c = divmod(i, self.phases)
            slot = (z % self.half) * self.phases + c
            pairs.append((i, (slot ^ k) * self.phases + z // self.half))
        return pairs

    def swap(self, value):
        mine = lax.dynamic_index_in_dim(value, self.phase, 0, False)
        other = lax.dynamic_index_in_dim(value, 1 - self.phase, 0, False)
        got = lax.ppermute(other, "span", [(i, i ^ 1) for i in range(self.span)])
        first = self.phase == 0
        return jnp.stack([jnp.where(first, mine, got), jnp.where(first, got, mine)])

    def between(self, value, pairs):
        p = self.phases
        return lax.ppermute(value, "span", [(a * p + c, b * p + c) for a, b in pairs for c in range(p)])

    def spread_near(self, value, step=1):
        if self.ranks != 4:
            return [self.across(value, k) for k in range(step, self.ranks, step)]
        return [self.across(value, 1), self.between(value, [(1, 2), (2, 1)]), self.between(value, [(0, 3), (3, 0)])]

    def spread_far(self, got):
        if self.ranks != 4:
            return got
        near, middle, ends = got
        near, middle = behind((near, middle))
        inner = self.between(near, [(1, 2), (2, 1)])
        return [near, middle, ends, inner, self.between(middle, [(1, 0), (2, 3)])]

    def choices(self, got):
        if self.ranks == 4:
            near, middle, ends, inner, outer = got
            return [near, outer, inner, ends, middle], ((0,), (1,), (2, 3), (4, 5))
        return got, tuple((k,) for k in range(len(got) + 1))

    def joined(self, own, got, axis=0, step=1):
        pieces, choices = self.choices(got)
        end = (self.rank == 0) | (self.rank == self.ranks - 1)
        return place_pieces([own, *pieces], choices, self.rank // step, end, axis)

    def dealt(self, pieces):
        return place_pieces(pieces, tuple((k,) for k in range(len(pieces))), self.rank, self.rank)

    def in_order(self, pieces, first, axis=0):
        size = pieces[0].shape[axis]
        shape = list(pieces[0].shape)
        shape[axis] = len(pieces) * size
        out = jnp.zeros(shape, pieces[0].dtype)
        for k, piece in enumerate(pieces):
            out = lax.dynamic_update_slice_in_dim(out, piece, (first ^ k) * size, axis)
        return out

    def spread(self, value):
        return behind(self.spread_far(self.spread_near(value)))

    def gather(self, value):
        return self.joined(value, self.spread(value))

    def piece(self, value, k):
        size = value.shape[0] // self.ranks
        return lax.dynamic_slice_in_dim(value, (self.rank ^ k) * size, size, 0)

    def split(self, value):
        return [self.piece(value, k) for k in range(self.ranks)]

    def sum_far(self, pieces):
        if self.ranks != 4:
            return [self.across(pieces[k], k) for k in range(1, self.ranks)]
        inner, outer = (self.between(pieces[2], pairs) for pairs in ([(1, 2), (2, 1)], [(0, 1), (3, 2)]))
        return [inner, outer, self.between(pieces[3], [(0, 3), (3, 0)])]

    def sum_near(self, pieces, got):
        if self.ranks != 4:
            return got
        inner, outer, ends = got
        inner, outer = behind((inner, outer))
        near = self.across(plus(pieces[1], inner), 1)
        return [near, self.between(plus(pieces[3], outer), [(1, 2), (2, 1)]), ends]

    def total(self, pieces, got):
        out = pieces[0].astype(jnp.float32)
        for piece in got:
            out = out + piece.astype(jnp.float32)
        return out

    def deal(self, blocks):
        return [lax.ppermute(block, "span", self.outward(k)) for k, block in enumerate(blocks)]

    def home(self, rows_of, places):
        blocks = rows_of.reshape(self.ranks, -1, rows_of.shape[1])
        pieces = []
        for k in places:
            block = lax.dynamic_index_in_dim(blocks, self.rank ^ k, 0, False)
            pieces.append(lax.ppermute(block, "span", [(b, a) for a, b in self.outward(k)]))
        return pieces

    def fetch(self, value):
        return lax.all_gather(value, ("seqs", "span"), axis=0, tiled=True, axis_index_groups=self.groups)

    def share(self, value):
        return lax.psum_scatter(
            value, ("seqs", "span"), scatter_dimension=0, tiled=True, axis_index_groups=self.groups
        )


def segment_ids(lengths_row, count):
    offsets = jnp.cumsum(lengths_row) - lengths_row
    positions = jnp.arange(count, dtype=jnp.int32)
    return jnp.sum((positions[:, None] >= offsets[None, 1:]).astype(jnp.int32), axis=1)


def local(tokens, attn_weight, mlp_weight, norm1_gain, norm2_gain, gate_bias, lengths, cotangent):
    phases, block_len, width = tokens.shape[1:]
    at = Layout(phases)
    rows = attn_weight.shape[0]
    ranks, copies = at.ranks, at.ranks // HEADS
    proj_cols = 3 * width + HEADS * SLOTS
    share_ff = FF // ranks
    qkv = 3 * HEAD_DIM
    gate_end = qkv + SLOTS
    bias_len = gate_bias.shape[0]
    head = at.rank // copies

    def columns(weight, *cuts):
        return [lax.dynamic_slice_in_dim(weight, start, size, 1) for start, size in cuts]

    extra = jnp.zeros((rows, SLOTS), jnp.bfloat16)
    extra = extra.at[0, :bias_len].set(gate_bias).at[1, :rows].set(norm1_gain).at[2, :rows].set(norm2_gain)
    in_blocks, late_blocks = [], []
    for j in range(ranks):
        to = at.slot ^ j
        cuts = [(n * width + to // copies * HEAD_DIM, HEAD_DIM) for n in range(3)]
        cuts.append((3 * width + to // copies * SLOTS, SLOTS))
        in_blocks.append(jnp.concatenate(columns(attn_weight, *cuts) + [extra], axis=1))
    for j in range(ranks):
        cuts = [(n * FF + (at.slot ^ j) * share_ff, share_ff) for n in range(3)]
        late_blocks.append(jnp.concatenate(columns(mlp_weight, *cuts), axis=1))
    in_pieces = at.deal(in_blocks)
    out_own = attn_weight[:, proj_cols:]
    out_near = at.spread_near(behind(out_own, in_blocks))

    rest = at.swap(tokens[0]).reshape(-1, width)
    dy = at.swap(cotangent[0]).reshape(-1, width)
    shard = rest.shape[0]
    in_pieces, out_near = behind((in_pieces, out_near, rest, dy, late_blocks))[:2]
    w_in = at.fetch(at.dealt(in_pieces))
    x_near = at.spread_near(behind(rest, in_pieces))
    out_got = behind(at.spread_far(out_near), x_near)
    both_got = behind(at.spread_far(x_near))
    out_rows = at.swap(at.joined(out_own, out_got).reshape(phases, at.half * rows, width))
    out_rows = out_rows.reshape(phases, at.half, rows, width).swapaxes(0, 1).reshape(-1, width)
    w_out = at.fetch(out_rows)
    late_pieces = at.deal(behind(late_blocks, both_got))

    extras = w_in.reshape(-1, rows, w_in.shape[1])[:, :3, gate_end:]
    bias = lax.dynamic_slice_in_dim(extras[:, 0, :bias_len].reshape(-1), head * SLOTS, SLOTS, 0).astype(jnp.float32)
    gain_one = extras[:, 1, :rows].reshape(1, -1).astype(jnp.float32)
    gain_two = extras[:, 2, :rows].reshape(1, -1).astype(jnp.float32)
    lengths_row = lax.dynamic_index_in_dim(lengths[0], at.phase, 0, False)
    seg = segment_ids(lengths_row, ranks * shard)
    both_got, bias, gain_one, gain_two, seg = behind((both_got, bias, gain_one, gain_two, seg))

    got, choices = at.choices(both_got)
    end = (at.rank == 0) | (at.rank == ranks - 1)
    x_all, in_one = place_tokens([rest, *got], choices, at.rank, end, gain_one)
    projected = dot(in_one, w_in, NN)
    projected = behind(projected, late_pieces[0], late_pieces[1])
    low, *saved = forward_mix(projected, bias, seg)
    low_near = at.spread_near(low, copies)
    w_mlp = at.fetch(at.dealt(behind(late_pieces, low)))
    w_gate_up, w_down = w_mlp[:, : 2 * share_ff], w_mlp[:, 2 * share_ff :]
    low_got = behind(at.spread_far(low_near))
    low_all = at.joined(low, low_got, 1, copies)

    dy_near = at.spread_near(behind(dy, low_got))
    dy_far = at.spread_far(dy_near)
    after_all = x_all.astype(jnp.float32) + dot(low_all, w_out, NT)
    in_two = (after_all * rms_scale(after_all) * gain_two).astype(jnp.bfloat16)
    after = at.piece(after_all, 0)
    scale_two = rms_scale(after)
    normed_two = after * scale_two

    dyl = at.joined(dy, behind(dy_far, after_all))
    hidden, grad_gate_up = hidden_and_grads(in_two, dyl, w_mlp, share_ff, w_mlp.shape[1], 512)
    two_part = dot(grad_gate_up, w_gate_up, NT, jnp.bfloat16)
    two_pieces = at.split(two_part)
    two_far = at.sum_far(two_pieces)
    hidden_later, grad_later = behind((hidden, grad_gate_up), two_pieces)
    grad_mlp_w = weight_grads(tn_pair_kernel, 256, in_two, grad_later, dyl, hidden_later)
    share_mlp = at.share(grad_mlp_w)
    two_far = behind(two_far, grad_mlp_w)
    mlp_part = dot(behind(hidden, grad_mlp_w), w_down, NT, jnp.bfloat16)
    two_near = behind(at.sum_near(two_pieces, two_far), mlp_part)
    back_two = at.total(two_pieces, two_near)
    scaled_two = back_two * gain_two

    grad_after = dy.astype(jnp.float32) + scale_two * (
        scaled_two - normed_two * jnp.mean(scaled_two * normed_two, axis=1, keepdims=True)
    )
    dal = grad_after.astype(jnp.bfloat16)
    don_all = dot(dal, w_out, NN, jnp.bfloat16)
    don_blocks = [
        lax.dynamic_slice_in_dim(don_all, (at.rank ^ j) // copies * HEAD_DIM, HEAD_DIM, 1) for j in range(ranks)
    ]
    don_got = behind([at.across(don_blocks[j], j) for j in range(1, ranks)])
    each = tuple((j,) for j in range(ranks))
    don = place_pieces([don_blocks[0], *don_got], each, at.rank, at.rank)
    dal_parts = dal.reshape(shard, at.seqs, ranks, -1)
    dal_blocks = [lax.dynamic_index_in_dim(dal_parts, at.rank ^ j, 2, False).reshape(shard, -1) for j in range(ranks)]
    dal_blocks = behind(dal_blocks, don_got)
    dal_got = [at.across(dal_blocks[j], j) for j in range(1, ranks)]
    mlp_pieces = at.split(behind(mlp_part, don_got))
    mlp_far = at.sum_far(mlp_pieces)

    grad_proj, bias_grad = backward_mix(projected, bias, seg, saved, don)

    bias_grad = jnp.concatenate([jnp.zeros_like(bias_grad), bias_grad], axis=1)
    row_ids = jnp.arange(width, dtype=jnp.int32)
    owners = SLOTS // bias_len
    holds = ((row_ids % rows == 0) & (row_ids // (rows * owners) == head)).astype(jnp.float32)
    mlp_near = at.sum_near(mlp_pieces, behind(mlp_far, grad_proj))
    mlp_far, dal_got, grad_proj = behind((mlp_far, dal_got, grad_proj))
    mlp_near = at.sum_near(mlp_pieces, mlp_far)
    grad_in_w = weight_grads(tn_extra_kernel, 512, in_one, grad_proj, holds[:, None], bias_grad)
    share_in = at.share(behind(grad_in_w, share_mlp))
    one_part = dot(behind(grad_proj, grad_in_w), w_in, NT, jnp.bfloat16)
    one_pieces = behind(at.split(one_part), mlp_near)
    one_far = at.sum_far(one_pieces)
    quarter = ranks // 4
    home_first = at.home(behind(share_mlp, one_pieces), range(2 * quarter))
    dal_rows = place_pieces([dal_blocks[0], *dal_got], each, at.rank, at.rank)
    dal_rows = behind(dal_rows, one_pieces)
    grad_out_w = weight_grads(tn_kernel, min(512, dal_rows.shape[1]), dal_rows, low_all)
    share_out = at.share(grad_out_w)
    mlp_out = at.total(mlp_pieces, mlp_near)
    mixed_rows = (after + mlp_out).astype(jnp.bfloat16)
    mixed = at.swap(mixed_rows.reshape(phases, block_len, width))[None]
    one_far, home_first, mixed = behind((one_far, home_first, mixed), grad_out_w)
    one_near = at.sum_near(one_pieces, one_far)
    home_second = at.home(behind(share_mlp, home_first), range(2 * quarter, ranks))
    in_home = at.home(behind(share_in, home_first), range(0, ranks, copies))
    back_one = at.total(one_pieces, behind(one_near, home_second[0])) / copies
    scaled_one = back_one * gain_one
    rest_float = rest.astype(jnp.float32)
    scale_one = rms_scale(rest_float)
    normed_one = rest_float * scale_one
    grad_rows = grad_after + scale_one * (
        scaled_one - normed_one * jnp.mean(scaled_one * normed_one, axis=1, keepdims=True)
    )
    grad_tokens = at.swap(grad_rows.reshape(phases, block_len, width))[None]

    mlp_home = home_first + home_second
    gate_up_weight = mlp_weight[:, : 2 * FF].astype(jnp.float32)
    down = at.in_order([p[:, 2 * share_ff :] for p in mlp_home], at.slot, 1).astype(jnp.float32)
    gates = at.in_order([p[:, :share_ff] for p in mlp_home], at.slot, 1).astype(jnp.float32)
    ups = at.in_order([p[:, share_ff : 2 * share_ff] for p in mlp_home], at.slot, 1).astype(jnp.float32)
    grad_mlp = jnp.concatenate([gates, ups, down], axis=1)
    gain_grad_two = jnp.sum(grad_mlp[:, : 2 * FF] * gate_up_weight, axis=1) / norm2_gain.astype(jnp.float32)

    slot_head = at.slot // copies
    parts = [
        at.in_order([p[:, j * HEAD_DIM : (j + 1) * HEAD_DIM] for p in in_home], slot_head, 1) for j in range(3)
    ]
    for j in range(HEADS):
        parts.append(sum(jnp.where(slot_head ^ n == j, p[:, qkv:gate_end], 0) for n, p in enumerate(in_home)))
    parts.append(share_out)
    grad_attn = jnp.concatenate(parts, axis=1).astype(jnp.float32)
    attn_float = attn_weight[:, :proj_cols].astype(jnp.float32)
    gain_grad_one = jnp.sum(grad_attn[:, :proj_cols] * attn_float, axis=1) / norm1_gain.astype(jnp.float32)
    bias_sums = sum(p[0, gate_end : gate_end + SLOTS].astype(jnp.float32) for p in in_home)
    owner = lax.axis_index("seqs") * at.span + lax.axis_index("span")
    bias_home = lax.dynamic_slice_in_dim(bias_sums, owner % owners * bias_len, bias_len, 0)
    return (mixed, grad_tokens, grad_attn, grad_mlp, gain_grad_one, gain_grad_two, bias_home)


def solution(mesh):
    placed = (
        P("seqs", None, "span", None),
        P(("seqs", "span"), None),
        P(("seqs", "span"), None),
        P(("seqs", "span")),
        P(("seqs", "span")),
        P(("seqs", "span")),
        P("seqs", None, None),
        P("seqs", None, "span", None),
    )
    return jax.shard_map(
        local,
        mesh=mesh,
        in_specs=placed,
        out_specs=(
            P("seqs", None, "span", None),
            P("seqs", None, "span", None),
            P(("seqs", "span"), None),
            P(("seqs", "span"), None),
            P(("seqs", "span")),
            P(("seqs", "span")),
            P(("seqs", "span")),
        ),
        check_vma=False,
    )
```

time: 636 us -> 596 us (0.937)
  waiting for transfers between devices: 265 us -> 199 us
  Pallas kernels: 72.4 us -> 91.4 us
  starting transfers between devices: 121 us -> 132 us
    ppermute x8, waiting for transfers between devices: 65.7 us -> 32.6 us  [deal(): lax.ppermute(block, 'span', self.outward(k))]
    ppermute x7 -> x13, waiting for transfers between devices: 43.3 us -> 23.8 us  [across(): lax.ppermute(value, 'span', [(i, i ^ step) for i in range(self.span)])]
    pallas_call x4 -> x13, Pallas kernels: 55.6 us -> 74.6 us  [the longest x2 39.7 us: slot_call(): pl.pallas_call(kernel, out_shape=outs, in_specs=[VMEM] * len(args), out_s...]
    dynamic_update_slice x32 -> x12, local copies, waits for them, and re-layouts: 18.1 us -> 0.36 us  [in_order(): out = lax.dynamic_update_slice_in_dim(out, piece, (first ^ k) * size, axis)]
    ppermute x8, waiting for transfers between devices: 60.7 us -> 43.5 us  [home(): lax.ppermute(block, 'span', [(b, a) for a, b in self.outward(k)])]
    ppermute x4 -> x5, starting transfers between devices: 23.5 us -> 8.02 us  [swap(): got = lax.ppermute(other, 'span', [(i, i ^ 1) for i in range(self.span)])]
    ppermute x28, starting transfers between devices: 44.1 us -> 59.2 us  [between(): lax.ppermute(value, 'span', [(a * p + c, b * p + c) for a, b in pairs for...]
    dynamic_update_slice x9 -> x0, other arithmetic: 11.6 us -> none  [in_order(): out = lax.dynamic_update_slice_in_dim(out, piece, (first ^ k) * size, axis)]
  transfers between devices with their start and end apart: 59 -> 68, of which waited for: 27 -> 26; matrix products, arithmetic and copies ran while one was open for 15% -> 16% of each run, Pallas kernels for 7% -> 10%
where the time goes in v2:
time: 596 us; the launch traced here: 587 us
  waiting for transfers between devices  199 us (33%)
  starting transfers between devices  132 us (22%)
  Pallas kernels  91.4 us (15%)
  local copies, waits for them, and re-layouts  65 us (11%)
  matrix products  45.4 us (8%)
  other arithmetic  38.1 us (6%)
  between operations  16.3 us (3%)
    ppermute x28, waiting for transfers between devices, between(): lax.ppermute(value, 'span', [(a * p + c, b * p + c) for a, b in pairs for...  89 us
    ppermute x28, starting transfers between devices, between(): lax.ppermute(value, 'span', [(a * p + c, b * p + c) for a, b in pairs for...  59.2 us
    dot_general x6, matrix products, dot(): lax.dot_general(a, b, (dims, ((), ())), preferred_element_type=jnp.float32)  45.4 us
    ppermute x8, waiting for transfers between devices, home(): lax.ppermute(block, 'span', [(b, a) for a, b in self.outward(k)])  43.5 us
    pallas_call x2, Pallas kernels, slot_call(): pl.pallas_call(kernel, out_shape=outs, in_specs=[VMEM] * len(args), out_s...  39.7 us
    ppermute x8, waiting for transfers between devices, deal(): lax.ppermute(block, 'span', self.outward(k))  32.6 us
    unnamed x130, local copies, waits for them, and re-layouts  30.3 us
    ppermute x8, starting transfers between devices, home(): lax.ppermute(block, 'span', [(b, a) for a, b in self.outward(k)])  27.5 us
  transfers between devices with their start and end apart: 68, of which 26 were waited for; matrix products, arithmetic and copies ran while one was open for 16% of the time, Pallas kernels for 10%

profile of v2, /device:TPU:5, one launch (start us, length us, event | category | flops | bytes accessed | tf_op | source)
XLA Modules:
  0.0 587.0 jit_solution(9645582830289108631)
XLA Ops:
  36.8 6.5 %collective-permute-done.3.refs_2_ = bf16[64,1664]{1,0:T(8,128)(2,1)S(1)} collective-permute-done((bf16[64,1664]{1,0:T(8,128)(2,1)}, bf16[64,1664]{1,0:T(8,128)(2,1)S(1)}, u32[]{:S(2)}, u32[]{:S(2)}) %collective-permute-start.3) | collective-permute-done | bytes 213024 | tf_op jit(solution)/shard_map/ppermute | solution.py:578
  62.2 20.4 %collective-permute-done.22.refs_2_ = bf16[64,2048]{1,0:T(8,128)(2,1)} collective-permute-done((bf16[64,2048]{1,0:T(8,128)(2,1)S(1)}, bf16[64,2048]{1,0:T(8,128)(2,1)}, u32[]{:S(2)}, u32[]{:S(2)}) %collective-permute-start.22) | collective-permute-done | bytes 262176 | tf_op jit(solution)/shard_map/ppermute | solution.py:506
  94.0 12.8 %collective-permute-done.13.refs_2_ = bf16[128,2048]{1,0:T(8,128)(2,1)} collective-permute-done((bf16[128,2048]{1,0:T(8,128)(2,1)S(1)}, bf16[128,2048]{1,0:T(8,128)(2,1)}, u32[]{:S(2)}, u32[]{:S(2)}) %collective-permute-start.13) | collective-permute-done | bytes 524320 | tf_op jit(solution)/shard_map/ppermute | solution.py:506
  127.7 10.0 %fusion.37.proj_ref = f32[512,1664]{1,0:T(8,128)} fusion(bf16[512,2048]{1,0:T(8,128)(2,1)} %get-tuple-element.178.a_ref, bf16[2048,1664]{1,0:T(8,128)(2,1)} %all-gather.4.cloned.1.call-done), kind=kOutput, calls=%fused_computation.195 | convolution fusion | flops 3489660928 | bytes 12320768 | tf_op jit(solution)/shard_map/dot_general | solution.py:321
  137.7 19.6 %collective-permute-done.15.refs_1_ = bf16[64,4224]{1,0:T(8,128)(2,1)S(1)} collective-permute-done((bf16[64,4224]{1,0:T(8,128)(2,1)}, bf16[64,4224]{1,0:T(8,128)(2,1)S(1)}, u32[]{:S(2)}, u32[]{:S(2)}) %collective-permute-start.15) | collective-permute-done | bytes 540704 | tf_op jit(solution)/shard_map/ppermute | solution.py:578
  158.9 14.6 %shard_map.137 = (bf16[512,512]{1,0:T(8,128)(2,1)}, f32[512,512]{1,0:T(8,128)}, f32[512,256]{1,0:T(8,128)}, f32[8,128,512]{2,1,0:T(8,128)}) custom-call(f32[512,1664]{1,0:T(8,128)} %fusion.37.proj_ref, f32[1,64]{1,0:T(1,128)} %bitcast.181, s32[512,1]{1,0:T(8,128)} %copy.38.segc_ref, s32[8,1,64]{2,1,0:T(1,128)} %reshape.351.segr_ref), custom_call_target="tpu_custom_call" | custom-call | flops 12000000000 | tf_op jit(solution)/shard_map/pallas_call | solution.py:284
  181.0 12.9 %collective-permute-done.16.refs_1_ = bf16[512,512]{1,0:T(8,128)(2,1)S(1)} collective-permute-done((bf16[512,512]{1,0:T(8,128)(2,1)S(1)}, bf16[512,512]{1,0:T(8,128)(2,1)S(1)}, u32[]{:S(2)}, u32[]{:S(2)}) %collective-permute-start.16) | collective-permute-done | bytes 524320 | tf_op jit(solution)/shard_map/ppermute | solution.py:487
  202.5 16.9 %collective-permute-done.20.refs_2_ = bf16[512,512]{1,0:T(8,128)(2,1)S(1)} collective-permute-done((bf16[512,512]{1,0:T(8,128)(2,1)S(1)}, bf16[512,512]{1,0:T(8,128)(2,1)S(1)}, u32[]{:S(2)}, u32[]{:S(2)}) %collective-permute-start.20) | collective-permute-done | bytes 524320 | tf_op jit(solution)/shard_map/ppermute | solution.py:506
  235.9 8.7 %multiply_reduce_fusion = (f32[512]{0:T(512)S(1)}, f32[512,2048]{1,0:T(8,128)S(1)}) fusion(bf16[512,2048]{1,0:T(8,128)(2,1)S(1)} %shard_map.138.b_ref, bf16[2048,2048]{1,0:T(8,128)(2,1)} %all-gather.6.cloned.1.call-done, bf16[512,2048]{1,0:T(8,128)(2,1)} %copy-done.29), kind=kOutput, calls=%fused_computation.6 | convolution fusion | flops 4299161088 | bytes 16779264 | tf_op jit(solution)/shard_map/dot_general | solution.py:321
  244.7 14.4 %collective-permute-done.28.refs_2_ = bf16[128,2048]{1,0:T(8,128)(2,1)} collective-permute-done((bf16[128,2048]{1,0:T(8,128)(2,1)}, bf16[128,2048]{1,0:T(8,128)(2,1)}, u32[]{:S(2)}, u32[]{:S(2)}) %collective-permute-start.28) | collective-permute-done | bytes 524320 | tf_op jit(solution)/shard_map/ppermute | solution.py:506
  268.5 16.8 %shard_map.142 = (bf16[512,1408]{1,0:T(8,128)(2,1)}, bf16[512,2816]{1,0:T(8,128)(2,1)}) custom-call(bf16[512,2048]{1,0:T(8,128)(2,1)} %multiply_convert_fusion.x_ref.a_ref, bf16[512,2048]{1,0:T(8,128)(2,1)} %copy-done.2, bf16[2048,4224]{1,0:T(8,128)(2,1)} %all-gather.8.cloned.1.call-done.w_ref), custom_call_target="tpu_custom_call" | custom-call | flops 8858370048 | bytes 17301504 | tf_op jit(solution)/shard_map/pallas_call | solution.py:397
  285.3 10.0 %fusion.4 = bf16[512,2048]{1,0:T(8,128)(2,1)S(1)} fusion(bf16[512,2816]{1,0:T(8,128)(2,1)} %get-tuple-element.219.b_ref, bf16[2048,4224]{1,0:T(8,128)(2,1)} %all-gather.8.cloned.1.call-done.w_ref), kind=kOutput, calls=%fused_computation.8 | convolution fusion | flops 5906628608 | bytes 16515072 | tf_op jit(solution)/shard_map/dot_general | solution.py:321
  298.9 14.5 %shard_map.143 = bf16[2048,4224]{1,0:T(8,128)(2,1)} custom-call(bf16[512,2048]{1,0:T(8,128)(2,1)S(1)} %copy-done.1, bf16[512,2816]{1,0:T(8,128)(2,1)} %get-tuple-element.219.b_ref, bf16[512,2048]{1,0:T(8,128)(2,1)S(1)} %copy-done.3, bf16[512,1408]{1,0:T(8,128)(2,1)S(1)} %copy-done.32), custom_call_target="tpu_custom_call" | custom-call | flops 8858370048 | bytes 17301504 | tf_op jit(solution)/shard_map/pallas_call | solution.py:363
  330.8 12.6 %collective-permute-done.33 = bf16[128,2048]{1,0:T(8,128)(2,1)} collective-permute-done((bf16[128,2048]{1,0:T(8,128)(2,1)}, bf16[128,2048]{1,0:T(8,128)(2,1)}, u32[]{:S(2)}, u32[]{:S(2)}) %collective-permute-start.33) | collective-permute-done | bytes 524320 | tf_op jit(solution)/shard_map/ppermute | solution.py:506
  347.1 7.5 %fusion.7 = bf16[512,2048]{1,0:T(8,128)(2,1)} fusion(bf16[512,1408]{1,0:T(8,128)(2,1)S(1)} %copy-done.33, bf16[2048,4224]{1,0:T(8,128)(2,1)} %all-gather.8.cloned.1.call-done.w_ref), kind=kOutput, calls=%fused_computation.10 | convolution fusion | flops 2953838592 | bytes 9306112 | tf_op jit(solution)/shard_map/dot_general | solution.py:321
  393.0 25.1 %shard_map.145 = (bf16[512,1664]{1,0:T(8,128)(2,1)}, f32[1,64]{1,0:T(1,128)}) custom-call(f32[512,1664]{1,0:T(8,128)} %fusion.37.proj_ref, f32[1,64]{1,0:T(1,128)} %bitcast.182, s32[512,1]{1,0:T(8,128)} %copy.38.segc_ref, s32[8,1,64]{2,1,0:T(1,128)} %reshape.351.segr_ref, f32[512,512]{1,0:T(8,128)} %get-tuple-element.237.out_ref, ...), custom_call_target="tpu_custom_call" | custom-call | flops 16000000000 | tf_op jit(solution)/shard_map/pallas_call | solution.py:284
  423.1 6.1 %shard_map.146 = bf16[2048,1664]{1,0:T(8,128)(2,1)} custom-call(bf16[512,2048]{1,0:T(8,128)(2,1)S(1)} %copy-done.28, bf16[512,1664]{1,0:T(8,128)(2,1)S(1)} %copy-done.30, f32[2048,1]{1,0:T(8,128)S(1)} %copy-done.4, f32[1,128]{1,0:T(1,128)S(1)} %concatenate.51.f_ref), custom_call_target="tpu_custom_call" | custom-call | flops 3489660928 | bytes 6815744 | tf_op jit(solution)/shard_map/pallas_call | solution.py:363
  441.1 7.7 %convolution_convert_fusion = bf16[512,2048]{1,0:T(8,128)(2,1)S(1)} fusion(bf16[512,1664]{1,0:T(8,128)(2,1)S(1)} %copy-done.31, bf16[2048,1664]{1,0:T(8,128)(2,1)} %all-gather.4.cloned.1.call-done), kind=kOutput, calls=%fused_computation.9 | convolution fusion | flops 3490709504 | bytes 10616832 | tf_op jit(solution)/shard_map/dot_general | solution.py:321
  481.1 8.5 %collective-permute-done.50 = bf16[64,4224]{1,0:T(8,128)(2,1)S(1)} collective-permute-done((bf16[64,4224]{1,0:T(8,128)(2,1)S(1)}, bf16[64,4224]{1,0:T(8,128)(2,1)S(1)}, u32[]{:S(2)}, u32[]{:S(2)}) %collective-permute-start.50) | collective-permute-done | bytes 540704 | tf_op jit(solution)/shard_map/ppermute | solution.py:585
  495.3 13.9 %collective-permute-start.61 = (bf16[64,4224]{1,0:T(8,128)(2,1)S(1)}, bf16[64,4224]{1,0:T(8,128)(2,1)S(1)}, u32[]{:S(2)}, u32[]{:S(2)}) collective-permute-start(bf16[64,4224]{1,0:T(8,128)(2,1)S(1)} %get-tuple-element.279), channel_id=1, source_target_pairs={{6,0},{4,1},{2,2},{0,3},{7,4},{5,5},{3,6},{1,7},{14,8},{12,9},{10,... | collective-permute-start | bytes 1622024 | tf_op jit(solution)/shard_map/ppermute | solution.py:585
  512.4 5.9 %collective-permute-start.53 = (bf16[128,2048]{1,0:T(8,128)(2,1)S(1)}, bf16[128,2048]{1,0:T(8,128)(2,1)S(1)}, u32[]{:S(2)}, u32[]{:S(2)}) collective-permute-start(bf16[128,2048]{1,0:T(8,128)(2,1)S(1)} %add_convert_fusion.1), channel_id=1, source_target_pairs={{0,2},{1,3},{2,0},{3,1},{4,6},{5,7},{6,4},{7,5},{8,10},{9,11},{10,... | collective-permute-start | bytes 1572872 | tf_op jit(solution)/shard_map/ppermute | solution.py:487
  518.5 18.1 %collective-permute-done.61 = bf16[64,4224]{1,0:T(8,128)(2,1)S(1)} collective-permute-done((bf16[64,4224]{1,0:T(8,128)(2,1)S(1)}, bf16[64,4224]{1,0:T(8,128)(2,1)S(1)}, u32[]{:S(2)}, u32[]{:S(2)}) %collective-permute-start.61) | collective-permute-done | bytes 540704 | tf_op jit(solution)/shard_map/ppermute | solution.py:585
  560.3 8.1 %collective-permute-done.59 = bf16[64,1664]{1,0:T(8,128)(2,1)S(1)} collective-permute-done((bf16[64,1664]{1,0:T(8,128)(2,1)S(1)}, bf16[64,1664]{1,0:T(8,128)(2,1)S(1)}, u32[]{:S(2)}, u32[]{:S(2)}) %collective-permute-start.59) | collective-permute-done | bytes 213024 | tf_op jit(solution)/shard_map/ppermute | solution.py:585
  568.4 5.8 collective-permute-done.60
  (377 shorter events, 273.0 us)
Async XLA Ops:
  7.2 108.8 %all-gather.4.cloned.1.call-start = ((), (), s32[]{:S(2)}) async-start(), calls=%async_computation.3 | async-start | bytes 7667712 | tf_op jit(solution)/shard_map/all_gather | solution.py:589
  15.7 35.9 %collective-permute-start.5 = (bf16[64,2048]{1,0:T(8,128)(2,1)S(1)}, bf16[64,2048]{1,0:T(8,128)(2,1)S(1)}, u32[]{:S(2)}, u32[]{:S(2)}) collective-permute-start(bf16[64,2048]{1,0:T(8,128)(2,1)S(1)} %slice.190.refs_0_), channel_id=1, source_target_pairs={{0,2},{1,3},{2,0},{3,1},{4,6},{5,7},{6,4},{7,5},{8,10},{9,11},{10,... | collective-permute-start | bytes 786440 | tf_op jit(solution)/shard_map/ppermute | solution.py:487
  17.0 34.6 %collective-permute-start.6 = (bf16[64,2048]{1,0:T(8,128)(2,1)S(1)}, bf16[64,2048]{1,0:T(8,128)(2,1)S(1)}, u32[]{:S(2)}, u32[]{:S(2)}) collective-permute-start(bf16[64,2048]{1,0:T(8,128)(2,1)S(1)} %slice.190.refs_0_), channel_id=1, source_target_pairs={{2,4},{3,5},{4,2},{5,3},{10,12},{11,13},{12,10},{13,11},{18,20},{1... | collective-permute-start | bytes 786440 | tf_op jit(solution)/shard_map/ppermute | solution.py:506
  17.7 34.0 %collective-permute-start.7 = (bf16[64,2048]{1,0:T(8,128)(2,1)S(1)}, bf16[64,2048]{1,0:T(8,128)(2,1)S(1)}, u32[]{:S(2)}, u32[]{:S(2)}) collective-permute-start(bf16[64,2048]{1,0:T(8,128)(2,1)S(1)} %slice.190.refs_0_), channel_id=1, source_target_pairs={{0,6},{1,7},{6,0},{7,1},{8,14},{9,15},{14,8},{15,9},{16,22},{17,23... | collective-permute-start | bytes 786440 | tf_op jit(solution)/shard_map/ppermute | solution.py:506
  53.2 182.7 %all-gather.6.cloned.1.call-start = ((), (), s32[]{:S(2)}) async-start(), calls=%async_computation.4 | async-start | bytes 9437184 | tf_op jit(solution)/shard_map/all_gather | solution.py:589
  53.3 29.3 %collective-permute-start.10 = (bf16[128,2048]{1,0:T(8,128)(2,1)S(1)}, bf16[128,2048]{1,0:T(8,128)(2,1)S(1)}, u32[]{:S(2)}, u32[]{:S(2)}) collective-permute-start(bf16[128,2048]{1,0:T(8,128)(2,1)S(1)} %bitcast.140), channel_id=1, source_target_pairs={{2,4},{3,5},{4,2},{5,3},{10,12},{11,13},{12,10},{13,11},{18,20},{1... | collective-permute-start | bytes 1572872 | tf_op jit(solution)/shard_map/ppermute | solution.py:506
  54.0 28.6 %collective-permute-start.9 = (bf16[128,2048]{1,0:T(8,128)(2,1)S(1)}, bf16[128,2048]{1,0:T(8,128)(2,1)S(1)}, u32[]{:S(2)}, u32[]{:S(2)}) collective-permute-start(bf16[128,2048]{1,0:T(8,128)(2,1)S(1)} %bitcast.141), channel_id=1, source_target_pairs={{0,2},{1,3},{2,0},{3,1},{4,6},{5,7},{6,4},{7,5},{8,10},{9,11},{10,... | collective-permute-start | bytes 1572872 | tf_op jit(solution)/shard_map/ppermute | solution.py:487
  55.2 27.4 %collective-permute-start.11 = (bf16[128,2048]{1,0:T(8,128)(2,1)S(1)}, bf16[128,2048]{1,0:T(8,128)(2,1)S(1)}, u32[]{:S(2)}, u32[]{:S(2)}) collective-permute-start(bf16[128,2048]{1,0:T(8,128)(2,1)S(1)} %bitcast.142), channel_id=1, source_target_pairs={{0,6},{1,7},{6,0},{7,1},{8,14},{9,15},{14,8},{15,9},{16,22},{17,23... | collective-permute-start | bytes 1572872 | tf_op jit(solution)/shard_map/ppermute | solution.py:506
  90.8 177.8 %all-gather.8.cloned.1.call-start = ((), (), s32[]{:S(2)}) async-start(), calls=%async_computation.5 | async-start | bytes 19464192 | tf_op jit(solution)/shard_map/all_gather | solution.py:589
  106.9 30.9 %collective-permute-start.14 = (bf16[64,4224]{1,0:T(8,128)(2,1)}, bf16[64,4224]{1,0:T(8,128)(2,1)S(1)}, u32[]{:S(2)}, u32[]{:S(2)}) collective-permute-start(bf16[64,4224]{1,0:T(8,128)(2,1)} %get-tuple-element.179), channel_id=1, source_target_pairs={{0,0},{1,2},{2,4},{3,6},{4,1},{5,3},{6,5},{7,7},{8,8},{9,10},{10,1... | collective-permute-start | bytes 1622024 | tf_op jit(solution)/shard_map/ppermute | solution.py:578
  110.7 46.7 %collective-permute-start.15 = (bf16[64,4224]{1,0:T(8,128)(2,1)}, bf16[64,4224]{1,0:T(8,128)(2,1)S(1)}, u32[]{:S(2)}, u32[]{:S(2)}) collective-permute-start(bf16[64,4224]{1,0:T(8,128)(2,1)} %get-tuple-element.180), channel_id=1, source_target_pairs={{0,2},{1,0},{2,6},{3,4},{4,3},{5,1},{6,7},{7,5},{8,10},{9,8},{10,1... | collective-permute-start | bytes 1622024 | tf_op jit(solution)/shard_map/ppermute | solution.py:578
  110.8 62.8 %collective-permute-start.29 = (bf16[64,4224]{1,0:T(8,128)(2,1)}, bf16[64,4224]{1,0:T(8,128)(2,1)S(1)}, u32[]{:S(2)}, u32[]{:S(2)}) collective-permute-start(bf16[64,4224]{1,0:T(8,128)(2,1)} %get-tuple-element.211), channel_id=1, source_target_pairs={{0,4},{1,6},{2,0},{3,2},{4,5},{5,7},{6,1},{7,3},{8,12},{9,14},{10,... | collective-permute-start | bytes 1622024 | tf_op jit(solution)/shard_map/ppermute | solution.py:578
  112.3 61.2 %collective-permute-start.30 = (bf16[64,4224]{1,0:T(8,128)(2,1)}, bf16[64,4224]{1,0:T(8,128)(2,1)}, u32[]{:S(2)}, u32[]{:S(2)}) collective-permute-start(bf16[64,4224]{1,0:T(8,128)(2,1)} %get-tuple-element.212), channel_id=1, source_target_pairs={{0,6},{1,4},{2,2},{3,0},{4,7},{5,5},{6,3},{7,1},{8,14},{9,12},{10,... | collective-permute-start | bytes 1622024 | tf_op jit(solution)/shard_map/ppermute | solution.py:578
  176.1 256.3 %reduce-scatter.4.cloned.1.call-start = ((), (), s32[]{:S(2)}) async-start(), calls=%async_computation.6 | async-start | bytes 19464192 | tf_op jit(solution)/shard_map/reduce_scatter | solution.py:592
  313.5 236.3 %reduce-scatter.6.cloned.1.call-start = ((), (), s32[]{:S(2)}) async-start(), calls=%async_computation.7 | async-start | bytes 7667712 | tf_op jit(solution)/shard_map/reduce_scatter | solution.py:592
  380.9 37.9 %collective-permute-start.39 = (bf16[128,2048]{1,0:T(8,128)(2,1)}, bf16[128,2048]{1,0:T(8,128)(2,1)S(1)}, u32[]{:S(2)}, u32[]{:S(2)}) collective-permute-start(bf16[128,2048]{1,0:T(8,128)(2,1)} %get-tuple-element.300), channel_id=1, source_target_pairs={{2,4},{3,5},{4,2},{5,3},{10,12},{11,13},{12,10},{13,11},{18,20},{1... | collective-permute-start | bytes 1572872 | tf_op jit(solution)/shard_map/ppermute | solution.py:506
  381.6 37.2 %collective-permute-start.40 = (bf16[128,2048]{1,0:T(8,128)(2,1)}, bf16[128,2048]{1,0:T(8,128)(2,1)S(1)}, u32[]{:S(2)}, u32[]{:S(2)}) collective-permute-start(bf16[128,2048]{1,0:T(8,128)(2,1)} %get-tuple-element.300), channel_id=1, source_target_pairs={{0,2},{1,3},{6,4},{7,5},{8,10},{9,11},{14,12},{15,13},{16,18},{17,... | collective-permute-start | bytes 1572872 | tf_op jit(solution)/shard_map/ppermute | solution.py:506
  387.5 31.3 %collective-permute-start.43 = (bf16[128,512]{1,0:T(8,128)(2,1)}, bf16[128,512]{1,0:T(8,128)(2,1)S(1)}, u32[]{:S(2)}, u32[]{:S(2)}) collective-permute-start(bf16[128,512]{1,0:T(8,128)(2,1)} %bitcast.137), channel_id=1, source_target_pairs={{0,4},{1,5},{2,6},{3,7},{4,0},{5,1},{6,2},{7,3},{8,12},{9,13},{10,... | collective-permute-start | bytes 393224 | tf_op jit(solution)/shard_map/ppermute | solution.py:487
  387.5 31.3 %collective-permute-start.44 = (bf16[128,512]{1,0:T(8,128)(2,1)S(1)}, bf16[128,512]{1,0:T(8,128)(2,1)S(1)}, u32[]{:S(2)}, u32[]{:S(2)}) collective-permute-start(bf16[128,512]{1,0:T(8,128)(2,1)S(1)} %bitcast.172), channel_id=1, source_target_pairs={{0,6},{1,7},{2,4},{3,5},{4,2},{5,3},{6,0},{7,1},{8,14},{9,15},{10,... | collective-permute-start | bytes 393224 | tf_op jit(solution)/shard_map/ppermute | solution.py:487
  389.0 29.9 %collective-permute-start.41 = (bf16[128,2048]{1,0:T(8,128)(2,1)S(1)}, bf16[128,2048]{1,0:T(8,128)(2,1)}, u32[]{:S(2)}, u32[]{:S(2)}) collective-permute-start(bf16[128,2048]{1,0:T(8,128)(2,1)S(1)} %get-tuple-element.299), channel_id=1, source_target_pairs={{0,6},{1,7},{6,0},{7,1},{8,14},{9,15},{14,8},{15,9},{16,22},{17,23... | collective-permute-start | bytes 1572872 | tf_op jit(solution)/shard_map/ppermute | solution.py:506
  432.5 142.0 %reduce-scatter.8.cloned.1.call-start = ((), (), s32[]{:S(2)}) async-start(), calls=%async_computation.8 | async-start | bytes 2359296 | tf_op jit(solution)/shard_map/reduce_scatter | solution.py:592
  495.3 41.3 %collective-permute-start.61 = (bf16[64,4224]{1,0:T(8,128)(2,1)S(1)}, bf16[64,4224]{1,0:T(8,128)(2,1)S(1)}, u32[]{:S(2)}, u32[]{:S(2)}) collective-permute-start(bf16[64,4224]{1,0:T(8,128)(2,1)S(1)} %get-tuple-element.279), channel_id=1, source_target_pairs={{6,0},{4,1},{2,2},{0,3},{7,4},{5,5},{3,6},{1,7},{14,8},{12,9},{10,... | collective-permute-start | bytes 1622024 | tf_op jit(solution)/shard_map/ppermute | solution.py:585
  510.5 26.5 %collective-permute-start.54 = (bf16[128,2048]{1,0:T(8,128)(2,1)S(1)}, bf16[128,2048]{1,0:T(8,128)(2,1)S(1)}, u32[]{:S(2)}, u32[]{:S(2)}) collective-permute-start(bf16[128,2048]{1,0:T(8,128)(2,1)S(1)} %add_convert_fusion), channel_id=1, source_target_pairs={{2,4},{3,5},{4,2},{5,3},{10,12},{11,13},{12,10},{13,11},{18,20},{1... | collective-permute-start | bytes 1572872 | tf_op jit(solution)/shard_map/ppermute | solution.py:506
  512.4 29.7 %collective-permute-start.53 = (bf16[128,2048]{1,0:T(8,128)(2,1)S(1)}, bf16[128,2048]{1,0:T(8,128)(2,1)S(1)}, u32[]{:S(2)}, u32[]{:S(2)}) collective-permute-start(bf16[128,2048]{1,0:T(8,128)(2,1)S(1)} %add_convert_fusion.1), channel_id=1, source_target_pairs={{0,2},{1,3},{2,0},{3,1},{4,6},{5,7},{6,4},{7,5},{8,10},{9,11},{10,... | collective-permute-start | bytes 1572872 | tf_op jit(solution)/shard_map/ppermute | solution.py:487
  (107 other events, 1018.2 us)
Sparse Core Ops, SparseCore 0:
  53.3 48.1 all-gather.3
  103.4 54.3 all-gather.5
  176.3 92.2 all-gather.7
  313.6 118.7 reduce-scatter.3
  436.1 64.2 reduce-scatter.5
  504.1 41.2 reduce-scatter.7

commit v3 on v2

--- a/solution.py
+++ b/solution.py
@@ -314,6 +314,17 @@
 
 
 HEADS = 4
+
+
+def product_cost(*sizes):
+    flops = 2
+    for size in sizes:
+        flops *= size
+    return pl.CostEstimate(flops=flops, bytes_accessed=2 * sizes[1] * sizes[2], transcendentals=0)
+
+
+def move_cost(nbytes):
+    return pl.CostEstimate(flops=0, bytes_accessed=nbytes, transcendentals=0)
 FF = 5632
 
 
@@ -366,7 +377,7 @@
         in_specs=specs,
         out_specs=pl.BlockSpec((block, cols), lambda i: (i, 0)),
         out_shape=jax.ShapeDtypeStruct((rows, cols), jnp.bfloat16),
-        cost_estimate=pl.CostEstimate(flops=2 * length * rows * cols, bytes_accessed=2 * rows * cols, transcendentals=0),
+        cost_estimate=product_cost(length, rows, cols),
         compiler_params=pltpu.CompilerParams(vmem_limit_bytes=48 * 2**20),
     )(*operands)
 
@@ -401,9 +412,34 @@
         out_specs=[pl.BlockSpec((length, n * width), lambda i: (0, 0)) for n in (1, 2)],
         out_shape=[jax.ShapeDtypeStruct((length, n * width), jnp.bfloat16) for n in (1, 2)],
         scratch_shapes=[pltpu.VMEM((length, 3 * width), jnp.float32)],
-        cost_estimate=pl.CostEstimate(flops=6 * length * depth * width, bytes_accessed=6 * depth * width, transcendentals=0),
+        cost_estimate=product_cost(length, depth, 3 * width),
         compiler_params=pltpu.CompilerParams(vmem_limit_bytes=56 * 2**20),
     )(x, y, weights)
+
+
+def head_blocks_kernel(copies, place_ref, w_ref, extra_ref, *out_refs):
+    width = HEADS * HEAD_DIM
+    for k, out_ref in enumerate(out_refs):
+        head = (place_ref[0] ^ k) // copies
+        for n in range(3):
+            start = pl.multiple_of(n * width + head * HEAD_DIM, HEAD_DIM)
+            out_ref[:, n * HEAD_DIM : (n + 1) * HEAD_DIM] = w_ref[:, pl.ds(start, HEAD_DIM)]
+        two = w_ref[:, pl.ds(pl.multiple_of(3 * width + head // 2 * 128, 128), 128)].astype(jnp.float32)
+        gate = jnp.where(head % 2 == 0, two[:, :SLOTS], two[:, SLOTS:]).astype(jnp.bfloat16)
+        out_ref[:, QKV:] = jnp.concatenate([gate, extra_ref[...]], axis=1)
+
+
+def head_blocks(weight, extra, slot, ranks):
+    rows = weight.shape[0]
+    shape = jax.ShapeDtypeStruct((rows, QKV + 2 * SLOTS), jnp.bfloat16)
+    return pl.pallas_call(
+        functools.partial(head_blocks_kernel, ranks // HEADS),
+        out_shape=[shape] * ranks,
+        in_specs=[pl.BlockSpec(memory_space=pltpu.SMEM), VMEM, VMEM],
+        out_specs=[VMEM] * ranks,
+        cost_estimate=move_cost(4 * ranks * rows * (QKV + 2 * SLOTS)),
+        compiler_params=pltpu.CompilerParams(vmem_limit_bytes=32 * 2**20),
+    )(slot.reshape(1).astype(jnp.int32), weight, extra)
 
 
 def place_kernel(axis, choices, place_ref, *refs):
@@ -427,13 +463,12 @@
     shape = list(pieces[0].shape)
     shape[axis] *= len(choices)
     vmem = pl.BlockSpec(memory_space=pltpu.VMEM)
-    nbytes = 4 * shape[0] * shape[1]
     return pl.pallas_call(
         functools.partial(place_kernel, axis, choices),
         out_shape=jax.ShapeDtypeStruct(shape, pieces[0].dtype),
         in_specs=[pl.BlockSpec(memory_space=pltpu.SMEM)] + [vmem] * len(pieces),
         out_specs=vmem,
-        cost_estimate=pl.CostEstimate(flops=0, bytes_accessed=nbytes, transcendentals=0),
+        cost_estimate=move_cost(4 * shape[0] * shape[1]),
         compiler_params=pltpu.CompilerParams(vmem_limit_bytes=48 * 2**20),
     )(jnp.stack([first, end]).astype(jnp.int32), *pieces)
 
@@ -464,9 +499,48 @@
         out_shape=[shape] * 2,
         in_specs=[pl.BlockSpec(memory_space=pltpu.SMEM)] + [VMEM] * (len(pieces) + 1),
         out_specs=[VMEM] * 2,
-        cost_estimate=pl.CostEstimate(flops=0, bytes_accessed=10 * len(choices) * size * width, transcendentals=0),
+        cost_estimate=move_cost(10 * len(choices) * size * width),
         compiler_params=pltpu.CompilerParams(vmem_limit_bytes=48 * 2**20),
     )(jnp.stack([first, end]).astype(jnp.int32), gain, *pieces)
+
+
+def nt_kernel(a_ref, b_ref, out_ref):
+    out_ref[...] = dot(a_ref[...], b_ref[...], NT, out_ref.dtype)
+
+
+def times_rows(a, weights, cols, place, block=512):
+    length = a.shape[0]
+    return pl.pallas_call(
+        nt_kernel,
+        grid=(weights.shape[0] // block,),
+        in_specs=[pl.BlockSpec(a.shape, lambda i: (0, 0)), pl.BlockSpec((block, cols), lambda i: (i, place))],
+        out_specs=pl.BlockSpec((length, block), lambda i: (0, i)),
+        out_shape=jax.ShapeDtypeStruct((length, weights.shape[0]), jnp.bfloat16),
+        cost_estimate=product_cost(length, weights.shape[0], cols),
+        compiler_params=pltpu.CompilerParams(vmem_limit_bytes=48 * 2**20),
+    )(a, weights)
+
+
+def nn_kernel(a_ref, b_ref, out_ref):
+    @pl.when(pl.program_id(0) == 0)
+    def _():
+        out_ref[...] = jnp.zeros_like(out_ref)
+
+    out_ref[...] += dot(a_ref[...], b_ref[...], NN)
+
+
+def times(a, weights, block=1024):
+    length, depth = a.shape
+    cols = weights.shape[1]
+    return pl.pallas_call(
+        nn_kernel,
+        grid=(depth // block,),
+        in_specs=[pl.BlockSpec((length, block), lambda i: (0, i)), pl.BlockSpec((block, cols), lambda i: (i, 0))],
+        out_specs=pl.BlockSpec((length, cols), lambda i: (0, 0)),
+        out_shape=jax.ShapeDtypeStruct((length, cols), jnp.float32),
+        cost_estimate=product_cost(length, depth, cols),
+        compiler_params=pltpu.CompilerParams(vmem_limit_bytes=48 * 2**20),
+    )(a, weights)
 
 
 class Layout:
@@ -615,29 +689,24 @@
     def columns(weight, *cuts):
         return [lax.dynamic_slice_in_dim(weight, start, size, 1) for start, size in cuts]
 
-    extra = jnp.zeros((rows, SLOTS), jnp.bfloat16)
-    extra = extra.at[0, :bias_len].set(gate_bias).at[1, :rows].set(norm1_gain).at[2, :rows].set(norm2_gain)
-    in_blocks, late_blocks = [], []
-    for j in range(ranks):
-        to = at.slot ^ j
-        cuts = [(n * width + to // copies * HEAD_DIM, HEAD_DIM) for n in range(3)]
-        cuts.append((3 * width + to // copies * SLOTS, SLOTS))
-        in_blocks.append(jnp.concatenate(columns(attn_weight, *cuts) + [extra], axis=1))
+    across = lambda v: jnp.pad(v, (0, SLOTS - v.shape[0]))[None, :]
+    row = lax.broadcasted_iota(jnp.int32, (rows, SLOTS), 0)
+    extra = jnp.where(row == 1, across(norm1_gain), jnp.where(row == 2, across(norm2_gain), 0))
+    extra = jnp.where(row == 0, across(gate_bias), extra).astype(jnp.bfloat16)
+    in_blocks, late_blocks = head_blocks(attn_weight[:, :proj_cols], extra, at.slot, ranks), []
     for j in range(ranks):
         cuts = [(n * FF + (at.slot ^ j) * share_ff, share_ff) for n in range(3)]
         late_blocks.append(jnp.concatenate(columns(mlp_weight, *cuts), axis=1))
     in_pieces = at.deal(in_blocks)
     out_own = attn_weight[:, proj_cols:]
-    out_near = at.spread_near(behind(out_own, in_blocks))
 
     rest = at.swap(tokens[0]).reshape(-1, width)
     dy = at.swap(cotangent[0]).reshape(-1, width)
     shard = rest.shape[0]
-    in_pieces, out_near = behind((in_pieces, out_near, rest, dy, late_blocks))[:2]
+    in_pieces = behind(in_pieces, rest, dy, late_blocks)
     w_in = at.fetch(at.dealt(in_pieces))
-    x_near = at.spread_near(behind(rest, in_pieces))
-    out_got = behind(at.spread_far(out_near), x_near)
-    both_got = behind(at.spread_far(x_near))
+    x_near, out_near = behind((at.spread_near(behind(rest, in_pieces)), at.spread_near(behind(out_own, in_pieces))))
+    both_got, out_got = behind((at.spread_far(x_near), at.spread_far(out_near)))
     out_rows = at.swap(at.joined(out_own, out_got).reshape(phases, at.half * rows, width))
     out_rows = out_rows.reshape(phases, at.half, rows, width).swapaxes(0, 1).reshape(-1, width)
     w_out = at.fetch(out_rows)
@@ -654,7 +723,7 @@
     got, choices = at.choices(both_got)
     end = (at.rank == 0) | (at.rank == ranks - 1)
     x_all, in_one = place_tokens([rest, *got], choices, at.rank, end, gain_one)
-    projected = dot(in_one, w_in, NN)
+    projected = times(in_one, w_in)
     projected = behind(projected, late_pieces[0], late_pieces[1])
     low, *saved = forward_mix(projected, bias, seg)
     low_near = at.spread_near(low, copies)
@@ -673,14 +742,16 @@
 
     dyl = at.joined(dy, behind(dy_far, after_all))
     hidden, grad_gate_up = hidden_and_grads(in_two, dyl, w_mlp, share_ff, w_mlp.shape[1], 512)
-    two_part = dot(grad_gate_up, w_gate_up, NT, jnp.bfloat16)
+    aligned = share_ff % 128 == 0
+    two_part = times_rows(grad_gate_up, w_mlp if aligned else w_gate_up, 2 * share_ff, 0)
     two_pieces = at.split(two_part)
     two_far = at.sum_far(two_pieces)
     hidden_later, grad_later = behind((hidden, grad_gate_up), two_pieces)
     grad_mlp_w = weight_grads(tn_pair_kernel, 256, in_two, grad_later, dyl, hidden_later)
-    share_mlp = at.share(grad_mlp_w)
-    two_far = behind(two_far, grad_mlp_w)
-    mlp_part = dot(behind(hidden, grad_mlp_w), w_down, NT, jnp.bfloat16)
+    passed = behind(two_far[:2], grad_mlp_w)
+    two_far = [*passed, *two_far[2:]]
+    share_mlp = at.share(behind(grad_mlp_w, passed))
+    mlp_part = times_rows(behind(hidden, grad_mlp_w), w_mlp if aligned else w_down, share_ff, 2 if aligned else 0)
     two_near = behind(at.sum_near(two_pieces, two_far), mlp_part)
     back_two = at.total(two_pieces, two_near)
     scaled_two = back_two * gain_two
@@ -709,20 +780,20 @@
     row_ids = jnp.arange(width, dtype=jnp.int32)
     owners = SLOTS // bias_len
     holds = ((row_ids % rows == 0) & (row_ids // (rows * owners) == head)).astype(jnp.float32)
-    mlp_near = at.sum_near(mlp_pieces, behind(mlp_far, grad_proj))
     mlp_far, dal_got, grad_proj = behind((mlp_far, dal_got, grad_proj))
     mlp_near = at.sum_near(mlp_pieces, mlp_far)
     grad_in_w = weight_grads(tn_extra_kernel, 512, in_one, grad_proj, holds[:, None], bias_grad)
-    share_in = at.share(behind(grad_in_w, share_mlp))
-    one_part = dot(behind(grad_proj, grad_in_w), w_in, NT, jnp.bfloat16)
+    one_part = times_rows(behind(grad_proj, grad_in_w), w_in, w_in.shape[1], 0)
     one_pieces = behind(at.split(one_part), mlp_near)
     one_far = at.sum_far(one_pieces)
     quarter = ranks // 4
-    home_first = at.home(behind(share_mlp, one_pieces), range(2 * quarter))
     dal_rows = place_pieces([dal_blocks[0], *dal_got], each, at.rank, at.rank)
     dal_rows = behind(dal_rows, one_pieces)
     grad_out_w = weight_grads(tn_kernel, min(512, dal_rows.shape[1]), dal_rows, low_all)
-    share_out = at.share(grad_out_w)
+    share_mlp = behind(share_mlp, grad_out_w)
+    share_in = at.share(behind(grad_in_w, share_mlp))
+    share_out = at.share(behind(grad_out_w, grad_in_w))
+    home_first = at.home(share_mlp, range(2 * quarter))
     mlp_out = at.total(mlp_pieces, mlp_near)
     mixed_rows = (after + mlp_out).astype(jnp.bfloat16)
     mixed = at.swap(mixed_rows.reshape(phases, block_len, width))[None]

time: 596 us -> 580 us (0.973)
  matrix products: 45.4 us -> 13.6 us
  Pallas kernels: 91.4 us -> 121 us
  waiting for transfers between devices: 199 us -> 188 us
    dot_general x6 -> x2, matrix products: 45.4 us -> 13.6 us  [dot(): lax.dot_general(a, b, (dims, ((), ())), preferred_element_type=jnp.float32)]
    pallas_call x0 -> x5, Pallas kernels: none -> 29.6 us  [the longest x3 23 us: times_rows(): pl.pallas_call(nt_kernel, grid=(weights.shape[0] // block,), in_specs=[pl...]
    ppermute x28, waiting for transfers between devices: 89 us -> 66.5 us  [between(): lax.ppermute(value, 'span', [(a * p + c, b * p + c) for a, b in pairs for...]
    ppermute x13, waiting for transfers between devices: 23.8 us -> 38 us  [across(): lax.ppermute(value, 'span', [(i, i ^ step) for i in range(self.span)])]
    all_gather x3, waiting for transfers between devices: 4.47 us -> 12.7 us  [fetch(): lax.all_gather(value, ('seqs', 'span'), axis=0, tiled=True, axis_index_gr...]
    ppermute x8, waiting for transfers between devices: 43.5 us -> 37.4 us  [home(): lax.ppermute(block, 'span', [(b, a) for a, b in self.outward(k)])]
    unnamed x130 -> x126, local copies, waits for them, and re-layouts: 30.3 us -> 32.7 us
  transfers between devices with their start and end apart: 68 -> 68, of which waited for: 26 -> 22; matrix products, arithmetic and copies ran while one was open for 16% -> 13% of each run, Pallas kernels for 10% -> 16%
where the time goes in v3:
time: 580 us; the launch traced here: 569 us
  waiting for transfers between devices  188 us (32%)
  starting transfers between devices  133 us (23%)
  Pallas kernels  121 us (21%)
  local copies, waits for them, and re-layouts  59.3 us (10%)
  other arithmetic  37.6 us (6%)
  between operations  16.2 us (3%)
  matrix products  13.6 us (2%)
    ppermute x28, waiting for transfers between devices, between(): lax.ppermute(value, 'span', [(a * p + c, b * p + c) for a, b in pairs for...  66.5 us
    ppermute x28, starting transfers between devices, between(): lax.ppermute(value, 'span', [(a * p + c, b * p + c) for a, b in pairs for...  58.3 us
    pallas_call x2, Pallas kernels, slot_call(): pl.pallas_call(kernel, out_shape=outs, in_specs=[VMEM] * len(args), out_s...  40 us
    ppermute x13, waiting for transfers between devices, across(): lax.ppermute(value, 'span', [(i, i ^ step) for i in range(self.span)])  38 us
    ppermute x8, waiting for transfers between devices, home(): lax.ppermute(block, 'span', [(b, a) for a, b in self.outward(k)])  37.4 us
    unnamed x126, local copies, waits for them, and re-layouts  32.7 us
    ppermute x8, waiting for transfers between devices, deal(): lax.ppermute(block, 'span', self.outward(k))  27.3 us
    ppermute x13, starting transfers between devices, across(): lax.ppermute(value, 'span', [(i, i ^ step) for i in range(self.span)])  26 us
  transfers between devices with their start and end apart: 68, of which 22 were waited for; matrix products, arithmetic and copies ran while one was open for 13% of the time, Pallas kernels for 16%

profile of v3, /device:TPU:5, one launch (start us, length us, event | category | flops | bytes accessed | tf_op | source)
XLA Modules:
  0.0 568.9 jit_solution(17515385240813229829)
XLA Ops:
  26.0 8.4 %collective-permute-done.2.refs_1_ = bf16[64,1664]{1,0:T(8,128)(2,1)S(1)} collective-permute-done((bf16[64,1664]{1,0:T(8,128)(2,1)S(1)}, bf16[64,1664]{1,0:T(8,128)(2,1)S(1)}, u32[]{:S(2)}, u32[]{:S(2)}) %collective-permute-start.2) | collective-permute-done | bytes 213024 | tf_op jit(solution)/shard_map/ppermute | solution.py:652
  47.5 22.3 %collective-permute-done.11.refs_4_ = bf16[64,2048]{1,0:T(8,128)(2,1)S(1)} collective-permute-done((bf16[64,2048]{1,0:T(8,128)(2,1)S(1)}, bf16[64,2048]{1,0:T(8,128)(2,1)S(1)}, u32[]{:S(2)}, u32[]{:S(2)}) %collective-permute-start.11) | collective-permute-done | bytes 262176 | tf_op jit(solution)/shard_map/ppermute | solution.py:580
  78.2 16.9 %collective-permute-done.15.refs_2_ = bf16[64,2048]{1,0:T(8,128)(2,1)} collective-permute-done((bf16[64,2048]{1,0:T(8,128)(2,1)S(1)}, bf16[64,2048]{1,0:T(8,128)(2,1)}, u32[]{:S(2)}, u32[]{:S(2)}) %collective-permute-start.15) | collective-permute-done | bytes 262176 | tf_op jit(solution)/shard_map/ppermute | solution.py:580
  122.2 6.4 %shard_map.138.proj_ref = f32[512,1664]{1,0:T(8,128)S(1)} custom-call(bf16[512,2048]{1,0:T(8,128)(2,1)S(1)} %copy-done.31, bf16[2048,1664]{1,0:T(8,128)(2,1)} %all-gather.4.cloned.1.call-done.b_ref), custom_call_target="tpu_custom_call" | custom-call | flops 3489660928 | bytes 6815744 | tf_op jit(solution)/shard_map/pallas_call | solution.py:535
  130.7 12.6 %collective-permute-done.16.refs_0_ = bf16[64,4224]{1,0:T(8,128)(2,1)S(1)} collective-permute-done((bf16[64,4224]{1,0:T(8,128)(2,1)}, bf16[64,4224]{1,0:T(8,128)(2,1)S(1)}, u32[]{:S(2)}, u32[]{:S(2)}) %collective-permute-start.16) | collective-permute-done | bytes 540704 | tf_op jit(solution)/shard_map/ppermute | solution.py:652
  151.2 14.7 %shard_map.139 = (bf16[512,512]{1,0:T(8,128)(2,1)}, f32[512,512]{1,0:T(8,128)}, f32[512,256]{1,0:T(8,128)}, f32[8,128,512]{2,1,0:T(8,128)}) custom-call(f32[512,1664]{1,0:T(8,128)} %copy-done.34, f32[1,64]{1,0:T(1,128)} %bitcast.165, s32[512,1]{1,0:T(8,128)} %copy.34.segc_ref, s32[8,1,64]{2,1,0:T(1,128)} %reshape.276.segr_ref), custom_call_target="tpu_custom_call" | custom-call | flops 12000000000 | tf_op jit(solution)/shard_map/pallas_call | solution.py:284
  175.4 20.5 %collective-permute-done.18.refs_1_ = bf16[512,512]{1,0:T(8,128)(2,1)S(1)} collective-permute-done((bf16[512,512]{1,0:T(8,128)(2,1)S(1)}, bf16[512,512]{1,0:T(8,128)(2,1)S(1)}, u32[]{:S(2)}, u32[]{:S(2)}) %collective-permute-start.18) | collective-permute-done | bytes 524320 | tf_op jit(solution)/shard_map/ppermute | solution.py:561
  201.1 11.4 %collective-permute-done.22.refs_2_ = bf16[512,512]{1,0:T(8,128)(2,1)S(1)} collective-permute-done((bf16[512,512]{1,0:T(8,128)(2,1)S(1)}, bf16[512,512]{1,0:T(8,128)(2,1)S(1)}, u32[]{:S(2)}, u32[]{:S(2)}) %collective-permute-start.22) | collective-permute-done | bytes 524320 | tf_op jit(solution)/shard_map/ppermute | solution.py:580
  228.9 8.7 %multiply_reduce_fusion = (f32[512]{0:T(512)S(1)}, f32[512,2048]{1,0:T(8,128)S(1)}) fusion(bf16[512,2048]{1,0:T(8,128)(2,1)S(1)} %shard_map.140.b_ref, bf16[2048,2048]{1,0:T(8,128)(2,1)} %all-gather.6.cloned.1.call-done, bf16[512,2048]{1,0:T(8,128)(2,1)} %copy-done.33), kind=kOutput, calls=%fused_computation.2 | convolution fusion | flops 4299161088 | bytes 16779264 | tf_op jit(solution)/shard_map/dot_general | solution.py:332
  237.7 7.6 %collective-permute-done.28.refs_2_ = bf16[128,2048]{1,0:T(8,128)(2,1)} collective-permute-done((bf16[128,2048]{1,0:T(8,128)(2,1)}, bf16[128,2048]{1,0:T(8,128)(2,1)}, u32[]{:S(2)}, u32[]{:S(2)}) %collective-permute-start.28) | collective-permute-done | bytes 524320 | tf_op jit(solution)/shard_map/ppermute | solution.py:580
  250.2 12.7 %all-gather.8.cloned.1.call-done.w_ref.b_ref = bf16[2048,4224]{1,0:T(8,128)(2,1)} async-done(((bf16[256,4224]{1,0:T(8,128)(2,1)}), bf16[2048,4224]{1,0:T(8,128)(2,1)}) %all-gather.8.cloned.1.call-update) | async-done | bytes 17301520 | tf_op jit(solution)/shard_map/all_gather | solution.py:663
  262.8 16.8 %shard_map.144 = (bf16[512,1408]{1,0:T(8,128)(2,1)}, bf16[512,2816]{1,0:T(8,128)(2,1)}) custom-call(bf16[512,2048]{1,0:T(8,128)(2,1)} %multiply_convert_fusion.x_ref.a_ref, bf16[512,2048]{1,0:T(8,128)(2,1)} %copy-done.7, bf16[2048,4224]{1,0:T(8,128)(2,1)} %all-gather.8.cloned.1.call-done.w_ref.b_ref), custom_call_target="tpu_custom_call" | custom-call | flops 8858370048 | bytes 17301504 | tf_op jit(solution)/shard_map/pallas_call | solution.py:408
  281.4 9.0 %shard_map.145 = bf16[512,2048]{1,0:T(8,128)(2,1)S(1)} custom-call(bf16[512,2816]{1,0:T(8,128)(2,1)S(1)} %copy-done.5, bf16[2048,4224]{1,0:T(8,128)(2,1)} %all-gather.8.cloned.1.call-done.w_ref.b_ref), custom_call_target="tpu_custom_call" | custom-call | flops 5905580032 | bytes 11534336 | tf_op jit(solution)/shard_map/pallas_call | solution.py:513
  298.9 14.7 %shard_map.146 = bf16[2048,4224]{1,0:T(8,128)(2,1)} custom-call(bf16[512,2048]{1,0:T(8,128)(2,1)S(1)} %copy-done.6, bf16[512,2816]{1,0:T(8,128)(2,1)} %get-tuple-element.198.a_ref.b_ref, bf16[512,2048]{1,0:T(8,128)(2,1)S(1)} %copy-done.8, bf16[512,1408]{1,0:T(8,128)(2,1)S(1)} %copy-done.9), custom_call_target="tpu_custom_call" | custom-call | flops 8858370048 | bytes 17301504 | tf_op jit(solution)/shard_map/pallas_call | solution.py:374
  326.1 7.3 %shard_map.147 = bf16[512,2048]{1,0:T(8,128)(2,1)S(1)} custom-call(bf16[512,1408]{1,0:T(8,128)(2,1)S(1)} %copy-done.10, bf16[2048,4224]{1,0:T(8,128)(2,1)} %all-gather.8.cloned.1.call-done.w_ref.b_ref), custom_call_target="tpu_custom_call" | custom-call | flops 2952790016 | bytes 5767168 | tf_op jit(solution)/shard_map/pallas_call | solution.py:513
  333.4 9.4 %collective-permute-done.33 = bf16[128,2048]{1,0:T(8,128)(2,1)} collective-permute-done((bf16[128,2048]{1,0:T(8,128)(2,1)}, bf16[128,2048]{1,0:T(8,128)(2,1)}, u32[]{:S(2)}, u32[]{:S(2)}) %collective-permute-start.33) | collective-permute-done | bytes 524320 | tf_op jit(solution)/shard_map/ppermute | solution.py:561
  379.4 25.4 %shard_map.149 = (bf16[512,1664]{1,0:T(8,128)(2,1)}, f32[1,64]{1,0:T(1,128)}) custom-call(f32[512,1664]{1,0:T(8,128)} %copy-done.34, f32[1,64]{1,0:T(1,128)} %bitcast.166, s32[512,1]{1,0:T(8,128)} %copy.34.segc_ref, s32[8,1,64]{2,1,0:T(1,128)} %reshape.276.segr_ref, f32[512,512]{1,0:T(8,128)} %get-tuple-element.215.out_ref, ...), custom_call_target="tpu_custom_call" | custom-call | flops 16000000000 | tf_op jit(solution)/shard_map/pallas_call | solution.py:284
  418.7 6.8 %shard_map.151 = bf16[512,2048]{1,0:T(8,128)(2,1)S(1)} custom-call(bf16[512,1664]{1,0:T(8,128)(2,1)S(1)} %copy-done.36, bf16[2048,1664]{1,0:T(8,128)(2,1)} %all-gather.4.cloned.1.call-done.b_ref), custom_call_target="tpu_custom_call" | custom-call | flops 3489660928 | bytes 6815744 | tf_op jit(solution)/shard_map/pallas_call | solution.py:513
  456.9 8.2 %collective-permute-done.49 = bf16[128,2048]{1,0:T(8,128)(2,1)} collective-permute-done((bf16[128,2048]{1,0:T(8,128)(2,1)}, bf16[128,2048]{1,0:T(8,128)(2,1)}, u32[]{:S(2)}, u32[]{:S(2)}) %collective-permute-start.49) | collective-permute-done | bytes 524320 | tf_op jit(solution)/shard_map/ppermute | solution.py:580
  465.1 7.3 %collective-permute-done.50 = bf16[64,4224]{1,0:T(8,128)(2,1)S(1)} collective-permute-done((bf16[64,4224]{1,0:T(8,128)(2,1)S(1)}, bf16[64,4224]{1,0:T(8,128)(2,1)S(1)}, u32[]{:S(2)}, u32[]{:S(2)}) %collective-permute-start.50) | collective-permute-done | bytes 540704 | tf_op jit(solution)/shard_map/ppermute | solution.py:659
  478.1 11.7 %collective-permute-start.61 = (bf16[64,4224]{1,0:T(8,128)(2,1)S(1)}, bf16[64,4224]{1,0:T(8,128)(2,1)S(1)}, u32[]{:S(2)}, u32[]{:S(2)}) collective-permute-start(bf16[64,4224]{1,0:T(8,128)(2,1)S(1)} %get-tuple-element.261), channel_id=1, source_target_pairs={{6,0},{4,1},{2,2},{0,3},{7,4},{5,5},{3,6},{1,7},{14,8},{12,9},{10,... | collective-permute-start | bytes 1622024 | tf_op jit(solution)/shard_map/ppermute | solution.py:659
  493.1 12.5 %collective-permute-start.53 = (bf16[128,2048]{1,0:T(8,128)(2,1)S(1)}, bf16[128,2048]{1,0:T(8,128)(2,1)S(1)}, u32[]{:S(2)}, u32[]{:S(2)}) collective-permute-start(bf16[128,2048]{1,0:T(8,128)(2,1)S(1)} %add_convert_fusion.1), channel_id=1, source_target_pairs={{0,2},{1,3},{2,0},{3,1},{4,6},{5,7},{6,4},{7,5},{8,10},{9,11},{10,... | collective-permute-start | bytes 1572872 | tf_op jit(solution)/shard_map/ppermute | solution.py:561
  505.7 12.9 %collective-permute-done.61 = bf16[64,4224]{1,0:T(8,128)(2,1)S(1)} collective-permute-done((bf16[64,4224]{1,0:T(8,128)(2,1)S(1)}, bf16[64,4224]{1,0:T(8,128)(2,1)S(1)}, u32[]{:S(2)}, u32[]{:S(2)}) %collective-permute-start.61) | collective-permute-done | bytes 540704 | tf_op jit(solution)/shard_map/ppermute | solution.py:659
  542.6 7.3 %collective-permute-done.59 = bf16[64,1664]{1,0:T(8,128)(2,1)S(1)} collective-permute-done((bf16[64,1664]{1,0:T(8,128)(2,1)S(1)}, bf16[64,1664]{1,0:T(8,128)(2,1)S(1)}, u32[]{:S(2)}, u32[]{:S(2)}) %collective-permute-start.59) | collective-permute-done | bytes 213024 | tf_op jit(solution)/shard_map/ppermute | solution.py:659
  (367 shorter events, 261.4 us)
Async XLA Ops:
  7.2 102.5 %all-gather.4.cloned.1.call-start = ((), (), s32[]{:S(2)}) async-start(), calls=%async_computation.3 | async-start | bytes 7667712 | tf_op jit(solution)/shard_map/all_gather | solution.py:663
  35.9 193.0 %all-gather.6.cloned.1.call-start = ((), (), s32[]{:S(2)}) async-start(), calls=%async_computation.4 | async-start | bytes 9437184 | tf_op jit(solution)/shard_map/all_gather | solution.py:663
  37.6 35.0 %collective-permute-start.6 = (bf16[128,2048]{1,0:T(8,128)(2,1)S(1)}, bf16[128,2048]{1,0:T(8,128)(2,1)S(1)}, u32[]{:S(2)}, u32[]{:S(2)}) collective-permute-start(bf16[128,2048]{1,0:T(8,128)(2,1)S(1)} %bitcast.130), channel_id=1, source_target_pairs={{0,2},{1,3},{2,0},{3,1},{4,6},{5,7},{6,4},{7,5},{8,10},{9,11},{10,... | collective-permute-start | bytes 1572872 | tf_op jit(solution)/shard_map/ppermute | solution.py:561
  39.6 33.1 %collective-permute-start.7 = (bf16[128,2048]{1,0:T(8,128)(2,1)S(1)}, bf16[128,2048]{1,0:T(8,128)(2,1)S(1)}, u32[]{:S(2)}, u32[]{:S(2)}) collective-permute-start(bf16[128,2048]{1,0:T(8,128)(2,1)S(1)} %bitcast.131), channel_id=1, source_target_pairs={{2,4},{3,5},{4,2},{5,3},{10,12},{11,13},{12,10},{13,11},{18,20},{1... | collective-permute-start | bytes 1572872 | tf_op jit(solution)/shard_map/ppermute | solution.py:580
  40.3 32.4 %collective-permute-start.8 = (bf16[128,2048]{1,0:T(8,128)(2,1)S(1)}, bf16[128,2048]{1,0:T(8,128)(2,1)S(1)}, u32[]{:S(2)}, u32[]{:S(2)}) collective-permute-start(bf16[128,2048]{1,0:T(8,128)(2,1)S(1)} %bitcast.132), channel_id=1, source_target_pairs={{0,6},{1,7},{6,0},{7,1},{8,14},{9,15},{14,8},{15,9},{16,22},{17,23... | collective-permute-start | bytes 1572872 | tf_op jit(solution)/shard_map/ppermute | solution.py:580
  102.0 160.8 %all-gather.8.cloned.1.call-start = ((), (), s32[]{:S(2)}) async-start(), calls=%async_computation.5 | async-start | bytes 19464192 | tf_op jit(solution)/shard_map/all_gather | solution.py:663
  102.5 40.9 %collective-permute-start.16 = (bf16[64,4224]{1,0:T(8,128)(2,1)}, bf16[64,4224]{1,0:T(8,128)(2,1)S(1)}, u32[]{:S(2)}, u32[]{:S(2)}) collective-permute-start(bf16[64,4224]{1,0:T(8,128)(2,1)} %get-tuple-element.163), channel_id=1, source_target_pairs={{0,0},{1,2},{2,4},{3,6},{4,1},{5,3},{6,5},{7,7},{8,8},{9,10},{10,1... | collective-permute-start | bytes 1622024 | tf_op jit(solution)/shard_map/ppermute | solution.py:652
  104.4 45.2 %collective-permute-start.17 = (bf16[64,4224]{1,0:T(8,128)(2,1)}, bf16[64,4224]{1,0:T(8,128)(2,1)S(1)}, u32[]{:S(2)}, u32[]{:S(2)}) collective-permute-start(bf16[64,4224]{1,0:T(8,128)(2,1)} %get-tuple-element.164), channel_id=1, source_target_pairs={{0,2},{1,0},{2,6},{3,4},{4,3},{5,1},{6,7},{7,5},{8,10},{9,8},{10,1... | collective-permute-start | bytes 1622024 | tf_op jit(solution)/shard_map/ppermute | solution.py:652
  104.5 61.3 %collective-permute-start.29 = (bf16[64,4224]{1,0:T(8,128)(2,1)}, bf16[64,4224]{1,0:T(8,128)(2,1)S(1)}, u32[]{:S(2)}, u32[]{:S(2)}) collective-permute-start(bf16[64,4224]{1,0:T(8,128)(2,1)} %get-tuple-element.190), channel_id=1, source_target_pairs={{0,4},{1,6},{2,0},{3,2},{4,5},{5,7},{6,1},{7,3},{8,12},{9,14},{10,... | collective-permute-start | bytes 1622024 | tf_op jit(solution)/shard_map/ppermute | solution.py:652
  106.1 59.8 %collective-permute-start.30 = (bf16[64,4224]{1,0:T(8,128)(2,1)S(1)}, bf16[64,4224]{1,0:T(8,128)(2,1)}, u32[]{:S(2)}, u32[]{:S(2)}) collective-permute-start(bf16[64,4224]{1,0:T(8,128)(2,1)S(1)} %copy-done.52), channel_id=1, source_target_pairs={{0,6},{1,4},{2,2},{3,0},{4,7},{5,5},{6,3},{7,1},{8,14},{9,12},{10,... | collective-permute-start | bytes 1622024 | tf_op jit(solution)/shard_map/ppermute | solution.py:652
  168.4 265.2 %reduce-scatter.4.cloned.1.call-start = ((), (), s32[]{:S(2)}) async-start(), calls=%async_computation.6 | async-start | bytes 19464192 | tf_op jit(solution)/shard_map/reduce_scatter | solution.py:666
  169.5 26.5 %collective-permute-start.18 = (bf16[512,512]{1,0:T(8,128)(2,1)S(1)}, bf16[512,512]{1,0:T(8,128)(2,1)S(1)}, u32[]{:S(2)}, u32[]{:S(2)}) collective-permute-start(bf16[512,512]{1,0:T(8,128)(2,1)S(1)} %copy-done.19), channel_id=1, source_target_pairs={{0,2},{1,3},{2,0},{3,1},{4,6},{5,7},{6,4},{7,5},{8,10},{9,11},{10,... | collective-permute-start | bytes 1572872 | tf_op jit(solution)/shard_map/ppermute | solution.py:561
  173.5 26.0 %collective-permute-start.20 = (bf16[512,512]{1,0:T(8,128)(2,1)S(1)}, bf16[512,512]{1,0:T(8,128)(2,1)S(1)}, u32[]{:S(2)}, u32[]{:S(2)}) collective-permute-start(bf16[512,512]{1,0:T(8,128)(2,1)S(1)} %copy-done.19), channel_id=1, source_target_pairs={{0,6},{1,7},{6,0},{7,1},{8,14},{9,15},{14,8},{15,9},{16,22},{17,23... | collective-permute-start | bytes 1572872 | tf_op jit(solution)/shard_map/ppermute | solution.py:580
  313.6 218.6 %reduce-scatter.6.cloned.1.call-start = ((), (), s32[]{:S(2)}) async-start(), calls=%async_computation.7 | async-start | bytes 7667712 | tf_op jit(solution)/shard_map/reduce_scatter | solution.py:666
  368.2 37.5 %collective-permute-start.39 = (bf16[128,2048]{1,0:T(8,128)(2,1)S(1)}, bf16[128,2048]{1,0:T(8,128)(2,1)S(1)}, u32[]{:S(2)}, u32[]{:S(2)}) collective-permute-start(bf16[128,2048]{1,0:T(8,128)(2,1)S(1)} %get-tuple-element.282), channel_id=1, source_target_pairs={{2,4},{3,5},{4,2},{5,3},{10,12},{11,13},{12,10},{13,11},{18,20},{1... | collective-permute-start | bytes 1572872 | tf_op jit(solution)/shard_map/ppermute | solution.py:580
  368.9 36.8 %collective-permute-start.40 = (bf16[128,2048]{1,0:T(8,128)(2,1)S(1)}, bf16[128,2048]{1,0:T(8,128)(2,1)S(1)}, u32[]{:S(2)}, u32[]{:S(2)}) collective-permute-start(bf16[128,2048]{1,0:T(8,128)(2,1)S(1)} %get-tuple-element.282), channel_id=1, source_target_pairs={{0,2},{1,3},{6,4},{7,5},{8,10},{9,11},{14,12},{15,13},{16,18},{17,... | collective-permute-start | bytes 1572872 | tf_op jit(solution)/shard_map/ppermute | solution.py:580
  373.6 32.1 %collective-permute-start.43 = (bf16[128,512]{1,0:T(8,128)(2,1)}, bf16[128,512]{1,0:T(8,128)(2,1)S(1)}, u32[]{:S(2)}, u32[]{:S(2)}) collective-permute-start(bf16[128,512]{1,0:T(8,128)(2,1)} %bitcast.127), channel_id=1, source_target_pairs={{0,4},{1,5},{2,6},{3,7},{4,0},{5,1},{6,2},{7,3},{8,12},{9,13},{10,... | collective-permute-start | bytes 393224 | tf_op jit(solution)/shard_map/ppermute | solution.py:561
  374.0 31.7 %collective-permute-start.44 = (bf16[128,512]{1,0:T(8,128)(2,1)S(1)}, bf16[128,512]{1,0:T(8,128)(2,1)S(1)}, u32[]{:S(2)}, u32[]{:S(2)}) collective-permute-start(bf16[128,512]{1,0:T(8,128)(2,1)S(1)} %bitcast.160), channel_id=1, source_target_pairs={{0,6},{1,7},{2,4},{3,5},{4,2},{5,3},{6,0},{7,1},{8,14},{9,15},{10,... | collective-permute-start | bytes 393224 | tf_op jit(solution)/shard_map/ppermute | solution.py:561
  375.8 29.9 %collective-permute-start.41 = (bf16[128,2048]{1,0:T(8,128)(2,1)S(1)}, bf16[128,2048]{1,0:T(8,128)(2,1)S(1)}, u32[]{:S(2)}, u32[]{:S(2)}) collective-permute-start(bf16[128,2048]{1,0:T(8,128)(2,1)S(1)} %get-tuple-element.281), channel_id=1, source_target_pairs={{0,6},{1,7},{6,0},{7,1},{8,14},{9,15},{14,8},{15,9},{16,22},{17,23... | collective-permute-start | bytes 1572872 | tf_op jit(solution)/shard_map/ppermute | solution.py:580
  433.7 122.7 %reduce-scatter.8.cloned.1.call-start = ((), (), s32[]{:S(2)}) async-start(), calls=%async_computation.8 | async-start | bytes 2359296 | tf_op jit(solution)/shard_map/reduce_scatter | solution.py:666
  476.5 29.1 %collective-permute-start.55 = (bf16[64,4224]{1,0:T(8,128)(2,1)S(1)}, bf16[64,4224]{1,0:T(8,128)(2,1)S(1)}, u32[]{:S(2)}, u32[]{:S(2)}) collective-permute-start(bf16[64,4224]{1,0:T(8,128)(2,1)S(1)} %get-tuple-element.262), channel_id=1, source_target_pairs={{4,0},{6,1},{0,2},{2,3},{5,4},{7,5},{1,6},{3,7},{12,8},{14,9},{8,1... | collective-permute-start | bytes 1622024 | tf_op jit(solution)/shard_map/ppermute | solution.py:659
  478.1 40.5 %collective-permute-start.61 = (bf16[64,4224]{1,0:T(8,128)(2,1)S(1)}, bf16[64,4224]{1,0:T(8,128)(2,1)S(1)}, u32[]{:S(2)}, u32[]{:S(2)}) collective-permute-start(bf16[64,4224]{1,0:T(8,128)(2,1)S(1)} %get-tuple-element.261), channel_id=1, source_target_pairs={{6,0},{4,1},{2,2},{0,3},{7,4},{5,5},{3,6},{1,7},{14,8},{12,9},{10,... | collective-permute-start | bytes 1622024 | tf_op jit(solution)/shard_map/ppermute | solution.py:659
  491.1 27.8 %collective-permute-start.54 = (bf16[128,2048]{1,0:T(8,128)(2,1)S(1)}, bf16[128,2048]{1,0:T(8,128)(2,1)S(1)}, u32[]{:S(2)}, u32[]{:S(2)}) collective-permute-start(bf16[128,2048]{1,0:T(8,128)(2,1)S(1)} %add_convert_fusion), channel_id=1, source_target_pairs={{2,4},{3,5},{4,2},{5,3},{10,12},{11,13},{12,10},{13,11},{18,20},{1... | collective-permute-start | bytes 1572872 | tf_op jit(solution)/shard_map/ppermute | solution.py:580
  493.1 31.1 %collective-permute-start.53 = (bf16[128,2048]{1,0:T(8,128)(2,1)S(1)}, bf16[128,2048]{1,0:T(8,128)(2,1)S(1)}, u32[]{:S(2)}, u32[]{:S(2)}) collective-permute-start(bf16[128,2048]{1,0:T(8,128)(2,1)S(1)} %add_convert_fusion.1), channel_id=1, source_target_pairs={{0,2},{1,3},{2,0},{3,1},{4,6},{5,7},{6,4},{7,5},{8,10},{9,11},{10,... | collective-permute-start | bytes 1572872 | tf_op jit(solution)/shard_map/ppermute | solution.py:561
  (105 other events, 1040.0 us)
Sparse Core Ops, SparseCore 0:
  36.0 48.4 all-gather.3
  102.2 53.3 all-gather.5
  168.6 94.2 all-gather.7
  313.7 119.9 reduce-scatter.3
  437.4 64.7 reduce-scatter.5
  505.9 41.2 reduce-scatter.7

commit v4 on v3

--- a/solution.py
+++ b/solution.py
@@ -194,10 +194,10 @@
         states_ref[i] = state[...]
         keep = fade.reshape(SLOTS, 1)
         send = tail * write
-        state[:SLOTS] = keep * keys_in + tn(send, k)
+        state[:SLOTS] = keep * keys_in + fine(send, k, TN)
         state[SLOTS:] = keep * values_in + fine(send, v, TN)
         pairs = nt(q, k) * same
-        score = scale * (over_sources(pairs, cum, write, falls, rises) + enter * nt(q, keys_in))
+        score = scale * (over_sources(pairs, cum, write, falls, rises) + enter * fine(q, keys_in, NT))
         prob = jnp.exp(score - jnp.max(score, axis=1, keepdims=True))
         prob = prob / jnp.sum(prob, axis=1, keepdims=True)
         mix = over_slots(prob, cum, write, falls, rises) * same
@@ -259,7 +259,7 @@
         )
         grad_ref[here, :QKV] = (dfeats * (sig * (1.0 + pre * (1.0 - sig)))).astype(jnp.bfloat16)
         heard = over_targets([(pairs, slope), (dmix, prob)], cum, falls, rises)
-        heard = heard + tail * (nt(k, dkeys) + nt(v, dvalues))
+        heard = heard + tail * (fine(k, dkeys, NT) + fine(v, dvalues, NT))
         product = dstate * state_next[...]
         held = lax.dot_general(jnp.ones((8, HEAD_DIM), jnp.float32), product[:SLOTS] + product[SLOTS:],
                                (((1,), (1,)), ((), ())), precision=lax.Precision.HIGHEST, preferred_element_type=jnp.float32)[:1]
@@ -269,7 +269,7 @@
         grad_ref[here, QKV:] = jnp.concatenate([dlogits, jnp.zeros_like(dlogits)], axis=1)
         bias_grad_ref[...] += jnp.sum(dlogits.astype(jnp.float32), axis=0, keepdims=True)
         keep = fade.reshape(SLOTS, 1)
-        state[:SLOTS] = keep * dkeys + tn(dcross, q)
+        state[:SLOTS] = keep * dkeys + fine(dcross, q, TN)
         state[SLOTS:] = keep * dvalues + fine(prob * enter, dout, TN)
         state_next[...] = states_in
         return 0

time: 580 us -> 578 us (level)
  transfers between devices with their start and end apart: 68 -> 68, of which waited for: 22 -> 22; matrix products, arithmetic and copies ran while one was open for 13% -> 13% of each run, Pallas kernels for 16% -> 17%
where the time goes in v4:
time: 578 us; the launch traced here: 570 us
  waiting for transfers between devices  187 us (32%)
  starting transfers between devices  134 us (23%)
  Pallas kernels  123 us (21%)
  local copies, waits for them, and re-layouts  59.5 us (10%)
  other arithmetic  37.6 us (7%)
  between operations  15.9 us (3%)
  matrix products  13.6 us (2%)
    ppermute x28, waiting for transfers between devices, between(): lax.ppermute(value, 'span', [(a * p + c, b * p + c) for a, b in pairs for...  66.5 us
    ppermute x28, starting transfers between devices, between(): lax.ppermute(value, 'span', [(a * p + c, b * p + c) for a, b in pairs for...  58.3 us
    pallas_call x2, Pallas kernels, slot_call(): pl.pallas_call(kernel, out_shape=outs, in_specs=[VMEM] * len(args), out_s...  41.7 us
    ppermute x8, waiting for transfers between devices, home(): lax.ppermute(block, 'span', [(b, a) for a, b in self.outward(k)])  37.4 us
    ppermute x13, waiting for transfers between devices, across(): lax.ppermute(value, 'span', [(i, i ^ step) for i in range(self.span)])  37.1 us
    unnamed x126, local copies, waits for them, and re-layouts  33 us
    ppermute x8, waiting for transfers between devices, deal(): lax.ppermute(block, 'span', self.outward(k))  26.9 us
    ppermute x13, starting transfers between devices, across(): lax.ppermute(value, 'span', [(i, i ^ step) for i in range(self.span)])  26.9 us
  transfers between devices with their start and end apart: 68, of which 22 were waited for; matrix products, arithmetic and copies ran while one was open for 13% of the time, Pallas kernels for 17%

profile of v4, /device:TPU:5, one launch (start us, length us, event | category | flops | bytes accessed | tf_op | source)
XLA Modules:
  0.0 570.5 jit_solution(2037546608679115372)
XLA Ops:
  26.0 8.4 %collective-permute-done.2.refs_1_ = bf16[64,1664]{1,0:T(8,128)(2,1)S(1)} collective-permute-done((bf16[64,1664]{1,0:T(8,128)(2,1)S(1)}, bf16[64,1664]{1,0:T(8,128)(2,1)S(1)}, u32[]{:S(2)}, u32[]{:S(2)}) %collective-permute-start.2) | collective-permute-done | bytes 213024 | tf_op jit(solution)/shard_map/ppermute | solution.py:652
  47.5 22.3 %collective-permute-done.11.refs_4_ = bf16[64,2048]{1,0:T(8,128)(2,1)S(1)} collective-permute-done((bf16[64,2048]{1,0:T(8,128)(2,1)S(1)}, bf16[64,2048]{1,0:T(8,128)(2,1)S(1)}, u32[]{:S(2)}, u32[]{:S(2)}) %collective-permute-start.11) | collective-permute-done | bytes 262176 | tf_op jit(solution)/shard_map/ppermute | solution.py:580
  78.2 16.9 %collective-permute-done.15.refs_2_ = bf16[64,2048]{1,0:T(8,128)(2,1)} collective-permute-done((bf16[64,2048]{1,0:T(8,128)(2,1)S(1)}, bf16[64,2048]{1,0:T(8,128)(2,1)}, u32[]{:S(2)}, u32[]{:S(2)}) %collective-permute-start.15) | collective-permute-done | bytes 262176 | tf_op jit(solution)/shard_map/ppermute | solution.py:580
  122.4 6.4 %shard_map.138.proj_ref = f32[512,1664]{1,0:T(8,128)S(1)} custom-call(bf16[512,2048]{1,0:T(8,128)(2,1)S(1)} %copy-done.31, bf16[2048,1664]{1,0:T(8,128)(2,1)} %all-gather.4.cloned.1.call-done.b_ref), custom_call_target="tpu_custom_call" | custom-call | flops 3489660928 | bytes 6815744 | tf_op jit(solution)/shard_map/pallas_call | solution.py:535
  131.1 12.3 %collective-permute-done.16.refs_0_ = bf16[64,4224]{1,0:T(8,128)(2,1)S(1)} collective-permute-done((bf16[64,4224]{1,0:T(8,128)(2,1)}, bf16[64,4224]{1,0:T(8,128)(2,1)S(1)}, u32[]{:S(2)}, u32[]{:S(2)}) %collective-permute-start.16) | collective-permute-done | bytes 540704 | tf_op jit(solution)/shard_map/ppermute | solution.py:652
  151.2 16.4 %shard_map.139 = (bf16[512,512]{1,0:T(8,128)(2,1)}, f32[512,512]{1,0:T(8,128)}, f32[512,256]{1,0:T(8,128)}, f32[8,128,512]{2,1,0:T(8,128)}) custom-call(f32[512,1664]{1,0:T(8,128)} %copy-done.34, f32[1,64]{1,0:T(1,128)} %bitcast.165, s32[512,1]{1,0:T(8,128)} %copy.34.segc_ref, s32[8,1,64]{2,1,0:T(1,128)} %reshape.276.segr_ref), custom_call_target="tpu_custom_call" | custom-call | flops 12000000000 | tf_op jit(solution)/shard_map/pallas_call | solution.py:284
  177.1 20.5 %collective-permute-done.18.refs_1_ = bf16[512,512]{1,0:T(8,128)(2,1)S(1)} collective-permute-done((bf16[512,512]{1,0:T(8,128)(2,1)S(1)}, bf16[512,512]{1,0:T(8,128)(2,1)S(1)}, u32[]{:S(2)}, u32[]{:S(2)}) %collective-permute-start.18) | collective-permute-done | bytes 524320 | tf_op jit(solution)/shard_map/ppermute | solution.py:561
  202.8 11.4 %collective-permute-done.22.refs_2_ = bf16[512,512]{1,0:T(8,128)(2,1)S(1)} collective-permute-done((bf16[512,512]{1,0:T(8,128)(2,1)S(1)}, bf16[512,512]{1,0:T(8,128)(2,1)S(1)}, u32[]{:S(2)}, u32[]{:S(2)}) %collective-permute-start.22) | collective-permute-done | bytes 524320 | tf_op jit(solution)/shard_map/ppermute | solution.py:580
  230.6 8.7 %multiply_reduce_fusion = (f32[512]{0:T(512)S(1)}, f32[512,2048]{1,0:T(8,128)S(1)}) fusion(bf16[512,2048]{1,0:T(8,128)(2,1)S(1)} %shard_map.140.b_ref, bf16[2048,2048]{1,0:T(8,128)(2,1)} %all-gather.6.cloned.1.call-done, bf16[512,2048]{1,0:T(8,128)(2,1)} %copy-done.33), kind=kOutput, calls=%fused_computation.2 | convolution fusion | flops 4299161088 | bytes 16779264 | tf_op jit(solution)/shard_map/dot_general | solution.py:332
  239.4 7.6 %collective-permute-done.28.refs_2_ = bf16[128,2048]{1,0:T(8,128)(2,1)} collective-permute-done((bf16[128,2048]{1,0:T(8,128)(2,1)}, bf16[128,2048]{1,0:T(8,128)(2,1)}, u32[]{:S(2)}, u32[]{:S(2)}) %collective-permute-start.28) | collective-permute-done | bytes 524320 | tf_op jit(solution)/shard_map/ppermute | solution.py:580
  252.1 12.4 %all-gather.8.cloned.1.call-done.w_ref.b_ref = bf16[2048,4224]{1,0:T(8,128)(2,1)} async-done(((bf16[256,4224]{1,0:T(8,128)(2,1)}), bf16[2048,4224]{1,0:T(8,128)(2,1)}) %all-gather.8.cloned.1.call-update) | async-done | bytes 17301520 | tf_op jit(solution)/shard_map/all_gather | solution.py:663
  264.5 16.8 %shard_map.144 = (bf16[512,1408]{1,0:T(8,128)(2,1)}, bf16[512,2816]{1,0:T(8,128)(2,1)}) custom-call(bf16[512,2048]{1,0:T(8,128)(2,1)} %multiply_convert_fusion.x_ref.a_ref, bf16[512,2048]{1,0:T(8,128)(2,1)} %copy-done.7, bf16[2048,4224]{1,0:T(8,128)(2,1)} %all-gather.8.cloned.1.call-done.w_ref.b_ref), custom_call_target="tpu_custom_call" | custom-call | flops 8858370048 | bytes 17301504 | tf_op jit(solution)/shard_map/pallas_call | solution.py:408
  283.2 9.0 %shard_map.145 = bf16[512,2048]{1,0:T(8,128)(2,1)S(1)} custom-call(bf16[512,2816]{1,0:T(8,128)(2,1)S(1)} %copy-done.5, bf16[2048,4224]{1,0:T(8,128)(2,1)} %all-gather.8.cloned.1.call-done.w_ref.b_ref), custom_call_target="tpu_custom_call" | custom-call | flops 5905580032 | bytes 11534336 | tf_op jit(solution)/shard_map/pallas_call | solution.py:513
  300.4 14.7 %shard_map.146 = bf16[2048,4224]{1,0:T(8,128)(2,1)} custom-call(bf16[512,2048]{1,0:T(8,128)(2,1)S(1)} %copy-done.6, bf16[512,2816]{1,0:T(8,128)(2,1)} %get-tuple-element.198.a_ref.b_ref, bf16[512,2048]{1,0:T(8,128)(2,1)S(1)} %copy-done.8, bf16[512,1408]{1,0:T(8,128)(2,1)S(1)} %copy-done.9), custom_call_target="tpu_custom_call" | custom-call | flops 8858370048 | bytes 17301504 | tf_op jit(solution)/shard_map/pallas_call | solution.py:374
  328.0 7.3 %shard_map.147 = bf16[512,2048]{1,0:T(8,128)(2,1)S(1)} custom-call(bf16[512,1408]{1,0:T(8,128)(2,1)S(1)} %copy-done.10, bf16[2048,4224]{1,0:T(8,128)(2,1)} %all-gather.8.cloned.1.call-done.w_ref.b_ref), custom_call_target="tpu_custom_call" | custom-call | flops 2952790016 | bytes 5767168 | tf_op jit(solution)/shard_map/pallas_call | solution.py:513
  335.3 8.5 %collective-permute-done.33 = bf16[128,2048]{1,0:T(8,128)(2,1)} collective-permute-done((bf16[128,2048]{1,0:T(8,128)(2,1)}, bf16[128,2048]{1,0:T(8,128)(2,1)}, u32[]{:S(2)}, u32[]{:S(2)}) %collective-permute-start.33) | collective-permute-done | bytes 524320 | tf_op jit(solution)/shard_map/ppermute | solution.py:561
  380.9 25.3 %shard_map.149 = (bf16[512,1664]{1,0:T(8,128)(2,1)}, f32[1,64]{1,0:T(1,128)}) custom-call(f32[512,1664]{1,0:T(8,128)} %copy-done.34, f32[1,64]{1,0:T(1,128)} %bitcast.166, s32[512,1]{1,0:T(8,128)} %copy.34.segc_ref, s32[8,1,64]{2,1,0:T(1,128)} %reshape.276.segr_ref, f32[512,512]{1,0:T(8,128)} %get-tuple-element.215.out_ref, ...), custom_call_target="tpu_custom_call" | custom-call | flops 16000000000 | tf_op jit(solution)/shard_map/pallas_call | solution.py:284
  420.3 6.9 %shard_map.151 = bf16[512,2048]{1,0:T(8,128)(2,1)S(1)} custom-call(bf16[512,1664]{1,0:T(8,128)(2,1)S(1)} %copy-done.36, bf16[2048,1664]{1,0:T(8,128)(2,1)} %all-gather.4.cloned.1.call-done.b_ref), custom_call_target="tpu_custom_call" | custom-call | flops 3489660928 | bytes 6815744 | tf_op jit(solution)/shard_map/pallas_call | solution.py:513
  458.6 8.2 %collective-permute-done.49 = bf16[128,2048]{1,0:T(8,128)(2,1)} collective-permute-done((bf16[128,2048]{1,0:T(8,128)(2,1)}, bf16[128,2048]{1,0:T(8,128)(2,1)}, u32[]{:S(2)}, u32[]{:S(2)}) %collective-permute-start.49) | collective-permute-done | bytes 524320 | tf_op jit(solution)/shard_map/ppermute | solution.py:580
  466.9 7.2 %collective-permute-done.50 = bf16[64,4224]{1,0:T(8,128)(2,1)S(1)} collective-permute-done((bf16[64,4224]{1,0:T(8,128)(2,1)S(1)}, bf16[64,4224]{1,0:T(8,128)(2,1)S(1)}, u32[]{:S(2)}, u32[]{:S(2)}) %collective-permute-start.50) | collective-permute-done | bytes 540704 | tf_op jit(solution)/shard_map/ppermute | solution.py:659
  479.8 11.6 %collective-permute-start.61 = (bf16[64,4224]{1,0:T(8,128)(2,1)S(1)}, bf16[64,4224]{1,0:T(8,128)(2,1)S(1)}, u32[]{:S(2)}, u32[]{:S(2)}) collective-permute-start(bf16[64,4224]{1,0:T(8,128)(2,1)S(1)} %get-tuple-element.261), channel_id=1, source_target_pairs={{6,0},{4,1},{2,2},{0,3},{7,4},{5,5},{3,6},{1,7},{14,8},{12,9},{10,... | collective-permute-start | bytes 1622024 | tf_op jit(solution)/shard_map/ppermute | solution.py:659
  494.6 12.6 %collective-permute-start.53 = (bf16[128,2048]{1,0:T(8,128)(2,1)S(1)}, bf16[128,2048]{1,0:T(8,128)(2,1)S(1)}, u32[]{:S(2)}, u32[]{:S(2)}) collective-permute-start(bf16[128,2048]{1,0:T(8,128)(2,1)S(1)} %add_convert_fusion.1), channel_id=1, source_target_pairs={{0,2},{1,3},{2,0},{3,1},{4,6},{5,7},{6,4},{7,5},{8,10},{9,11},{10,... | collective-permute-start | bytes 1572872 | tf_op jit(solution)/shard_map/ppermute | solution.py:561
  507.4 12.8 %collective-permute-done.61 = bf16[64,4224]{1,0:T(8,128)(2,1)S(1)} collective-permute-done((bf16[64,4224]{1,0:T(8,128)(2,1)S(1)}, bf16[64,4224]{1,0:T(8,128)(2,1)S(1)}, u32[]{:S(2)}, u32[]{:S(2)}) %collective-permute-start.61) | collective-permute-done | bytes 540704 | tf_op jit(solution)/shard_map/ppermute | solution.py:659
  544.4 7.3 %collective-permute-done.59 = bf16[64,1664]{1,0:T(8,128)(2,1)S(1)} collective-permute-done((bf16[64,1664]{1,0:T(8,128)(2,1)S(1)}, bf16[64,1664]{1,0:T(8,128)(2,1)S(1)}, u32[]{:S(2)}, u32[]{:S(2)}) %collective-permute-start.59) | collective-permute-done | bytes 213024 | tf_op jit(solution)/shard_map/ppermute | solution.py:659
  (367 shorter events, 263.0 us)
Async XLA Ops:
  7.2 102.5 %all-gather.4.cloned.1.call-start = ((), (), s32[]{:S(2)}) async-start(), calls=%async_computation.3 | async-start | bytes 7667712 | tf_op jit(solution)/shard_map/all_gather | solution.py:663
  35.9 194.7 %all-gather.6.cloned.1.call-start = ((), (), s32[]{:S(2)}) async-start(), calls=%async_computation.4 | async-start | bytes 9437184 | tf_op jit(solution)/shard_map/all_gather | solution.py:663
  37.6 35.0 %collective-permute-start.6 = (bf16[128,2048]{1,0:T(8,128)(2,1)S(1)}, bf16[128,2048]{1,0:T(8,128)(2,1)S(1)}, u32[]{:S(2)}, u32[]{:S(2)}) collective-permute-start(bf16[128,2048]{1,0:T(8,128)(2,1)S(1)} %bitcast.130), channel_id=1, source_target_pairs={{0,2},{1,3},{2,0},{3,1},{4,6},{5,7},{6,4},{7,5},{8,10},{9,11},{10,... | collective-permute-start | bytes 1572872 | tf_op jit(solution)/shard_map/ppermute | solution.py:561
  39.6 33.1 %collective-permute-start.7 = (bf16[128,2048]{1,0:T(8,128)(2,1)S(1)}, bf16[128,2048]{1,0:T(8,128)(2,1)S(1)}, u32[]{:S(2)}, u32[]{:S(2)}) collective-permute-start(bf16[128,2048]{1,0:T(8,128)(2,1)S(1)} %bitcast.131), channel_id=1, source_target_pairs={{2,4},{3,5},{4,2},{5,3},{10,12},{11,13},{12,10},{13,11},{18,20},{1... | collective-permute-start | bytes 1572872 | tf_op jit(solution)/shard_map/ppermute | solution.py:580
  40.3 32.4 %collective-permute-start.8 = (bf16[128,2048]{1,0:T(8,128)(2,1)S(1)}, bf16[128,2048]{1,0:T(8,128)(2,1)S(1)}, u32[]{:S(2)}, u32[]{:S(2)}) collective-permute-start(bf16[128,2048]{1,0:T(8,128)(2,1)S(1)} %bitcast.132), channel_id=1, source_target_pairs={{0,6},{1,7},{6,0},{7,1},{8,14},{9,15},{14,8},{15,9},{16,22},{17,23... | collective-permute-start | bytes 1572872 | tf_op jit(solution)/shard_map/ppermute | solution.py:580
  102.0 162.5 %all-gather.8.cloned.1.call-start = ((), (), s32[]{:S(2)}) async-start(), calls=%async_computation.5 | async-start | bytes 19464192 | tf_op jit(solution)/shard_map/all_gather | solution.py:663
  102.5 40.9 %collective-permute-start.16 = (bf16[64,4224]{1,0:T(8,128)(2,1)}, bf16[64,4224]{1,0:T(8,128)(2,1)S(1)}, u32[]{:S(2)}, u32[]{:S(2)}) collective-permute-start(bf16[64,4224]{1,0:T(8,128)(2,1)} %get-tuple-element.163), channel_id=1, source_target_pairs={{0,0},{1,2},{2,4},{3,6},{4,1},{5,3},{6,5},{7,7},{8,8},{9,10},{10,1... | collective-permute-start | bytes 1622024 | tf_op jit(solution)/shard_map/ppermute | solution.py:652
  104.4 45.2 %collective-permute-start.17 = (bf16[64,4224]{1,0:T(8,128)(2,1)}, bf16[64,4224]{1,0:T(8,128)(2,1)S(1)}, u32[]{:S(2)}, u32[]{:S(2)}) collective-permute-start(bf16[64,4224]{1,0:T(8,128)(2,1)} %get-tuple-element.164), channel_id=1, source_target_pairs={{0,2},{1,0},{2,6},{3,4},{4,3},{5,1},{6,7},{7,5},{8,10},{9,8},{10,1... | collective-permute-start | bytes 1622024 | tf_op jit(solution)/shard_map/ppermute | solution.py:652
  104.5 63.0 %collective-permute-start.29 = (bf16[64,4224]{1,0:T(8,128)(2,1)}, bf16[64,4224]{1,0:T(8,128)(2,1)S(1)}, u32[]{:S(2)}, u32[]{:S(2)}) collective-permute-start(bf16[64,4224]{1,0:T(8,128)(2,1)} %get-tuple-element.190), channel_id=1, source_target_pairs={{0,4},{1,6},{2,0},{3,2},{4,5},{5,7},{6,1},{7,3},{8,12},{9,14},{10,... | collective-permute-start | bytes 1622024 | tf_op jit(solution)/shard_map/ppermute | solution.py:652
  106.1 61.5 %collective-permute-start.30 = (bf16[64,4224]{1,0:T(8,128)(2,1)S(1)}, bf16[64,4224]{1,0:T(8,128)(2,1)}, u32[]{:S(2)}, u32[]{:S(2)}) collective-permute-start(bf16[64,4224]{1,0:T(8,128)(2,1)S(1)} %copy-done.52), channel_id=1, source_target_pairs={{0,6},{1,4},{2,2},{3,0},{4,7},{5,5},{6,3},{7,1},{8,14},{9,12},{10,... | collective-permute-start | bytes 1622024 | tf_op jit(solution)/shard_map/ppermute | solution.py:652
  170.1 265.2 %reduce-scatter.4.cloned.1.call-start = ((), (), s32[]{:S(2)}) async-start(), calls=%async_computation.6 | async-start | bytes 19464192 | tf_op jit(solution)/shard_map/reduce_scatter | solution.py:666
  171.2 26.5 %collective-permute-start.18 = (bf16[512,512]{1,0:T(8,128)(2,1)S(1)}, bf16[512,512]{1,0:T(8,128)(2,1)S(1)}, u32[]{:S(2)}, u32[]{:S(2)}) collective-permute-start(bf16[512,512]{1,0:T(8,128)(2,1)S(1)} %copy-done.19), channel_id=1, source_target_pairs={{0,2},{1,3},{2,0},{3,1},{4,6},{5,7},{6,4},{7,5},{8,10},{9,11},{10,... | collective-permute-start | bytes 1572872 | tf_op jit(solution)/shard_map/ppermute | solution.py:561
  175.2 26.0 %collective-permute-start.20 = (bf16[512,512]{1,0:T(8,128)(2,1)S(1)}, bf16[512,512]{1,0:T(8,128)(2,1)S(1)}, u32[]{:S(2)}, u32[]{:S(2)}) collective-permute-start(bf16[512,512]{1,0:T(8,128)(2,1)S(1)} %copy-done.19), channel_id=1, source_target_pairs={{0,6},{1,7},{6,0},{7,1},{8,14},{9,15},{14,8},{15,9},{16,22},{17,23... | collective-permute-start | bytes 1572872 | tf_op jit(solution)/shard_map/ppermute | solution.py:580
  315.1 218.9 %reduce-scatter.6.cloned.1.call-start = ((), (), s32[]{:S(2)}) async-start(), calls=%async_computation.7 | async-start | bytes 7667712 | tf_op jit(solution)/shard_map/reduce_scatter | solution.py:666
  370.0 37.2 %collective-permute-start.39 = (bf16[128,2048]{1,0:T(8,128)(2,1)S(1)}, bf16[128,2048]{1,0:T(8,128)(2,1)S(1)}, u32[]{:S(2)}, u32[]{:S(2)}) collective-permute-start(bf16[128,2048]{1,0:T(8,128)(2,1)S(1)} %get-tuple-element.282), channel_id=1, source_target_pairs={{2,4},{3,5},{4,2},{5,3},{10,12},{11,13},{12,10},{13,11},{18,20},{1... | collective-permute-start | bytes 1572872 | tf_op jit(solution)/shard_map/ppermute | solution.py:580
  370.7 36.5 %collective-permute-start.40 = (bf16[128,2048]{1,0:T(8,128)(2,1)S(1)}, bf16[128,2048]{1,0:T(8,128)(2,1)S(1)}, u32[]{:S(2)}, u32[]{:S(2)}) collective-permute-start(bf16[128,2048]{1,0:T(8,128)(2,1)S(1)} %get-tuple-element.282), channel_id=1, source_target_pairs={{0,2},{1,3},{6,4},{7,5},{8,10},{9,11},{14,12},{15,13},{16,18},{17,... | collective-permute-start | bytes 1572872 | tf_op jit(solution)/shard_map/ppermute | solution.py:580
  375.2 31.9 %collective-permute-start.43 = (bf16[128,512]{1,0:T(8,128)(2,1)}, bf16[128,512]{1,0:T(8,128)(2,1)S(1)}, u32[]{:S(2)}, u32[]{:S(2)}) collective-permute-start(bf16[128,512]{1,0:T(8,128)(2,1)} %bitcast.127), channel_id=1, source_target_pairs={{0,4},{1,5},{2,6},{3,7},{4,0},{5,1},{6,2},{7,3},{8,12},{9,13},{10,... | collective-permute-start | bytes 393224 | tf_op jit(solution)/shard_map/ppermute | solution.py:561
  375.7 31.4 %collective-permute-start.44 = (bf16[128,512]{1,0:T(8,128)(2,1)S(1)}, bf16[128,512]{1,0:T(8,128)(2,1)S(1)}, u32[]{:S(2)}, u32[]{:S(2)}) collective-permute-start(bf16[128,512]{1,0:T(8,128)(2,1)S(1)} %bitcast.160), channel_id=1, source_target_pairs={{0,6},{1,7},{2,4},{3,5},{4,2},{5,3},{6,0},{7,1},{8,14},{9,15},{10,... | collective-permute-start | bytes 393224 | tf_op jit(solution)/shard_map/ppermute | solution.py:561
  377.6 29.6 %collective-permute-start.41 = (bf16[128,2048]{1,0:T(8,128)(2,1)S(1)}, bf16[128,2048]{1,0:T(8,128)(2,1)S(1)}, u32[]{:S(2)}, u32[]{:S(2)}) collective-permute-start(bf16[128,2048]{1,0:T(8,128)(2,1)S(1)} %get-tuple-element.281), channel_id=1, source_target_pairs={{0,6},{1,7},{6,0},{7,1},{8,14},{9,15},{14,8},{15,9},{16,22},{17,23... | collective-permute-start | bytes 1572872 | tf_op jit(solution)/shard_map/ppermute | solution.py:580
  435.4 122.8 %reduce-scatter.8.cloned.1.call-start = ((), (), s32[]{:S(2)}) async-start(), calls=%async_computation.8 | async-start | bytes 2359296 | tf_op jit(solution)/shard_map/reduce_scatter | solution.py:666
  478.2 29.1 %collective-permute-start.55 = (bf16[64,4224]{1,0:T(8,128)(2,1)S(1)}, bf16[64,4224]{1,0:T(8,128)(2,1)S(1)}, u32[]{:S(2)}, u32[]{:S(2)}) collective-permute-start(bf16[64,4224]{1,0:T(8,128)(2,1)S(1)} %get-tuple-element.262), channel_id=1, source_target_pairs={{4,0},{6,1},{0,2},{2,3},{5,4},{7,5},{1,6},{3,7},{12,8},{14,9},{8,1... | collective-permute-start | bytes 1622024 | tf_op jit(solution)/shard_map/ppermute | solution.py:659
  479.8 40.5 %collective-permute-start.61 = (bf16[64,4224]{1,0:T(8,128)(2,1)S(1)}, bf16[64,4224]{1,0:T(8,128)(2,1)S(1)}, u32[]{:S(2)}, u32[]{:S(2)}) collective-permute-start(bf16[64,4224]{1,0:T(8,128)(2,1)S(1)} %get-tuple-element.261), channel_id=1, source_target_pairs={{6,0},{4,1},{2,2},{0,3},{7,4},{5,5},{3,6},{1,7},{14,8},{12,9},{10,... | collective-permute-start | bytes 1622024 | tf_op jit(solution)/shard_map/ppermute | solution.py:659
  492.7 27.9 %collective-permute-start.54 = (bf16[128,2048]{1,0:T(8,128)(2,1)S(1)}, bf16[128,2048]{1,0:T(8,128)(2,1)S(1)}, u32[]{:S(2)}, u32[]{:S(2)}) collective-permute-start(bf16[128,2048]{1,0:T(8,128)(2,1)S(1)} %add_convert_fusion), channel_id=1, source_target_pairs={{2,4},{3,5},{4,2},{5,3},{10,12},{11,13},{12,10},{13,11},{18,20},{1... | collective-permute-start | bytes 1572872 | tf_op jit(solution)/shard_map/ppermute | solution.py:580
  494.6 31.3 %collective-permute-start.53 = (bf16[128,2048]{1,0:T(8,128)(2,1)S(1)}, bf16[128,2048]{1,0:T(8,128)(2,1)S(1)}, u32[]{:S(2)}, u32[]{:S(2)}) collective-permute-start(bf16[128,2048]{1,0:T(8,128)(2,1)S(1)} %add_convert_fusion.1), channel_id=1, source_target_pairs={{0,2},{1,3},{2,0},{3,1},{4,6},{5,7},{6,4},{7,5},{8,10},{9,11},{10,... | collective-permute-start | bytes 1572872 | tf_op jit(solution)/shard_map/ppermute | solution.py:561
  (105 other events, 1039.2 us)
Sparse Core Ops, SparseCore 0:
  36.0 48.4 all-gather.3
  102.2 53.3 all-gather.5
  170.3 94.2 all-gather.7
  315.2 120.1 reduce-scatter.3
  439.1 64.2 reduce-scatter.5
  507.1 41.2 reduce-scatter.7

commit v5 on v4

--- a/solution.py
+++ b/solution.py
@@ -382,6 +382,39 @@
     )(*operands)
 
 
+def attn_grads_kernel(owned, parts, a_ref, b_ref, holds_ref, bias_ref, c_ref, d_ref, out_ref):
+    width, cols = b_ref.shape[1], d_ref.shape[1] // parts
+    first = dot(a_ref[...], b_ref[...], TN)
+    out_ref[:, : width - 128] = first[:, : width - 128].astype(jnp.bfloat16)
+    extra = holds_ref[...] * bias_ref[...]
+    out_ref[:, width - 128 : width] = (first[:, width - 128 :] + extra).astype(jnp.bfloat16)
+    second = dot(c_ref[...], d_ref[...], TN, jnp.bfloat16)
+    for owner in range(second.shape[0] // owned):
+        for part in range(parts):
+            place = (owner * parts + part) * owned
+            tile = second[owner * owned : (owner + 1) * owned, part * cols : (part + 1) * cols]
+            out_ref[place : place + owned, width:] = tile
+
+
+def attn_grads(a, b, holds, bias, c, d, owned, parts):
+    (length, rows), width = a.shape, b.shape[1]
+    step = 128 // owned
+    block, cols = step * owned * parts, width + d.shape[1] // parts
+    whole = lambda v: pl.BlockSpec(v.shape, lambda i: (0, 0))
+    return pl.pallas_call(
+        functools.partial(attn_grads_kernel, owned, parts),
+        grid=(rows // block,),
+        in_specs=[
+            pl.BlockSpec((length, block), lambda i: (0, i)), whole(b), pl.BlockSpec((block, 1), lambda i: (i, 0)),
+            whole(bias), pl.BlockSpec((length, 128), lambda i: (0, i)), whole(d),
+        ],
+        out_specs=pl.BlockSpec((block, cols), lambda i: (i, 0)),
+        out_shape=jax.ShapeDtypeStruct((rows, cols), jnp.bfloat16),
+        cost_estimate=product_cost(length, rows, cols),
+        compiler_params=pltpu.CompilerParams(vmem_limit_bytes=56 * 2**20),
+    )(a, b, holds, bias, c, d)
+
+
 def hidden_kernel(width, x_ref, y_ref, w_ref, hid_ref, grad_ref, acc):
     step = pl.program_id(0)
 
@@ -732,7 +765,7 @@
     low_got = behind(at.spread_far(low_near))
     low_all = at.joined(low, low_got, 1, copies)
 
-    dy_near = at.spread_near(behind(dy, low_got))
+    dy_near = at.spread_near(behind(dy, low_near[:2]))
     dy_far = at.spread_far(dy_near)
     after_all = x_all.astype(jnp.float32) + dot(low_all, w_out, NT)
     in_two = (after_all * rms_scale(after_all) * gain_two).astype(jnp.bfloat16)
@@ -782,26 +815,23 @@
     holds = ((row_ids % rows == 0) & (row_ids // (rows * owners) == head)).astype(jnp.float32)
     mlp_far, dal_got, grad_proj = behind((mlp_far, dal_got, grad_proj))
     mlp_near = at.sum_near(mlp_pieces, mlp_far)
-    grad_in_w = weight_grads(tn_extra_kernel, 512, in_one, grad_proj, holds[:, None], bias_grad)
-    one_part = times_rows(behind(grad_proj, grad_in_w), w_in, w_in.shape[1], 0)
+    dal_rows = place_pieces([dal_blocks[0], *dal_got], each, at.rank, at.rank)
+    grad_attn_w = attn_grads(in_one, grad_proj, holds[:, None], bias_grad, dal_rows, low_all, rows, ranks)
+    one_part = times_rows(behind(grad_proj, grad_attn_w), w_in, w_in.shape[1], 0)
     one_pieces = behind(at.split(one_part), mlp_near)
     one_far = at.sum_far(one_pieces)
     quarter = ranks // 4
-    dal_rows = place_pieces([dal_blocks[0], *dal_got], each, at.rank, at.rank)
-    dal_rows = behind(dal_rows, one_pieces)
-    grad_out_w = weight_grads(tn_kernel, min(512, dal_rows.shape[1]), dal_rows, low_all)
-    share_mlp = behind(share_mlp, grad_out_w)
-    share_in = at.share(behind(grad_in_w, share_mlp))
-    share_out = at.share(behind(grad_out_w, grad_in_w))
+    share_mlp = behind(share_mlp, one_pieces)
+    share_attn = at.share(behind(grad_attn_w, share_mlp))
     home_first = at.home(share_mlp, range(2 * quarter))
     mlp_out = at.total(mlp_pieces, mlp_near)
     mixed_rows = (after + mlp_out).astype(jnp.bfloat16)
     mixed = at.swap(mixed_rows.reshape(phases, block_len, width))[None]
-    one_far, home_first, mixed = behind((one_far, home_first, mixed), grad_out_w)
+    one_far, home_first, mixed = behind((one_far, home_first, mixed))
     one_near = at.sum_near(one_pieces, one_far)
     home_second = at.home(behind(share_mlp, home_first), range(2 * quarter, ranks))
-    in_home = at.home(behind(share_in, home_first), range(0, ranks, copies))
-    back_one = at.total(one_pieces, behind(one_near, home_second[0])) / copies
+    in_home = at.home(behind(share_attn[:, : gate_end + SLOTS], home_first), range(0, ranks, copies))
+    back_one = at.total(one_pieces, behind(one_near, home_second[0], in_home[0], in_home[1])) / copies
     scaled_one = back_one * gain_one
     rest_float = rest.astype(jnp.float32)
     scale_one = rms_scale(rest_float)
@@ -825,7 +855,8 @@
     ]
     for j in range(HEADS):
         parts.append(sum(jnp.where(slot_head ^ n == j, p[:, qkv:gate_end], 0) for n, p in enumerate(in_home)))
-    parts.append(share_out)
+    by_part = share_attn[:, gate_end + SLOTS :].reshape(ranks, rows, -1)
+    parts += [by_part[j] for j in range(ranks)]
     grad_attn = jnp.concatenate(parts, axis=1).astype(jnp.float32)
     attn_float = attn_weight[:, :proj_cols].astype(jnp.float32)
     gain_grad_one = jnp.sum(grad_attn[:, :proj_cols] * attn_float, axis=1) / norm1_gain.astype(jnp.float32)

time: 578 us -> 577 us (level)
  waiting for transfers between devices: 187 us -> 177 us
    pallas_call x0 -> x1, Pallas kernels: none -> 10.3 us  [attn_grads(): pl.pallas_call(functools.partial(attn_grads_kernel, owned, parts), grid=(...]
    ppermute x13, waiting for transfers between devices: 37.1 us -> 27.4 us  [across(): lax.ppermute(value, 'span', [(i, i ^ step) for i in range(self.span)])]
    pallas_call x3 -> x1, Pallas kernels: 22.1 us -> 14.6 us  [weight_grads(): pl.pallas_call(kernel, grid=(rows // block,), in_specs=specs, out_specs=p...]
  transfers between devices with their start and end apart: 68 -> 67, of which waited for: 22 -> 24; matrix products, arithmetic and copies ran while one was open for 13% -> 14% of each run, Pallas kernels for 17% -> 17%
where the time goes in v5:
time: 577 us; the launch traced here: 567 us
  waiting for transfers between devices  177 us (31%)
  starting transfers between devices  134 us (23%)
  Pallas kernels  126 us (22%)
  local copies, waits for them, and re-layouts  60 us (10%)
  other arithmetic  39.3 us (7%)
  between operations  15.5 us (3%)
  matrix products  14.3 us (2%)
    ppermute x28, waiting for transfers between devices, between(): lax.ppermute(value, 'span', [(a * p + c, b * p + c) for a, b in pairs for...  69.3 us
    ppermute x28, starting transfers between devices, between(): lax.ppermute(value, 'span', [(a * p + c, b * p + c) for a, b in pairs for...  56.2 us
    pallas_call x2, Pallas kernels, slot_call(): pl.pallas_call(kernel, out_shape=outs, in_specs=[VMEM] * len(args), out_s...  41.6 us
    ppermute x8, waiting for transfers between devices, home(): lax.ppermute(block, 'span', [(b, a) for a, b in self.outward(k)])  38.1 us
    unnamed x126, local copies, waits for them, and re-layouts  33.7 us
    ppermute x13, starting transfers between devices, across(): lax.ppermute(value, 'span', [(i, i ^ step) for i in range(self.span)])  27.9 us
    ppermute x13, waiting for transfers between devices, across(): lax.ppermute(value, 'span', [(i, i ^ step) for i in range(self.span)])  27.4 us
    ppermute x8, starting transfers between devices, home(): lax.ppermute(block, 'span', [(b, a) for a, b in self.outward(k)])  26 us
  transfers between devices with their start and end apart: 67, of which 24 were waited for; matrix products, arithmetic and copies ran while one was open for 14% of the time, Pallas kernels for 17%

profile of v5, /device:TPU:5, one launch (start us, length us, event | category | flops | bytes accessed | tf_op | source)
XLA Modules:
  0.0 567.0 jit_solution(3868853587588582074)
XLA Ops:
  27.8 6.5 %collective-permute-done.2.refs_1_ = bf16[64,1664]{1,0:T(8,128)(2,1)S(1)} collective-permute-done((bf16[64,1664]{1,0:T(8,128)(2,1)S(1)}, bf16[64,1664]{1,0:T(8,128)(2,1)S(1)}, u32[]{:S(2)}, u32[]{:S(2)}) %collective-permute-start.2) | collective-permute-done | bytes 213024 | tf_op jit(solution)/shard_map/ppermute | solution.py:685
  47.5 22.3 %collective-permute-done.11.refs_4_ = bf16[64,2048]{1,0:T(8,128)(2,1)S(1)} collective-permute-done((bf16[64,2048]{1,0:T(8,128)(2,1)S(1)}, bf16[64,2048]{1,0:T(8,128)(2,1)S(1)}, u32[]{:S(2)}, u32[]{:S(2)}) %collective-permute-start.11) | collective-permute-done | bytes 262176 | tf_op jit(solution)/shard_map/ppermute | solution.py:613
  78.2 16.9 %collective-permute-done.15.refs_2_ = bf16[64,2048]{1,0:T(8,128)(2,1)} collective-permute-done((bf16[64,2048]{1,0:T(8,128)(2,1)S(1)}, bf16[64,2048]{1,0:T(8,128)(2,1)}, u32[]{:S(2)}, u32[]{:S(2)}) %collective-permute-start.15) | collective-permute-done | bytes 262176 | tf_op jit(solution)/shard_map/ppermute | solution.py:613
  122.4 6.5 %shard_map.138.proj_ref = f32[512,1664]{1,0:T(8,128)S(1)} custom-call(bf16[512,2048]{1,0:T(8,128)(2,1)S(1)} %copy-done.25, bf16[2048,1664]{1,0:T(8,128)(2,1)} %all-gather.4.cloned.1.call-done.b_ref), custom_call_target="tpu_custom_call" | custom-call | flops 3489660928 | bytes 6815744 | tf_op jit(solution)/shard_map/pallas_call | solution.py:568
  131.1 12.3 %collective-permute-done.16.refs_0_ = bf16[64,4224]{1,0:T(8,128)(2,1)S(1)} collective-permute-done((bf16[64,4224]{1,0:T(8,128)(2,1)}, bf16[64,4224]{1,0:T(8,128)(2,1)S(1)}, u32[]{:S(2)}, u32[]{:S(2)}) %collective-permute-start.16) | collective-permute-done | bytes 540704 | tf_op jit(solution)/shard_map/ppermute | solution.py:685
  151.1 16.4 %shard_map.139 = (bf16[512,512]{1,0:T(8,128)(2,1)}, f32[512,512]{1,0:T(8,128)}, f32[512,256]{1,0:T(8,128)}, f32[8,128,512]{2,1,0:T(8,128)}) custom-call(f32[512,1664]{1,0:T(8,128)} %copy-done.27, f32[1,64]{1,0:T(1,128)} %bitcast.150, s32[512,1]{1,0:T(8,128)} %copy.38.segc_ref, s32[8,1,64]{2,1,0:T(1,128)} %reshape.285.segr_ref), custom_call_target="tpu_custom_call" | custom-call | flops 12000000000 | tf_op jit(solution)/shard_map/pallas_call | solution.py:284
  175.2 11.2 %collective-permute-done.18.refs_1_ = bf16[512,512]{1,0:T(8,128)(2,1)S(1)} collective-permute-done((bf16[512,512]{1,0:T(8,128)(2,1)S(1)}, bf16[512,512]{1,0:T(8,128)(2,1)S(1)}, u32[]{:S(2)}, u32[]{:S(2)}) %collective-permute-start.18) | collective-permute-done | bytes 524320 | tf_op jit(solution)/shard_map/ppermute | solution.py:594
  211.7 15.8 %collective-permute-done.22.refs_2_ = bf16[512,512]{1,0:T(8,128)(2,1)} collective-permute-done((bf16[512,512]{1,0:T(8,128)(2,1)S(1)}, bf16[512,512]{1,0:T(8,128)(2,1)}, u32[]{:S(2)}, u32[]{:S(2)}) %collective-permute-start.22) | collective-permute-done | bytes 524320 | tf_op jit(solution)/shard_map/ppermute | solution.py:613
  233.1 9.4 %multiply_reduce_fusion = (f32[512]{0:T(512)S(1)}, f32[512,2048]{1,0:T(8,128)S(1)}) fusion(bf16[512,2048]{1,0:T(8,128)(2,1)S(1)} %shard_map.140.d_ref, bf16[2048,2048]{1,0:T(8,128)(2,1)} %all-gather.6.cloned.1.call-done, bf16[512,2048]{1,0:T(8,128)(2,1)} %copy-done.26), kind=kOutput, calls=%fused_computation.2 | convolution fusion | flops 4299161088 | bytes 16779264 | tf_op jit(solution)/shard_map/dot_general | solution.py:332
  249.5 14.9 %all-gather.8.cloned.1.call-done.w_ref.b_ref = bf16[2048,4224]{1,0:T(8,128)(2,1)} async-done(((bf16[256,4224]{1,0:T(8,128)(2,1)}), bf16[2048,4224]{1,0:T(8,128)(2,1)}) %all-gather.8.cloned.1.call-update) | async-done | bytes 17301520 | tf_op jit(solution)/shard_map/all_gather | solution.py:696
  264.5 16.8 %shard_map.144 = (bf16[512,1408]{1,0:T(8,128)(2,1)}, bf16[512,2816]{1,0:T(8,128)(2,1)}) custom-call(bf16[512,2048]{1,0:T(8,128)(2,1)} %multiply_convert_fusion.x_ref.a_ref, bf16[512,2048]{1,0:T(8,128)(2,1)} %copy-done.5, bf16[2048,4224]{1,0:T(8,128)(2,1)} %all-gather.8.cloned.1.call-done.w_ref.b_ref), custom_call_target="tpu_custom_call" | custom-call | flops 8858370048 | bytes 17301504 | tf_op jit(solution)/shard_map/pallas_call | solution.py:441
  283.1 9.0 %shard_map.145 = bf16[512,2048]{1,0:T(8,128)(2,1)S(1)} custom-call(bf16[512,2816]{1,0:T(8,128)(2,1)S(1)} %copy-done.2, bf16[2048,4224]{1,0:T(8,128)(2,1)} %all-gather.8.cloned.1.call-done.w_ref.b_ref), custom_call_target="tpu_custom_call" | custom-call | flops 5905580032 | bytes 11534336 | tf_op jit(solution)/shard_map/pallas_call | solution.py:546
  300.3 14.6 %shard_map.146 = bf16[2048,4224]{1,0:T(8,128)(2,1)} custom-call(bf16[512,2048]{1,0:T(8,128)(2,1)S(1)} %copy-done.3, bf16[512,2816]{1,0:T(8,128)(2,1)} %get-tuple-element.196.a_ref.b_ref, bf16[512,2048]{1,0:T(8,128)(2,1)S(1)} %copy-done.6, bf16[512,1408]{1,0:T(8,128)(2,1)S(1)} %copy-done.7), custom_call_target="tpu_custom_call" | custom-call | flops 8858370048 | bytes 17301504 | tf_op jit(solution)/shard_map/pallas_call | solution.py:374
  328.7 7.3 %shard_map.147 = bf16[512,2048]{1,0:T(8,128)(2,1)S(1)} custom-call(bf16[512,1408]{1,0:T(8,128)(2,1)S(1)} %copy-done.8, bf16[2048,4224]{1,0:T(8,128)(2,1)} %all-gather.8.cloned.1.call-done.w_ref.b_ref), custom_call_target="tpu_custom_call" | custom-call | flops 2952790016 | bytes 5767168 | tf_op jit(solution)/shard_map/pallas_call | solution.py:546
  336.0 8.2 %collective-permute-done.33 = bf16[128,2048]{1,0:T(8,128)(2,1)} collective-permute-done((bf16[128,2048]{1,0:T(8,128)(2,1)}, bf16[128,2048]{1,0:T(8,128)(2,1)}, u32[]{:S(2)}, u32[]{:S(2)}) %collective-permute-start.33) | collective-permute-done | bytes 524320 | tf_op jit(solution)/shard_map/ppermute | solution.py:594
  386.5 25.3 %shard_map.149 = (bf16[512,1664]{1,0:T(8,128)(2,1)}, f32[1,64]{1,0:T(1,128)}) custom-call(f32[512,1664]{1,0:T(8,128)} %copy-done.27, f32[1,64]{1,0:T(1,128)} %bitcast.151, s32[512,1]{1,0:T(8,128)} %copy.38.segc_ref, s32[8,1,64]{2,1,0:T(1,128)} %reshape.285.segr_ref, f32[512,512]{1,0:T(8,128)} %get-tuple-element.213.out_ref, ...), custom_call_target="tpu_custom_call" | custom-call | flops 16000000000 | tf_op jit(solution)/shard_map/pallas_call | solution.py:284
  421.0 10.3 %shard_map.151 = bf16[2048,2176]{1,0:T(8,128)(2,1)} custom-call(bf16[512,2048]{1,0:T(8,128)(2,1)} %get-tuple-element.160.a_ref, bf16[512,1664]{1,0:T(8,128)(2,1)} %get-tuple-element.223.b_ref.a_ref, f32[2048,1]{1,0:T(8,128)} %fusion.10.holds_ref, f32[1,128]{1,0:T(1,128)} %concatenate.29.bias_ref, bf16[512,512]{1,0:T(8,128)(2,1)} %copy-done.10, ...), custom_call_target="tpu_custom_call" | custom-call | flops 4563402752 | bytes 8912896 | tf_op jit(solution)/shard_map/pallas_call | solution.py:404
  432.7 6.5 %shard_map.152 = bf16[512,2048]{1,0:T(8,128)(2,1)S(1)} custom-call(bf16[512,1664]{1,0:T(8,128)(2,1)S(1)} %copy-done.28, bf16[2048,1664]{1,0:T(8,128)(2,1)} %all-gather.4.cloned.1.call-done.b_ref), custom_call_target="tpu_custom_call" | custom-call | flops 3489660928 | bytes 6815744 | tf_op jit(solution)/shard_map/pallas_call | solution.py:546
  463.4 6.7 %collective-permute-done.49 = bf16[128,2048]{1,0:T(8,128)(2,1)S(1)} collective-permute-done((bf16[128,2048]{1,0:T(8,128)(2,1)}, bf16[128,2048]{1,0:T(8,128)(2,1)S(1)}, u32[]{:S(2)}, u32[]{:S(2)}) %collective-permute-start.49) | collective-permute-done | bytes 524320 | tf_op jit(solution)/shard_map/ppermute | solution.py:613
  470.1 8.3 %collective-permute-done.50 = bf16[64,4224]{1,0:T(8,128)(2,1)S(1)} collective-permute-done((bf16[64,4224]{1,0:T(8,128)(2,1)S(1)}, bf16[64,4224]{1,0:T(8,128)(2,1)S(1)}, u32[]{:S(2)}, u32[]{:S(2)}) %collective-permute-start.50) | collective-permute-done | bytes 540704 | tf_op jit(solution)/shard_map/ppermute | solution.py:692
  485.0 12.5 %collective-permute-start.61 = (bf16[64,4224]{1,0:T(8,128)(2,1)S(1)}, bf16[64,4224]{1,0:T(8,128)(2,1)S(1)}, u32[]{:S(2)}, u32[]{:S(2)}) collective-permute-start(bf16[64,4224]{1,0:T(8,128)(2,1)S(1)} %get-tuple-element.253), channel_id=1, source_target_pairs={{6,0},{4,1},{2,2},{0,3},{7,4},{5,5},{3,6},{1,7},{14,8},{12,9},{10,... | collective-permute-start | bytes 1622024 | tf_op jit(solution)/shard_map/ppermute | solution.py:692
  500.4 10.0 %collective-permute-start.53 = (bf16[128,2048]{1,0:T(8,128)(2,1)}, bf16[128,2048]{1,0:T(8,128)(2,1)S(1)}, u32[]{:S(2)}, u32[]{:S(2)}) collective-permute-start(bf16[128,2048]{1,0:T(8,128)(2,1)} %add_convert_fusion.1), channel_id=1, source_target_pairs={{0,2},{1,3},{2,0},{3,1},{4,6},{5,7},{6,4},{7,5},{8,10},{9,11},{10,... | collective-permute-start | bytes 1572872 | tf_op jit(solution)/shard_map/ppermute | solution.py:594
  510.6 12.4 %collective-permute-done.61 = bf16[64,4224]{1,0:T(8,128)(2,1)S(1)} collective-permute-done((bf16[64,4224]{1,0:T(8,128)(2,1)S(1)}, bf16[64,4224]{1,0:T(8,128)(2,1)S(1)}, u32[]{:S(2)}, u32[]{:S(2)}) %collective-permute-start.61) | collective-permute-done | bytes 540704 | tf_op jit(solution)/shard_map/ppermute | solution.py:692
  538.7 7.7 %collective-permute-done.59 = bf16[64,1664]{1,0:T(8,128)(2,1)S(1)} collective-permute-done((bf16[64,1664]{1,0:T(8,128)(2,1)S(1)}, bf16[64,1664]{1,0:T(8,128)(2,1)S(1)}, u32[]{:S(2)}, u32[]{:S(2)}) %collective-permute-start.59) | collective-permute-done | bytes 213024 | tf_op jit(solution)/shard_map/ppermute | solution.py:692
  (370 shorter events, 264.0 us)
Async XLA Ops:
  7.2 102.5 %all-gather.4.cloned.1.call-start = ((), (), s32[]{:S(2)}) async-start(), calls=%async_computation.2 | async-start | bytes 7667712 | tf_op jit(solution)/shard_map/all_gather | solution.py:696
  35.9 197.2 %all-gather.6.cloned.1.call-start = ((), (), s32[]{:S(2)}) async-start(), calls=%async_computation.3 | async-start | bytes 9437184 | tf_op jit(solution)/shard_map/all_gather | solution.py:696
  37.6 35.0 %collective-permute-start.6 = (bf16[128,2048]{1,0:T(8,128)(2,1)S(1)}, bf16[128,2048]{1,0:T(8,128)(2,1)S(1)}, u32[]{:S(2)}, u32[]{:S(2)}) collective-permute-start(bf16[128,2048]{1,0:T(8,128)(2,1)S(1)} %bitcast.118), channel_id=1, source_target_pairs={{0,2},{1,3},{2,0},{3,1},{4,6},{5,7},{6,4},{7,5},{8,10},{9,11},{10,... | collective-permute-start | bytes 1572872 | tf_op jit(solution)/shard_map/ppermute | solution.py:594
  39.6 33.1 %collective-permute-start.7 = (bf16[128,2048]{1,0:T(8,128)(2,1)S(1)}, bf16[128,2048]{1,0:T(8,128)(2,1)S(1)}, u32[]{:S(2)}, u32[]{:S(2)}) collective-permute-start(bf16[128,2048]{1,0:T(8,128)(2,1)S(1)} %bitcast.119), channel_id=1, source_target_pairs={{2,4},{3,5},{4,2},{5,3},{10,12},{11,13},{12,10},{13,11},{18,20},{1... | collective-permute-start | bytes 1572872 | tf_op jit(solution)/shard_map/ppermute | solution.py:613
  40.3 32.4 %collective-permute-start.8 = (bf16[128,2048]{1,0:T(8,128)(2,1)S(1)}, bf16[128,2048]{1,0:T(8,128)(2,1)S(1)}, u32[]{:S(2)}, u32[]{:S(2)}) collective-permute-start(bf16[128,2048]{1,0:T(8,128)(2,1)S(1)} %bitcast.120), channel_id=1, source_target_pairs={{0,6},{1,7},{6,0},{7,1},{8,14},{9,15},{14,8},{15,9},{16,22},{17,23... | collective-permute-start | bytes 1572872 | tf_op jit(solution)/shard_map/ppermute | solution.py:613
  102.0 162.5 %all-gather.8.cloned.1.call-start = ((), (), s32[]{:S(2)}) async-start(), calls=%async_computation.4 | async-start | bytes 19464192 | tf_op jit(solution)/shard_map/all_gather | solution.py:696
  102.5 40.9 %collective-permute-start.16 = (bf16[64,4224]{1,0:T(8,128)(2,1)}, bf16[64,4224]{1,0:T(8,128)(2,1)S(1)}, u32[]{:S(2)}, u32[]{:S(2)}) collective-permute-start(bf16[64,4224]{1,0:T(8,128)(2,1)} %get-tuple-element.161), channel_id=1, source_target_pairs={{0,0},{1,2},{2,4},{3,6},{4,1},{5,3},{6,5},{7,7},{8,8},{9,10},{10,1... | collective-permute-start | bytes 1622024 | tf_op jit(solution)/shard_map/ppermute | solution.py:685
  104.4 45.2 %collective-permute-start.17 = (bf16[64,4224]{1,0:T(8,128)(2,1)}, bf16[64,4224]{1,0:T(8,128)(2,1)S(1)}, u32[]{:S(2)}, u32[]{:S(2)}) collective-permute-start(bf16[64,4224]{1,0:T(8,128)(2,1)} %get-tuple-element.162), channel_id=1, source_target_pairs={{0,2},{1,0},{2,6},{3,4},{4,3},{5,1},{6,7},{7,5},{8,10},{9,8},{10,1... | collective-permute-start | bytes 1622024 | tf_op jit(solution)/shard_map/ppermute | solution.py:685
  104.5 63.0 %collective-permute-start.29 = (bf16[64,4224]{1,0:T(8,128)(2,1)}, bf16[64,4224]{1,0:T(8,128)(2,1)S(1)}, u32[]{:S(2)}, u32[]{:S(2)}) collective-permute-start(bf16[64,4224]{1,0:T(8,128)(2,1)} %get-tuple-element.188), channel_id=1, source_target_pairs={{0,4},{1,6},{2,0},{3,2},{4,5},{5,7},{6,1},{7,3},{8,12},{9,14},{10,... | collective-permute-start | bytes 1622024 | tf_op jit(solution)/shard_map/ppermute | solution.py:685
  106.1 61.4 %collective-permute-start.30 = (bf16[64,4224]{1,0:T(8,128)(2,1)S(1)}, bf16[64,4224]{1,0:T(8,128)(2,1)}, u32[]{:S(2)}, u32[]{:S(2)}) collective-permute-start(bf16[64,4224]{1,0:T(8,128)(2,1)S(1)} %copy-done.47), channel_id=1, source_target_pairs={{0,6},{1,4},{2,2},{3,0},{4,7},{5,5},{6,3},{7,1},{8,14},{9,12},{10,... | collective-permute-start | bytes 1622024 | tf_op jit(solution)/shard_map/ppermute | solution.py:685
  170.1 270.4 %reduce-scatter.3.cloned.1.call-start = ((), (), s32[]{:S(2)}) async-start(), calls=%async_computation.5 | async-start | bytes 19464192 | tf_op jit(solution)/shard_map/reduce_scatter | solution.py:699
  194.6 32.9 %collective-permute-start.22 = (bf16[512,512]{1,0:T(8,128)(2,1)S(1)}, bf16[512,512]{1,0:T(8,128)(2,1)}, u32[]{:S(2)}, u32[]{:S(2)}) collective-permute-start(bf16[512,512]{1,0:T(8,128)(2,1)S(1)} %collective-permute-done.19.refs_5_), channel_id=1, source_target_pairs={{2,0},{3,1},{4,6},{5,7},{10,8},{11,9},{12,14},{13,15},{18,16},{19,... | collective-permute-start | bytes 1572872 | tf_op jit(solution)/shard_map/ppermute | solution.py:613
  200.5 42.0 %collective-permute-start.26 = (bf16[128,2048]{1,0:T(8,128)(2,1)S(1)}, bf16[128,2048]{1,0:T(8,128)(2,1)}, u32[]{:S(2)}, u32[]{:S(2)}) collective-permute-start(bf16[128,2048]{1,0:T(8,128)(2,1)S(1)} %bitcast.124), channel_id=1, source_target_pairs={{0,6},{1,7},{6,0},{7,1},{8,14},{9,15},{14,8},{15,9},{16,22},{17,23... | collective-permute-start | bytes 1572872 | tf_op jit(solution)/shard_map/ppermute | solution.py:613
  202.4 40.1 %collective-permute-start.27 = (bf16[128,2048]{1,0:T(8,128)(2,1)}, bf16[128,2048]{1,0:T(8,128)(2,1)}, u32[]{:S(2)}, u32[]{:S(2)}) collective-permute-start(bf16[128,2048]{1,0:T(8,128)(2,1)} %collective-permute-done.24.refs_1_), channel_id=1, source_target_pairs={{2,4},{3,5},{4,2},{5,3},{10,12},{11,13},{12,10},{13,11},{18,20},{1... | collective-permute-start | bytes 1572872 | tf_op jit(solution)/shard_map/ppermute | solution.py:613
  210.4 34.0 %collective-permute-start.28 = (bf16[128,2048]{1,0:T(8,128)(2,1)}, bf16[128,2048]{1,0:T(8,128)(2,1)}, u32[]{:S(2)}, u32[]{:S(2)}) collective-permute-start(bf16[128,2048]{1,0:T(8,128)(2,1)} %collective-permute-done.25.refs_5_), channel_id=1, source_target_pairs={{2,0},{3,1},{4,6},{5,7},{10,8},{11,9},{12,14},{13,15},{18,16},{19,... | collective-permute-start | bytes 1572872 | tf_op jit(solution)/shard_map/ppermute | solution.py:613
  315.0 213.0 %reduce-scatter.5.cloned.1.call-start = ((), (), s32[]{:S(2)}) async-start(), calls=%async_computation.6 | async-start | bytes 10027008 | tf_op jit(solution)/shard_map/reduce_scatter | solution.py:699
  374.3 38.8 %collective-permute-start.39 = (bf16[128,2048]{1,0:T(8,128)(2,1)}, bf16[128,2048]{1,0:T(8,128)(2,1)}, u32[]{:S(2)}, u32[]{:S(2)}) collective-permute-start(bf16[128,2048]{1,0:T(8,128)(2,1)} %get-tuple-element.274), channel_id=1, source_target_pairs={{2,4},{3,5},{4,2},{5,3},{10,12},{11,13},{12,10},{13,11},{18,20},{1... | collective-permute-start | bytes 1572872 | tf_op jit(solution)/shard_map/ppermute | solution.py:613
  375.8 37.4 %collective-permute-start.40 = (bf16[128,2048]{1,0:T(8,128)(2,1)}, bf16[128,2048]{1,0:T(8,128)(2,1)}, u32[]{:S(2)}, u32[]{:S(2)}) collective-permute-start(bf16[128,2048]{1,0:T(8,128)(2,1)} %get-tuple-element.274), channel_id=1, source_target_pairs={{0,2},{1,3},{6,4},{7,5},{8,10},{9,11},{14,12},{15,13},{16,18},{17,... | collective-permute-start | bytes 1572872 | tf_op jit(solution)/shard_map/ppermute | solution.py:613
  381.1 32.0 %collective-permute-start.43 = (bf16[128,512]{1,0:T(8,128)(2,1)}, bf16[128,512]{1,0:T(8,128)(2,1)S(1)}, u32[]{:S(2)}, u32[]{:S(2)}) collective-permute-start(bf16[128,512]{1,0:T(8,128)(2,1)} %copy.44), channel_id=1, source_target_pairs={{0,4},{1,5},{2,6},{3,7},{4,0},{5,1},{6,2},{7,3},{8,12},{9,13},{10,... | collective-permute-start | bytes 393224 | tf_op jit(solution)/shard_map/ppermute | solution.py:594
  381.2 31.9 %collective-permute-start.44 = (bf16[128,512]{1,0:T(8,128)(2,1)S(1)}, bf16[128,512]{1,0:T(8,128)(2,1)S(1)}, u32[]{:S(2)}, u32[]{:S(2)}) collective-permute-start(bf16[128,512]{1,0:T(8,128)(2,1)S(1)} %copy.45), channel_id=1, source_target_pairs={{0,6},{1,7},{2,4},{3,5},{4,2},{5,3},{6,0},{7,1},{8,14},{9,15},{10,... | collective-permute-start | bytes 393224 | tf_op jit(solution)/shard_map/ppermute | solution.py:594
  383.6 29.5 %collective-permute-start.41 = (bf16[128,2048]{1,0:T(8,128)(2,1)}, bf16[128,2048]{1,0:T(8,128)(2,1)}, u32[]{:S(2)}, u32[]{:S(2)}) collective-permute-start(bf16[128,2048]{1,0:T(8,128)(2,1)} %get-tuple-element.273), channel_id=1, source_target_pairs={{0,6},{1,7},{6,0},{7,1},{8,14},{9,15},{14,8},{15,9},{16,22},{17,23... | collective-permute-start | bytes 1572872 | tf_op jit(solution)/shard_map/ppermute | solution.py:613
  485.0 37.9 %collective-permute-start.61 = (bf16[64,4224]{1,0:T(8,128)(2,1)S(1)}, bf16[64,4224]{1,0:T(8,128)(2,1)S(1)}, u32[]{:S(2)}, u32[]{:S(2)}) collective-permute-start(bf16[64,4224]{1,0:T(8,128)(2,1)S(1)} %get-tuple-element.253), channel_id=1, source_target_pairs={{6,0},{4,1},{2,2},{0,3},{7,4},{5,5},{3,6},{1,7},{14,8},{12,9},{10,... | collective-permute-start | bytes 1622024 | tf_op jit(solution)/shard_map/ppermute | solution.py:692
  498.5 55.7 %collective-permute-start.54 = (bf16[128,2048]{1,0:T(8,128)(2,1)}, bf16[128,2048]{1,0:T(8,128)(2,1)S(1)}, u32[]{:S(2)}, u32[]{:S(2)}) collective-permute-start(bf16[128,2048]{1,0:T(8,128)(2,1)} %add_convert_fusion), channel_id=1, source_target_pairs={{2,4},{3,5},{4,2},{5,3},{10,12},{11,13},{12,10},{13,11},{18,20},{1... | collective-permute-start | bytes 1572872 | tf_op jit(solution)/shard_map/ppermute | solution.py:613
  500.4 53.8 %collective-permute-start.53 = (bf16[128,2048]{1,0:T(8,128)(2,1)}, bf16[128,2048]{1,0:T(8,128)(2,1)S(1)}, u32[]{:S(2)}, u32[]{:S(2)}) collective-permute-start(bf16[128,2048]{1,0:T(8,128)(2,1)} %add_convert_fusion.1), channel_id=1, source_target_pairs={{0,2},{1,3},{2,0},{3,1},{4,6},{5,7},{6,4},{7,5},{8,10},{9,11},{10,... | collective-permute-start | bytes 1572872 | tf_op jit(solution)/shard_map/ppermute | solution.py:594
  (105 other events, 1145.3 us)
Sparse Core Ops, SparseCore 0:
  36.0 48.4 all-gather.3
  102.2 53.3 all-gather.5
  170.2 94.2 all-gather.7
  315.1 117.5 reduce-scatter.2
  440.6 75.3 reduce-scatter.4
